TPU v7x, 32 devices: a whole 2x2x4 slice. The times are simulated.
32 devices in a mesh: groups: 2 (over y), fsdp: 4 (over x, core), tp: 4 (over z).
Axes of the slice: x: 2, y: 2, z: 4, core: 2. Of those that a mesh axis runs over, the one named last changes fastest.
Arguments:
- hidden_in: bfloat16 [8192, 8192], P(('groups', 'fsdp', 'tp')), parts along dimension 0, may hold values from -6 to 6
- segment_ids: int32 [8192], P(('groups', 'fsdp', 'tp')), parts along dimension 0, may hold values from 0 to 15, never falling along the last dimension, each value on 1 to 512 neighbouring positions
- norm_gain: float32 [16384], P('groups'), parts along dimension 0, may hold values from 0.25 to 1.75
- query_weight: bfloat16 [16384, 4096], P(('groups', 'fsdp', 'tp')), parts along dimension 0, may hold values from -3 to 3
- key_weight: bfloat16 [16384, 512], P(('groups', 'fsdp', 'tp')), parts along dimension 0, may hold values from -3 to 3
- value_weight: bfloat16 [16384, 512], P(('groups', 'fsdp', 'tp')), parts along dimension 0, may hold values from -0.0625 to 0.0625
- output_weight: bfloat16 [16384, 4096], P(('groups', 'fsdp', 'tp')), parts along dimension 0, may hold values from -0.09375 to 0.09375
- query_bias: float32 [8192], P('groups'), parts along dimension 0, may hold values from -3 to 3
- key_bias: float32 [1024], P('groups'), parts along dimension 0, may hold values from -3 to 3
- value_bias: float32 [1024], P('groups'), parts along dimension 0, may hold values from -3 to 3
Outputs:
- hidden_out: bfloat16 [8192, 8192], P(('groups', 'fsdp', 'tp')), parts along dimension 0
There are 2 independent parts, one for each index of `groups`. A program takes and returns all parts, laid end to end along the dimension named above; each array names one. Nothing has to cross between parts.
Inputs may be any that keep to these rules, and one draw needn't show every extreme that they name: `segment_ids`: ids never fall along the rows; each id covers 1 to 512 consecutive rows, and some id covers exactly 512.
All inputs are finite; a program needn't handle non-finite values.
Results may differ from a plain program's by a relative error of at most 0.012.
The roundings to bfloat16 on the way count: a program that leaves them out, or rounds other values in their place, can miss the bound.
Values may be sent and summed in bfloat16 or wider, within the bound.
No kernel may reach another device: no remote copies, remote signals or barrier semaphores. Data moves between devices by JAX's collectives and lax.ppermute only.
A program may use at most 192 MiB of HBM per device.

v0:
```python
import jax
import jax.numpy as jnp
from jax import lax
from jax.sharding import PartitionSpec as P

HEAD = 128


rope_base = 1000000.0
norm_eps = 1e-06


def normalize(hidden, gain):
    widened = hidden.astype(jnp.float32)
    mean_square = jnp.mean(widened * widened, axis=-1, keepdims=True)
    return (widened * lax.rsqrt(mean_square + norm_eps) * gain).astype(jnp.bfloat16)


def segment_positions(segments):
    row_count = segments.shape[0]
    places = jnp.arange(row_count, dtype=jnp.int32)
    same_seg = segments[:, None] == segments[None, :]
    starts = jnp.min(jnp.where(same_seg, places[None, :], row_count), axis=1)
    return (places - starts).astype(jnp.float32)


def rotary(vectors, positions):
    head_width = vectors.shape[-1]
    half_width = head_width // 2
    frequency = rope_base ** (-(jnp.arange(half_width, dtype=jnp.float32) * 2.0 / head_width))
    angles = positions[:, None] * frequency[None, :]
    cosine = jnp.concatenate([jnp.cos(angles), jnp.cos(angles)], axis=-1)[:, None, :]
    sine_part = jnp.concatenate([jnp.sin(angles), jnp.sin(angles)], axis=-1)[:, None, :]
    turned = jnp.concatenate([-vectors[..., half_width:], vectors[..., :half_width]], axis=-1)
    return vectors * cosine + turned * sine_part


def attend(queries, key_rows, value_rows, segments):
    score_scale = key_rows.shape[-1] ** (-0.5)
    scores = (
        jnp.einsum("tgh,sh->gts", queries, key_rows, preferred_element_type=jnp.float32)
        * score_scale
    )
    row_ids = jnp.arange(segments.shape[0], dtype=jnp.int32)
    allowed = (row_ids[None, :] <= row_ids[:, None]) & (segments[:, None] == segments[None, :])
    scores = jnp.where(allowed[None], scores, -1e30)
    row_max = jnp.max(scores, axis=-1, keepdims=True)
    weights = jnp.exp(scores - row_max)
    probs = (weights / jnp.sum(weights, axis=-1, keepdims=True)).astype(jnp.bfloat16)
    return jnp.einsum("gts,sh->tgh", probs, value_rows, preferred_element_type=jnp.float32)


def per_device(
    hidden_in,
    segment_ids,
    norm_gain,
    query_weight,
    key_weight,
    value_weight,
    output_weight,
    query_bias,
    key_bias,
    value_bias,
):
    tp_count = lax.axis_size("tp")
    tp_index = lax.axis_index("tp")
    head_size = HEAD
    kv_heads = key_weight.shape[1] // head_size
    repeats = tp_count // kv_heads
    local_rows = key_weight.shape[0]
    contract_last = (((1,), (1,)), ((), ()))
    normed = normalize(hidden_in, norm_gain)
    tokens, segments = (
        lax.all_gather(normed, "tp", axis=0, tiled=True),
        lax.all_gather(segment_ids, "tp", axis=0, tiled=True),
    )

    def widen(weight):
        spread_heads = jnp.broadcast_to(
            weight.reshape(local_rows, kv_heads, 1, head_size),
            (local_rows, kv_heads, repeats, head_size),
        )
        return spread_heads.reshape(local_rows, tp_count * head_size)

    query_part, key_part, value_part, output_part = (
        lax.all_to_all(query_weight, "tp", split_axis=1, concat_axis=0, tiled=True),
        lax.all_to_all(widen(key_weight), "tp", split_axis=1, concat_axis=0, tiled=True),
        lax.all_to_all(widen(value_weight), "tp", split_axis=1, concat_axis=0, tiled=True),
        lax.all_to_all(output_weight, "tp", split_axis=1, concat_axis=0, tiled=True),
    )
    query_cols = query_part.shape[1]
    token_count = tokens.shape[0]
    query_full, key_full, value_full = (
        lax.all_gather(query_part, "fsdp", axis=0, tiled=True),
        lax.all_gather(key_part, "fsdp", axis=0, tiled=True),
        lax.all_gather(value_part, "fsdp", axis=0, tiled=True),
    )
    queries = jnp.dot(tokens, query_full, preferred_element_type=jnp.float32)
    key_rows = jnp.dot(tokens, key_full, preferred_element_type=jnp.float32)
    value_rows = jnp.dot(tokens, value_full, preferred_element_type=jnp.float32)
    queries = queries + lax.dynamic_slice_in_dim(query_bias, tp_index * query_cols, query_cols)
    kv_start = tp_index // repeats * head_size
    key_rows = key_rows + lax.dynamic_slice_in_dim(key_bias, kv_start, head_size)
    value_rows = value_rows + lax.dynamic_slice_in_dim(value_bias, kv_start, head_size)
    positions = segment_positions(segments)
    query_rot = rotary(
        queries.reshape(token_count, query_cols // head_size, head_size), positions
    ).astype(jnp.bfloat16)
    key_rot = (
        rotary(key_rows.reshape(token_count, 1, head_size), positions)
        .reshape(token_count, head_size)
        .astype(jnp.bfloat16)
    )
    mixed = attend(query_rot, key_rot, value_rows.astype(jnp.bfloat16), segments)
    mixed = mixed.astype(jnp.bfloat16).reshape(token_count, query_cols)
    partials = lax.dot_general(
        mixed,
        lax.all_gather(output_part, "fsdp", axis=0, tiled=True),
        contract_last,
        preferred_element_type=jnp.float32,
    )
    summed = lax.psum_scatter(
        partials.astype(jnp.bfloat16), "tp", scatter_dimension=0, tiled=True
    ).astype(jnp.float32)
    return (hidden_in.astype(jnp.float32) + summed).astype(jnp.bfloat16)


def solution(mesh):
    return jax.shard_map(
        per_device,
        mesh=mesh,
        in_specs=(
            P(("groups", "fsdp", "tp"), None),
            P(("groups", "fsdp", "tp")),
            P("groups"),
            P(("groups", "fsdp", "tp"), None),
            P(("groups", "fsdp", "tp"), None),
            P(("groups", "fsdp", "tp"), None),
            P(("groups", "fsdp", "tp"), None),
            P("groups"),
            P("groups"),
            P("groups"),
        ),
        out_specs=P(("groups", "fsdp", "tp"), None),
        check_vma=False,
    )
```

profile of v0, /device:TPU:0, one launch (start us, length us, event | category | flops | bytes accessed | tf_op | source)
XLA Modules:
  0.0 1068.3 jit_solution(8469316449728620850)
XLA Ops:
  6.5 0.0 copy-start.2
  6.5 0.0 all-gather.11.cloned.1.call-start
  6.5 1.3 copy.31
  7.8 20.6 %all_to_all.76 = bf16[512,4,128]{0,2,1:T(8,128)(2,1)S(1)} all-to-all(bf16[512,4,128]{0,2,1:T(8,128)(2,1)S(1)} %bitcast.72), channel_id=1, replica_groups=mesh['groups'=2,'fsdp'=4,'tp'=4] {'tp'}, dimensions={1} | all-to-all | bytes 1048576 | tf_op jit(solution)/shard_map/all_to_all | solution.py:87
  28.4 1.0 copy.32
  29.4 0.0 all-gather.11.cloned.1.call-update
  29.4 0.0 all-gather.7.cloned.1.call-start
  29.5 0.0 copy-start
  29.5 3.3 fusion.6
  32.8 0.0 copy-done.2
  32.8 0.2 copy-done
  32.9 3.2 fusion.8
  36.1 0.0 all-gather.7.cloned.1.call-update
  36.2 0.0 all-gather.13.cloned.1.call-start
  36.2 6.6 copy.33
  42.8 204.4 %all_to_all.77 = bf16[512,4,1024]{0,2,1:T(8,128)(2,1)} all-to-all(bf16[512,4,1024]{0,2,1:T(8,128)(2,1)} %bitcast.66), channel_id=1, replica_groups=mesh['groups'=2,'fsdp'=4,'tp'=4] {'tp'}, dimensions={1} | all-to-all | bytes 8388608 | tf_op jit(solution)/shard_map/all_to_all | solution.py:86
  247.2 6.3 copy.34
  253.5 0.0 copy-start.1
  253.6 0.0 all-gather.13.cloned.1.call-update
  253.6 1.0 copy-done.1
  254.6 1.0 copy.29
  255.6 3.5 all-to-all-start
  259.1 6.5 copy.39
  265.6 16.6 %all-to-all-done = bf16[512,4,128]{0,2,1:T(8,128)(2,1)S(1)} async-done(((bf16[512,4,128]{0,2,1:T(8,128)(2,1)}), bf16[512,4,128]{0,2,1:T(8,128)(2,1)S(1)}, u32[]{:S(2)}, u32[]{:S(2)}) %all-to-all-start) | async-done | bytes 524320 | tf_op jit(solution)/shard_map/all_to_all | solution.py:88
  282.3 4.8 all-to-all-start.3
  287.1 0.0 all-gather.9.cloned.1.call-start
  287.2 1.0 copy.30
  288.2 0.0 all-gather.9.cloned.1.call-update
  288.2 0.0 all-gather.15.cloned.1.call-start
  288.2 187.9 %all-to-all-done.3 = bf16[512,4,1024]{0,2,1:T(8,128)(2,1)} async-done(((bf16[512,4,1024]{0,2,1:T(8,128)(2,1)}), bf16[512,4,1024]{0,2,1:T(8,128)(2,1)}, u32[]{:S(2)}, u32[]{:S(2)}) %all-to-all-start.3) | async-done | bytes 4194336 | tf_op jit(solution)/shard_map/all_to_all | solution.py:89
  476.2 6.3 copy.40
  482.4 0.0 copy-start.3
  482.4 0.0 all-gather.15.cloned.1.call-update
  482.5 0.0 reduce-scatter.2.cloned.1.call-start
  482.5 0.8 dynamic_slice.10
  483.3 0.8 dynamic_slice.9
  484.0 0.0 copy-done.3
  484.0 8.5 all-gather
  492.5 0.6 fusion.10
  493.2 1.0 multiply_cosine_fusion
  494.2 1.6 compare_and_fusion
  495.7 0.0 dynamic-slice-start
  495.7 0.0 all-gather.11.cloned.1.call-done
  495.7 16.1 %all-gather.7.cloned.1.call-done = bf16[1024,8192]{1,0:T(8,128)(2,1)} async-done(((bf16[256,8192]{1,0:T(8,128)(2,1)}), bf16[1024,8192]{1,0:T(8,128)(2,1)}) %all-gather.7.cloned.1.call-update) | async-done | bytes 16777232 | tf_op jit(solution)/shard_map/all_gather | solution.py:74
  511.8 12.0 %convolution_add_fusion.1 = f32[1024,128]{0,1:T(8,128)S(1)} fusion(bf16[1024,8192]{1,0:T(8,128)(2,1)} %all-gather.7.cloned.1.call-done, bf16[8192,128]{1,0:T(8,128)(2,1)} %all-gather.11.cloned.1.call-done, f32[128]{0:T(128)S(1)} %dynamic_slice.10), kind=kOutput, calls=%fused_computation.29 | convolution fusion | flops 2147614720 | bytes 19399168 | tf_op jit(solution)/shard_map/dot_general | solution.py:99
  523.9 0.2 pad_maximum_fusion
  524.2 94.3 %all-gather.13.cloned.1.call-done = bf16[8192,1024]{1,0:T(8,128)(2,1)} async-done(((bf16[2048,1024]{1,0:T(8,128)(2,1)}), bf16[8192,1024]{1,0:T(8,128)(2,1)}) %all-gather.13.cloned.1.call-update) | async-done | bytes 16777232 | tf_op jit(solution)/shard_map/all_gather | solution.py:94
  618.5 0.0 dynamic-slice-done
  618.5 23.4 %convolution_add_fusion = f32[1024,1024]{0,1:T(8,128)S(1)} fusion(bf16[1024,8192]{1,0:T(8,128)(2,1)} %all-gather.7.cloned.1.call-done, bf16[8192,1024]{1,0:T(8,128)(2,1)} %all-gather.13.cloned.1.call-done, f32[1024]{0:T(1024)S(1)} %dynamic-slice-done), kind=kOutput, calls=%fused_computation.26 | convolution fusion | flops 17180917760 | bytes 37752832 | tf_op jit(solution)/shard_map/dot_general | solution.py:98
  641.9 0.4 slice_negate_fusion
  642.3 0.7 maximum_multiply_fusion
  643.0 1.2 fusion.11
  644.2 20.3 %fusion.24 = (f32[8,1024]{1,0:T(8,128)S(1)}, f32[8,1024,1024]{1,2,0:T(8,128)}) fusion(pred[1024,1024]{0,1:T(8,128)(4,1)} %compare_and_fusion, bf16[1024,128,1]{0,1,2:T(8,128)(2,1)S(1)} %get-tuple-element.10, bf16[1024,8,128]{0,2,1:T(8,128)(2,1)S(1)} %bitcast.73), kind=kOutput, calls=%fused_computation.50 | convolution fusion | flops 2181039104 | bytes 36995072 | tf_op jit(solution)/shard_map/sub | solution.py:48
  664.6 0.0 all-gather.9.cloned.1.call-done
  664.6 19.7 %fusion.14 = bf16[128,8,1024]{2,0,1:T(8,128)(2,1)S(1)} fusion(f32[8,1024,1024]{1,2,0:T(8,128)} %get-tuple-element.15, f32[8,1024]{1,0:T(8,128)S(1)} %get-tuple-element.14, bf16[1024,8192]{1,0:T(8,128)(2,1)} %all-gather.7.cloned.1.call-done, bf16[8192,128]{1,0:T(8,128)(2,1)} %all-gather.9.cloned.1.call-done, f32[128]{0:T(128)S(1)} %dynamic_slice.9), kind=kOutput, calls=%fused_computation.28 | convolution fusion | flops 4313055232 | bytes 54559232 | tf_op jit(solution)/shard_map/gts,sh->tgh/dot_general | solution.py:50
  684.3 65.6 %all-gather.15.cloned.1.call-done = bf16[8192,1024]{1,0:T(8,128)(2,1)} async-done(((bf16[2048,1024]{1,0:T(8,128)(2,1)}), bf16[8192,1024]{1,0:T(8,128)(2,1)}) %all-gather.15.cloned.1.call-update) | async-done | bytes 16777232 | tf_op jit(solution)/shard_map/all_gather | solution.py:118
  749.9 24.1 %convolution_convert_fusion = bf16[1024,8192]{1,0:T(8,128)(2,1)} fusion(bf16[1024,1024]{0,1:T(8,128)(2,1)S(1)} %bitcast.77, bf16[8192,1024]{1,0:T(8,128)(2,1)} %all-gather.15.cloned.1.call-done), kind=kOutput, calls=%fused_computation.9 | convolution fusion | flops 17188257792 | bytes 35651584 | tf_op jit(solution)/shard_map/dot_general | solution.py:116
  774.0 0.0 reduce-scatter.2.cloned.1.call-update
  774.0 280.5 %reduce-scatter.2.cloned.1.call-done = bf16[256,8192]{1,0:T(8,128)(2,1)} async-done(((bf16[1024,8192]{1,0:T(8,128)(2,1)}), bf16[256,8192]{1,0:T(8,128)(2,1)}) %reduce-scatter.2.cloned.1.call-update) | async-done | bytes 4194320 | tf_op jit(solution)/shard_map/reduce_scatter | solution.py:122
  1054.5 7.0 fusion.9
  (4 shorter events, 0.1 us)
Async XLA Ops:
  6.5 26.2 %copy-start.2 = (f32[8192]{0:T(1024)S(1)}, f32[8192]{0:T(1024)}, u32[]{:S(2)}) copy-start(f32[8192]{0:T(1024)} %param.12) | copy-start | bytes 98308
  6.5 489.2 %all-gather.11.cloned.1.call-start = ((), (), s32[]{:S(2)}) async-start(), calls=%async_computation.7 | async-start | bytes 2621440 | tf_op jit(solution)/shard_map/all_gather | solution.py:95
  29.4 482.4 %all-gather.7.cloned.1.call-start = ((), (), s32[]{:S(2)}) async-start(), calls=%async_computation.5 | async-start | bytes 20971520 | tf_op jit(solution)/shard_map/all_gather | solution.py:74
  29.5 3.5 copy-start
  36.2 582.3 %all-gather.13.cloned.1.call-start = ((), (), s32[]{:S(2)}) async-start(), calls=%async_computation.8 | async-start | bytes 20971520 | tf_op jit(solution)/shard_map/all_gather | solution.py:94
  253.5 1.1 copy-start.1
  255.6 26.6 %all-to-all-start = ((bf16[512,4,128]{0,2,1:T(8,128)(2,1)}), bf16[512,4,128]{0,2,1:T(8,128)(2,1)S(1)}, u32[]{:S(2)}, u32[]{:S(2)}) async-start(bf16[512,4,128]{0,2,1:T(8,128)(2,1)} %bitcast), calls=%async_computation | async-start | bytes 1048576 | tf_op jit(solution)/shard_map/all_to_all | solution.py:88
  282.3 193.9 %all-to-all-start.3 = ((bf16[512,4,1024]{0,2,1:T(8,128)(2,1)}), bf16[512,4,1024]{0,2,1:T(8,128)(2,1)}, u32[]{:S(2)}, u32[]{:S(2)}) async-start(bf16[512,4,1024]{0,2,1:T(8,128)(2,1)} %bitcast.63), calls=%async_computation.3 | async-start | bytes 8388608 | tf_op jit(solution)/shard_map/all_to_all | solution.py:89
  287.1 377.5 %all-gather.9.cloned.1.call-start = ((), (), s32[]{:S(2)}) async-start(), calls=%async_computation.6 | async-start | bytes 2621440 | tf_op jit(solution)/shard_map/all_gather | solution.py:96
  288.2 461.7 %all-gather.15.cloned.1.call-start = ((), (), s32[]{:S(2)}) async-start(), calls=%async_computation.9 | async-start | bytes 20971520 | tf_op jit(solution)/shard_map/all_gather | solution.py:118
  482.4 1.6 copy-start.3
  482.5 572.0 %reduce-scatter.2.cloned.1.call-start = ((), (), s32[]{:S(2)}) async-start(), calls=%async_computation.10 | async-start | bytes 20971520 | tf_op jit(solution)/shard_map/reduce_scatter | solution.py:122
  495.7 122.8 %dynamic-slice-start = ((f32[4096]{0:T(1024)}, s32[]{:T(128)}), f32[1024]{0:T(1024)S(1)}, s32[]{:S(2)}) async-start(f32[4096]{0:T(1024)} %param.17, s32[]{:T(128)} %select_n.20), calls=%async_computation.11 | async-start | bytes 8704 | tf_op jit(solution)/shard_map/dynamic_slice | solution.py:101
Sparse Core Ops, SparseCore 0:
  29.6 21.6 all-gather.10
  52.9 458.9 all-gather.6
  513.4 105.0 all-gather.12
  619.9 22.5 all-gather.8
  643.9 105.9 all-gather.14
  774.1 280.2 reduce-scatter.1
where the time goes:
time: 1070 us
  waiting for transfers between devices  661 us (62%)
  blocking collectives  233 us (22%)
  matrix products  99.5 us (9%)
  local copies, waits for them, and re-layouts  32.7 us (3%)
  other arithmetic  19.3 us (2%)
  between operations  13.6 us (1%)
    reduce_scatter x1, waiting for transfers between devices, per_device(): lax.psum_scatter(partials.astype(jnp.bfloat16), 'tp', scatter_dimension=0...  280 us
    all_to_all x1, blocking collectives, per_device(): lax.all_to_all(query_weight, 'tp', split_axis=1, concat_axis=0, tiled=True)  204 us
    all_to_all x1, waiting for transfers between devices, per_device(): lax.all_to_all(output_weight, 'tp', split_axis=1, concat_axis=0, tiled=True)  188 us
    all_gather x1, waiting for transfers between devices, per_device(): lax.all_gather(query_part, 'fsdp', axis=0, tiled=True)  94.3 us
    all_gather x1, waiting for transfers between devices, per_device(): lax.all_gather(output_part, 'fsdp', axis=0, tiled=True)  65.6 us
    dot_general x1, matrix products, per_device(): lax.dot_general(mixed, lax.all_gather(output_part, 'fsdp', axis=0, tiled=...  24.1 us
    dot_general x1, matrix products, per_device(): queries = jnp.dot(tokens, query_full, preferred_element_type=jnp.float32)  23.4 us
  transfers between devices with their start and end apart: 8, of which 6 were waited for; matrix products, arithmetic and copies ran while one was open for 11% of the time, Pallas kernels for 0%

commit v1 on v0

v1 whole, which is shorter than its diff:
```python
import functools

import jax
import jax.numpy as jnp
from jax import lax
from jax.experimental import pallas as pl
from jax.experimental.pallas import tpu as pltpu
from jax.sharding import PartitionSpec as P

HEAD = 128
LONGEST = 512
rope_base = 1000000.0
norm_eps = 1e-06
MASKED = -1e30
NOWHERE = 1 << 20
LEVEL = ("fsdp", "tp")


LIGHT = pl.CostEstimate(flops=1, bytes_accessed=1, transcendentals=0)
ROOM = pltpu.CompilerParams(vmem_limit_bytes=48 << 20)


def normalize(hidden, gain, order, n_f, depth, cuts):
    rows, width = hidden.shape
    n_t, cut = len(order), depth // cuts
    places = [(k, h, i) for k in range(n_t) for h in range(cuts) for i in range(n_f)]

    def scale(hidden):
        widened = hidden.astype(jnp.float32)
        return lax.rsqrt(jnp.mean(widened * widened, axis=-1, keepdims=True) + norm_eps)

    if cut % 128:
        normed = (hidden.astype(jnp.float32) * scale(hidden) * gain).astype(jnp.bfloat16)
        return jnp.concatenate([
            lax.dynamic_slice_in_dim(normed, (i * n_t + order[k]) * depth + h * cut, cut, 1)
            for k, h, i in places
        ], axis=1)

    def kernel(order_ref, hidden_ref, gain_ref, out_ref):
        factor = scale(hidden_ref[...])
        for place, (k, h, i) in enumerate(places):
            start = pl.multiple_of((i * n_t + order_ref[k]) * depth + h * cut, cut)
            span = pl.ds(start, cut)
            run = hidden_ref[:, span].astype(jnp.float32) * factor * gain_ref[:, span]
            out_ref[:, place * cut:(place + 1) * cut] = run.astype(jnp.bfloat16)

    block = min(64, rows)
    own = pl.BlockSpec((block, width), lambda m, order_ref: (m, 0))
    return pl.pallas_call(
        kernel,
        grid_spec=pltpu.PrefetchScalarGridSpec(
            num_scalar_prefetch=1,
            grid=(rows // block,),
            in_specs=[own, pl.BlockSpec((1, width), lambda m, order_ref: (0, 0))],
            out_specs=own,
        ),
        out_shape=jax.ShapeDtypeStruct(hidden.shape, jnp.bfloat16),
        compiler_params=ROOM,
        cost_estimate=LIGHT,
    )(jnp.stack(order).astype(jnp.int32), hidden, gain[None])


def segment_starts(segments):
    places = jnp.arange(segments.shape[-1], dtype=jnp.int32)
    same = segments[:, None] == segments[None, :]
    return jnp.min(jnp.where(same, places, segments.shape[-1]), axis=-1)


def rotary_tables(positions):
    half = HEAD // 2
    frequency = rope_base ** (-(jnp.arange(half, dtype=jnp.float32) * 2.0 / HEAD))
    angles = positions[:, None] * frequency[None, :]
    cosine, sine = jnp.cos(angles), jnp.sin(angles)
    return jnp.concatenate([cosine, cosine], -1), jnp.concatenate([-sine, sine], -1)


def attention_kernel(heads, scale, q_ref, bias_ref, cos_ref, sin_ref, start_ref, row_ref,
                     col_ref, k_ref, v_ref, out_ref):
    cosine, sine = cos_ref[...], sin_ref[...]
    columns = col_ref[...]
    allowed = (columns >= start_ref[...]) & (columns <= row_ref[...])
    keys, values = k_ref[0], v_ref[0]
    for head in range(heads):
        span = slice(head * HEAD, (head + 1) * HEAD)
        query = q_ref[:, span] + bias_ref[:, span]
        query = query * cosine + pltpu.roll(query, HEAD // 2, 1) * sine
        scores = lax.dot_general(
            query.astype(jnp.bfloat16), keys, (((1,), (1,)), ((), ())),
            preferred_element_type=jnp.float32,
        ) * scale
        scores = jnp.where(allowed, scores, MASKED)
        weights = jnp.exp(scores - jnp.max(scores, axis=-1, keepdims=True))
        probs = (weights / jnp.sum(weights, axis=-1, keepdims=True)).astype(jnp.bfloat16)
        mixed = jnp.dot(probs, values, preferred_element_type=jnp.float32)
        out_ref[:, span] = mixed.astype(jnp.bfloat16)


def attention(part, *, rows, groups, width, f, projected, bias, cosine, sine, starts, row_ids,
              columns, key_value):
    n_keys = key_value.shape[1]
    mine = lambda g, f_ref: (2 * g + part, 0)

    def place(g, f_ref):
        d = g ^ f_ref[0]
        return (d // 2 + (d % 2) * (groups // 2), 0)

    def kernel(f_ref, *refs):
        attention_kernel(width // HEAD, HEAD ** -0.5, *refs)

    return pl.pallas_call(
        kernel,
        grid_spec=pltpu.PrefetchScalarGridSpec(
            num_scalar_prefetch=1,
            grid=(groups,),
            in_specs=[
                pl.BlockSpec((rows, width), mine),
                pl.BlockSpec((1, width), lambda g, f_ref: (0, 0)),
                pl.BlockSpec((rows, HEAD), mine),
                pl.BlockSpec((rows, HEAD), mine),
                pl.BlockSpec((rows, 1), mine),
                pl.BlockSpec((rows, 1), mine),
                pl.BlockSpec((1, n_keys), lambda g, f_ref: (0, 0)),
                pl.BlockSpec((1, n_keys, HEAD), lambda g, f_ref: (g, 0, 0)),
                pl.BlockSpec((1, n_keys, HEAD), lambda g, f_ref: (g, 0, 1)),
            ],
            out_specs=pl.BlockSpec((rows, width), place),
        ),
        out_shape=jax.ShapeDtypeStruct((groups * rows, width), jnp.bfloat16),
        compiler_params=ROOM,
        cost_estimate=LIGHT,
    )(jnp.full((1,), f, jnp.int32), projected, bias, cosine, sine, starts, row_ids, columns,
      key_value, key_value)


def project(tokens, weights, total=None):
    n_rows, width = tokens.shape[0], weights[0].shape[1]
    block, n_w = min(512, n_rows), len(weights)

    def kernel(*refs):
        part, done = None, 0
        for ref in refs[1:1 + n_w]:
            depth = ref.shape[0]
            more = jnp.dot(
                refs[0][:, done:done + depth], ref[...], preferred_element_type=jnp.float32
            )
            part, done = more if part is None else part + more, done + depth
        refs[-1][...] = part if total is None else part + refs[1 + n_w][...]

    sums = pl.BlockSpec((block, width), lambda m: (m, 0))
    return pl.pallas_call(
        kernel,
        grid=(n_rows // block,),
        in_specs=[pl.BlockSpec((block, tokens.shape[1]), lambda m: (m, 0))]
        + [pl.BlockSpec(w.shape, lambda m: (0, 0)) for w in weights]
        + ([] if total is None else [sums]),
        out_specs=sums,
        out_shape=jax.ShapeDtypeStruct((n_rows, width), jnp.float32),
        input_output_aliases={} if total is None else {1 + n_w: 0},
        compiler_params=ROOM,
        cost_estimate=LIGHT,
    )(tokens, *weights, *([] if total is None else [total]))


def times_transposed(left, right):
    return lax.dot_general(
        left, right, (((1,), (1,)), ((), ())), preferred_element_type=jnp.float32
    ).astype(jnp.bfloat16)


def partials_of_one(mixed, first, second, take_first):
    n_rows, depth = mixed.shape
    width = first.shape[0]
    block = n_rows // 2

    def kernel(take_ref, mixed_ref, first_ref, second_ref, kept_ref, given_ref):
        def multiply(weight_ref, out_ref):
            out_ref[...] = times_transposed(mixed_ref[...], weight_ref[...])

        for taken, weight_ref in ((1, first_ref), (0, second_ref)):
            for half, out_ref in enumerate((given_ref, kept_ref)):
                chosen = (take_ref[0] == taken) & (pl.program_id(0) == half)
                pl.when(chosen)(functools.partial(multiply, weight_ref, out_ref))

    whole = lambda m, take_ref: (0, 0)
    return pl.pallas_call(
        kernel,
        grid_spec=pltpu.PrefetchScalarGridSpec(
            num_scalar_prefetch=1,
            grid=(2,),
            in_specs=[
                pl.BlockSpec((block, depth), lambda m, take_ref: (1 - m, 0)),
                pl.BlockSpec((width, depth), whole),
                pl.BlockSpec((width, depth), whole),
            ],
            out_specs=[pl.BlockSpec((block, width), whole)] * 2,
        ),
        out_shape=[jax.ShapeDtypeStruct((block, width), jnp.bfloat16)] * 2,
        compiler_params=ROOM,
        cost_estimate=LIGHT,
    )(jnp.full((1,), take_first, jnp.int32), mixed, first, second)


def partials_of_two(mixed_a, mixed_b, weight):
    n_rows, depth = mixed_a.shape
    width = weight.shape[0]
    block = n_rows // 2

    def kernel(a_ref, b_ref, weight_ref, kept_ref, given_ref):
        step = pl.program_id(0)
        for place, mixed_ref in enumerate((a_ref, b_ref)):
            for half, out_ref in enumerate((given_ref, kept_ref)):
                def multiply(mixed_ref=mixed_ref, out_ref=out_ref):
                    out_ref[0] = times_transposed(mixed_ref[...], weight_ref[...])

                pl.when(step == 2 * half + place)(multiply)

    rows = pl.BlockSpec((block, depth), lambda m: (1 - m // 2, 0))
    return pl.pallas_call(
        kernel,
        grid=(4,),
        in_specs=[rows, rows, pl.BlockSpec((width, depth), lambda m: (0, 0))],
        out_specs=[
            pl.BlockSpec((1, block, width), lambda m: (jnp.maximum(m - 2, 0), 0, 0)),
            pl.BlockSpec((1, block, width), lambda m: (jnp.minimum(m, 1), 0, 0)),
        ],
        out_shape=[jax.ShapeDtypeStruct((2, block, width), jnp.bfloat16)] * 2,
        compiler_params=ROOM,
        cost_estimate=LIGHT,
    )(mixed_a, mixed_b, weight)


def add_up(result, hidden, terms, other, use_terms, level, n_t, cuts, cut, h, first):
    rows = result.shape[0]
    count = terms[-1].shape[1] // cut
    wide = lambda term: term.astype(jnp.float32)
    if cut % 128:
        total = sum(wide(term[:rows]) for term in terms)
        if other is not None:
            total = jnp.where(use_terms, total, wide(other))
        for i in range(count):
            column = ((first + i) * n_t + level) * cuts * cut + h * cut
            before = wide(lax.dynamic_slice_in_dim(hidden, column, cut, 1))
            result = lax.dynamic_update_slice_in_dim(
                result, (before + total[:, i * cut:(i + 1) * cut]).astype(jnp.bfloat16), column, 1)
        return result

    def kernel(at_ref, result_ref, hidden_ref, *refs):
        total = sum(wide(ref[...]) for ref in refs[:len(terms)])
        if other is not None:
            total = jnp.where(at_ref[1] == 1, total, wide(refs[len(terms)][...]))
        refs[-1][...] = (wide(hidden_ref[...]) + total).astype(jnp.bfloat16)

    place = pl.BlockSpec(
        (rows, cut), lambda i, at_ref: (0, ((first + i) * n_t + at_ref[0]) * cuts + h))
    extra = [] if other is None else [other]
    return pl.pallas_call(
        kernel,
        grid_spec=pltpu.PrefetchScalarGridSpec(
            num_scalar_prefetch=1,
            grid=(count,),
            in_specs=[pl.BlockSpec(memory_space=pl.ANY), place]
            + [pl.BlockSpec((rows, cut), lambda i, at_ref: (0, i))] * (len(terms) + len(extra)),
            out_specs=place,
        ),
        out_shape=jax.ShapeDtypeStruct(result.shape, result.dtype),
        input_output_aliases={1: 0},
        compiler_params=ROOM,
        cost_estimate=LIGHT,
    )(jnp.stack([level, use_terms.astype(jnp.int32)]), result, hidden, *terms, *extra)


def per_device(
    hidden_in,
    segment_ids,
    norm_gain,
    query_weight,
    key_weight,
    value_weight,
    output_weight,
    query_bias,
    key_bias,
    value_bias,
):
    n_f, n_t = lax.axis_size("fsdp"), lax.axis_size("tp")
    f, t = lax.axis_index("fsdp"), lax.axis_index("tp")
    rows, width = hidden_in.shape
    depth = query_weight.shape[0]
    q_cols = query_weight.shape[1] // n_f
    kv_heads = key_weight.shape[1] // HEAD
    kv_head = f * kv_heads // n_f
    cuts = max(1, depth // 256)
    cut = depth // cuts
    n_pairs = n_t // 2
    inner = [2 * j + 1 - j % 2 for j in range(n_pairs)]
    outer = [2 * j + j % 2 for j in range(n_pairs)]
    pair = t // 2
    my_inner = 2 * pair + 1 - pair % 2
    my_outer = 2 * pair + pair % 2
    is_inner = t == my_inner
    inward = [(outer[j], inner[j]) for j in range(n_pairs)]
    outward = [(inner[j], outer[j]) for j in range(n_pairs)]
    every = list(range(n_t))
    tie = lax.optimization_barrier

    def shift(s):
        return [(inner[(j + s) % n_pairs], inner[j]) for j in range(n_pairs)]

    def send(value, pairs):
        return lax.ppermute(value, "tp", pairs)

    def swap(value, d, levels):
        return lax.ppermute(value, LEVEL, [
            (i * n_t + z, (i ^ d) * n_t + z) for i in range(n_f) for z in levels
        ])

    order = []
    for s in range(n_pairs):
        p = (pair + s) % n_pairs
        order += [2 * p + 1 - p % 2, 2 * p + p % 2]

    def by_index(pieces):
        bit = 1
        while bit < n_f:
            here = (f & bit) != 0
            pieces = [jnp.where(here, pieces[d ^ bit], pieces[d]) for d in range(n_f)]
            bit *= 2
        return jnp.concatenate(pieces, axis=0)

    def level_exchange(block_for, levels):
        return by_index([block_for(f)] + [
            swap(block_for(f ^ d), d, levels) for d in range(1, n_f)
        ])

    def projection_block(weights, h):
        def block(c):
            head = c * kv_heads // n_f
            span = slice(h * cut, (h + 1) * cut)
            return jnp.concatenate([
                lax.dynamic_slice_in_dim(weights[0][span], c * q_cols, q_cols, 1),
                lax.dynamic_slice_in_dim(weights[1][span], head * HEAD, HEAD, 1),
                lax.dynamic_slice_in_dim(weights[2][span], head * HEAD, HEAD, 1),
            ], axis=1)
        return block

    segments = lax.all_gather(segment_ids, "tp", axis=0, tiled=True)
    segments, hidden, output_weight, weights = tie(
        (segments, hidden_in, output_weight, (query_weight, key_weight, value_weight)))
    my_starts = lax.dynamic_slice_in_dim(segment_starts(segments), t * rows, rows)
    digits = jnp.stack([my_starts // 256, my_starts % 256], axis=1).astype(jnp.bfloat16)
    digits = jnp.pad(digits, ((0, 0), (0, HEAD - 2)))

    mine = normalize(hidden, norm_gain, order, n_f, depth, cuts)
    part = n_f * depth

    def gather(k, theirs, outputs):
        both = jnp.concatenate([mine[:, k * part:(k + 1) * part], theirs], axis=0)
        chunks = outputs.shape[1] // part
        outputs = jnp.concatenate(
            [outputs[:, c * part:(c + 1) * part] for c in range(chunks)], axis=0)
        payload = jnp.where(is_inner, both, outputs)
        if k == 0:
            payload = jnp.concatenate(
                [payload, jnp.concatenate([digits, their_digits], axis=0)], axis=1)
        return lax.all_gather(payload, "fsdp", axis=0, tiled=True)

    def output_rows(gathered, count):
        blocks = gathered[:, :part].reshape(n_f, -1, count, part)
        column = f * q_cols
        blocks = lax.dynamic_slice(
            blocks, (0, column // part, 0, column % part), (n_f, 1, count, q_cols))
        return blocks.reshape(n_f, count, q_cols)

    count = 2 * rows * part // output_weight.shape[1]
    early = max(width // 2, part)

    own = [level_exchange(projection_block(weights, 0), every)]
    head = send(jnp.concatenate([mine[:, :early], digits], axis=1), inward)
    raw = [send(output_weight[:cut], outward)]
    own, head, raw, mine, weights, output_weight = tie(
        (own, head, raw, mine, weights, output_weight))
    their_digits = head[:, early:]

    def source(k):
        runs = cut // count
        run, at = k // runs, (k % runs) * count
        h, level = run // 2, run % 2
        if h >= cuts:
            return jnp.zeros((count, output_weight.shape[1]), output_weight.dtype)
        some = raw[h] if level == 0 else output_weight[h * cut:(h + 1) * cut]
        return some[at:at + count]

    across = [send(own[0], shift(1))] if n_pairs > 1 else []
    own += [level_exchange(projection_block(weights, h), every) for h in range(1, cuts)]
    tail = send(mine[:, early:], inward)
    ahead = max(1, n_t // 2)
    gathered = [gather(k, head[:, k * part:(k + 1) * part], source(k)) for k in range(ahead)]
    own, across, tail, mine, output_weight, raw = tie((own, across, tail, mine, output_weight, raw))
    theirs = jnp.concatenate([head[:, :early], tail], axis=1)

    beyond = []
    projected = None
    for h in range(cuts):
        if n_pairs > 1 and h + 1 < cuts:
            across.append(send(own[h + 1], shift(1)))
        elif n_pairs > 1 and h:
            across.append(send(beyond[0], shift(1)))
        beyond.append(send(own[h], inward))
        if h + 1 < cuts:
            raw.append(send(output_weight[(h + 1) * cut:(h + 2) * cut], outward))
        if h == 0:
            projected = project(gathered[0], own)
        own, beyond, across, raw, output_weight, projected = tie(
            (own, beyond, across, raw, output_weight, projected))
    gathered += [
        gather(k, theirs[:, k * part:(k + 1) * part], source(k)) for k in range(ahead, n_t)
    ]

    def outer_run(r):
        return jnp.concatenate([
            output_rows(gathered[k], count)
            for k in range(r * (cut // count), (r + 1) * (cut // count))
        ], axis=1).reshape(-1, q_cols)

    at_outer = [outer_run(0)]
    at_inner = [send(at_outer[0], inward)]
    if n_pairs > 1:
        across += [send(w, shift(1)) for w in beyond[len(across) - cuts:]]
    projected = project(gathered[1], beyond, projected)
    if n_pairs > 1:
        projected = project(gathered[2], across[:cuts], projected)
    projected, across, at_inner, at_outer = tie((projected, across, at_inner, at_outer))

    groups = []
    half = n_f // 2
    for s in range(1, n_pairs):
        halves = [(s, r, p) for r in range(2 * cuts) for p in range(2)]
        inside = halves[1:-1]
        groups += [halves[:1]] + [inside[i:i + 2] for i in range(0, len(inside), 2)] + [halves[-1:]]

    def send_group(group):
        return send(jnp.concatenate([
            at_inner[r][p * half * cut:(p + 1) * half * cut] for _, r, p in group
        ], axis=0), shift(group[0][0]))

    arrived = {}

    def arrive(group, got):
        for place, (s, r, p) in enumerate(group):
            arrived[s, r, p] = got[place * half * cut:(place + 1) * half * cut]

    got = send_group(groups[0]) if groups else None
    if len(at_inner) < 2 * cuts:
        at_outer.append(outer_run(1))
        at_inner.append(send(at_outer[1], inward))
    for s in range(1, n_pairs):
        if s > 1:
            across = [send(w, shift(s)) for w in own + beyond]
            projected = project(gathered[2 * s], across[:cuts], projected)
        projected = project(gathered[2 * s + 1], across[cuts:], projected)

    level_ids = jnp.arange(rows, dtype=jnp.int32)
    pair_ids = jnp.concatenate([my_inner * rows + level_ids, my_outer * rows + level_ids])
    row_ids = jnp.tile(pair_ids, n_f)
    digits = gathered[0][:, part:part + 2].astype(jnp.int32)
    starts = digits[:, 0] * 256 + digits[:, 1]
    cosine, sine = rotary_tables((row_ids - starts).astype(jnp.float32))

    key_rows = projected[:, q_cols:q_cols + HEAD]
    key_rows = key_rows + lax.dynamic_slice_in_dim(key_bias, kv_head * HEAD, HEAD)
    turned = jnp.concatenate([key_rows[:, HEAD // 2:], key_rows[:, :HEAD // 2]], axis=-1)
    keys = (key_rows * cosine + turned * sine).astype(jnp.bfloat16)
    values = projected[:, q_cols + HEAD:] + lax.dynamic_slice_in_dim(value_bias, kv_head * HEAD, HEAD)
    values = values.astype(jnp.bfloat16)
    pair_rows = 2 * rows
    key_value = jnp.concatenate(
        [keys.reshape(n_f, pair_rows, HEAD), values.reshape(n_f, pair_rows, HEAD)], axis=-1
    )
    seen, columns = [key_value], [pair_ids]
    for s in range(1, min(n_pairs - 1, -(-(LONGEST - 1) // pair_rows)) + 1):
        seen.append(send(key_value, [(inner[j - s], inner[j]) for j in range(s, n_pairs)]))
        p = pair - s
        ids = jnp.concatenate([
            (2 * p + 1 - p % 2) * rows + level_ids, (2 * p + p % 2) * rows + level_ids
        ])
        columns.append(jnp.where(p >= 0, ids, NOWHERE))
    attend = functools.partial(
        attention, rows=rows, groups=n_f, width=q_cols, f=f, projected=projected,
        bias=lax.dynamic_slice_in_dim(query_bias, f * q_cols, q_cols)[None],
        cosine=cosine, sine=sine, starts=starts[:, None], row_ids=row_ids[:, None],
        columns=jnp.concatenate(columns)[None], key_value=jnp.concatenate(seen, axis=1),
    )
    def between_chips(kept, given):
        crossed = []
        for d in range(2, n_f, 2):
            span = slice(d // 2 * rows, (d // 2 + 1) * rows)
            share = kept[..., span, :].astype(jnp.float32) + given[..., span, :].astype(jnp.float32)
            crossed.append(swap(share.astype(jnp.bfloat16), d, every))
        return crossed

    def own_pair(result, r):
        kept, given = partials_of_one(mixed, at_inner[r], at_outer[r], is_inner)
        given = swap(given, 1, every)
        return [kept, given] + between_chips(kept, given)

    def other_pair(half_run):
        kept, given = partials_of_two(mixed_inner, mixed_outer, arrived[half_run])
        given = swap(given, 1, every)
        crossed = between_chips(kept, given)
        return [kept[:, :rows], given[:, :rows]] + crossed

    def put_own(result, r, terms):
        return add_up(result, hidden_in, terms, None, is_inner, order[r % 2], n_t, cuts, cut, r // 2, 0)

    def put_other(result, half_run, terms):
        s, r, p = half_run
        sums = sum(term[1].astype(jnp.float32) for term in terms).astype(jnp.bfloat16)
        return add_up(
            result, hidden_in, [term[0] for term in terms], send(sums, outward), is_inner,
            order[2 * s + r % 2], n_t, cuts, cut, r // 2, p * half)

    result = hidden_in
    key_value, got, at_inner, at_outer = tie((attend.keywords["key_value"], got, at_inner, at_outer))
    attend.keywords["key_value"] = key_value
    if groups:
        arrive(groups[0], got)
    mixed, waiting = None, list(groups[:1])
    phase = 1
    while phase < max(len(groups), 4):
        got = send_group(groups[phase]) if phase < len(groups) else None
        if len(at_inner) < 2 * cuts:
            at_outer.append(outer_run(len(at_inner)))
            at_inner.append(send(at_outer[-1], inward))
        if phase == 1:
            mixed_outer = attend(1)
            mixed_inner = attend(0)
            mixed_inner, mixed_outer, got, at_inner, at_outer = tie(
                (mixed_inner, mixed_outer, got, at_inner, at_outer))
        else:
            done = {}
            if phase == 2:
                mixed = jnp.where(is_inner, mixed_inner, send(mixed_outer, outward))
            if phase == 3:
                done = {r: own_pair(result, r) for r in range(2 * cuts)}
            else:
                done = {item: other_pair(item) for group in waiting for item in group}
                waiting = []
            done, mixed, got, at_inner, at_outer = tie((done, mixed, got, at_inner, at_outer))
            for item, terms in done.items():
                result = (put_own if phase == 3 else put_other)(result, item, terms)
        if got is not None:
            arrive(groups[phase], got)
            waiting.append(groups[phase])
        phase += 1
    for group in waiting:
        for item in group:
            result = put_other(result, item, other_pair(item))
    return result


def solution(mesh):
    return jax.shard_map(
        per_device,
        mesh=mesh,
        in_specs=(
            P(("groups", "fsdp", "tp"), None),
            P(("groups", "fsdp", "tp")),
            P("groups"),
            P(("groups", "fsdp", "tp"), None),
            P(("groups", "fsdp", "tp"), None),
            P(("groups", "fsdp", "tp"), None),
            P(("groups", "fsdp", "tp"), None),
            P("groups"),
            P("groups"),
            P("groups"),
        ),
        out_specs=P(("groups", "fsdp", "tp"), None),
        check_vma=False,
    )
```

time: 1070 us -> 864 us (0.81)
  waiting for transfers between devices: 661 us -> 304 us
  blocking collectives: 233 us -> 12.8 us
  Pallas kernels: 0 us -> 217 us
  starting transfers between devices: 8.53 us -> 136 us
  matrix products: 99.5 us -> 0 us
  local copies, waits for them, and re-layouts: 32.7 us -> 107 us
  other arithmetic: 19.3 us -> 59.3 us
    reduce_scatter x1 -> x0, waiting for transfers between devices: 280 us -> none  [per_device(): lax.psum_scatter(partials.astype(jnp.bfloat16), 'tp', scatter_dimension=0...]
    ppermute x0 -> x59, waiting for transfers between devices: none -> 258 us  [the longest x29 146 us: send(): return lax.ppermute(value, 'tp', pairs)]
    all_to_all x2 -> x0, blocking collectives: 225 us -> none  [the longest x1 204 us: per_device(): lax.all_to_all(query_weight, 'tp', split_axis=1, concat_axis=0, tiled=True)]
    pallas_call x0 -> x31, Pallas kernels: none -> 217 us  [the longest x4 68.2 us: project(): pl.pallas_call(kernel, grid=(n_rows // block,), in_specs=[pl.BlockSpec((b...]
    all_to_all x2 -> x0, waiting for transfers between devices: 205 us -> none  [the longest x1 188 us: per_device(): lax.all_to_all(output_weight, 'tp', split_axis=1, concat_axis=0, tiled=True)]
    ppermute x0 -> x59, starting transfers between devices: none -> 136 us  [the longest x29 119 us: send(): return lax.ppermute(value, 'tp', pairs)]
    all_gather x5 -> x4, waiting for transfers between devices: 176 us -> 46 us  [gather(): return lax.all_gather(payload, 'fsdp', axis=0, tiled=True)]
    dot_general x4 -> x0, matrix products: 79.2 us -> none  [the longest x1 24.1 us: per_device(): lax.dot_general(mixed, lax.all_gather(output_part, 'fsdp', axis=0, tiled=...]
  transfers between devices with their start and end apart: 8 -> 63, of which waited for: 6 -> 20; matrix products, arithmetic and copies ran while one was open for 11% -> 15% of each run, Pallas kernels for 0% -> 23%
where the time goes in v1:
time: 864 us; the launch traced here: 852 us
  waiting for transfers between devices  304 us (35%)
  Pallas kernels  217 us (25%)
  starting transfers between devices  136 us (16%)
  local copies, waits for them, and re-layouts  107 us (12%)
  other arithmetic  59.3 us (7%)
  between operations  14.6 us (2%)
  blocking collectives  12.8 us (1%)
    ppermute x29, waiting for transfers between devices, send(): return lax.ppermute(value, 'tp', pairs)  146 us
    ppermute x29, starting transfers between devices, send(): return lax.ppermute(value, 'tp', pairs)  119 us
    ppermute x30, waiting for transfers between devices, swap(): lax.ppermute(value, LEVEL, [(i * n_t + z, (i ^ d) * n_t + z) for i in ran...  112 us
    pallas_call x4, Pallas kernels, project(): pl.pallas_call(kernel, grid=(n_rows // block,), in_specs=[pl.BlockSpec((b...  68.2 us
    pallas_call x2, Pallas kernels, attention(): pl.pallas_call(kernel, grid_spec=pltpu.PrefetchScalarGridSpec(num_scalar_...  47.7 us
    all_gather x4, waiting for transfers between devices, gather(): return lax.all_gather(payload, 'fsdp', axis=0, tiled=True)  46 us
    pallas_call x8, Pallas kernels, partials_of_two(): pl.pallas_call(kernel, grid=(4,), in_specs=[rows, rows, pl.BlockSpec((wid...  44.7 us
    pallas_call x12, Pallas kernels, add_up(): pl.pallas_call(kernel, grid_spec=pltpu.PrefetchScalarGridSpec(num_scalar_...  29.2 us
  transfers between devices with their start and end apart: 63, of which 20 were waited for; matrix products, arithmetic and copies ran while one was open for 15% of the time, Pallas kernels for 23%

profile of v1, /device:TPU:0, one launch (start us, length us, event | category | flops | bytes accessed | tf_op | source)
XLA Modules:
  0.0 851.9 jit_solution(2251726150205632767)
XLA Ops:
  6.5 12.8 %all-gather = s32[4,1,256]{2,1,0:T(1,128)S(1)} all-gather(s32[1,1,256]{2,1,0:T(1,128)} %bitcast.118), channel_id=1, replica_groups=mesh['groups'=2,'fsdp'=4,'tp'=4] {'tp'}, dimensions={0}, use_global_device_ids=true | all-gather | bytes 5120 | tf_op jit(solution)/shard_map/all_gather | solution.py:345
  26.3 4.6 shard_map.100
  35.7 2.8 collective-permute-start.3
  43.5 15.0 %collective-permute-done.1 = bf16[256,1280]{1,0:T(8,128)(2,1)S(1)} collective-permute-done((bf16[256,1280]{1,0:T(8,128)(2,1)S(1)}, bf16[256,1280]{1,0:T(8,128)(2,1)S(1)}, u32[]{:S(2)}, u32[]{:S(2)}) %collective-permute-start.1) | collective-permute-done | bytes 655392 | tf_op jit(solution)/shard_map/ppermute | solution.py:312
  60.6 29.6 %collective-permute-done.4 = bf16[256,4096]{1,0:T(8,128)(2,1)} collective-permute-done((bf16[256,4096]{1,0:T(8,128)(2,1)}, bf16[256,4096]{1,0:T(8,128)(2,1)}, u32[]{:S(2)}, u32[]{:S(2)}) %collective-permute-start.4) | collective-permute-done | bytes 2097184 | tf_op jit(solution)/shard_map/ppermute | solution.py:309
  91.1 3.4 fusion.15
  101.3 2.3 maximum_select_fusion.3
  109.4 3.4 collective-permute-start.9
  114.6 30.0 %collective-permute-done.6 = bf16[256,1280]{1,0:T(8,128)(2,1)S(1)} collective-permute-done((bf16[256,1280]{1,0:T(8,128)(2,1)S(1)}, bf16[256,1280]{1,0:T(8,128)(2,1)S(1)}, u32[]{:S(2)}, u32[]{:S(2)}) %collective-permute-start.6) | collective-permute-done | bytes 655392 | tf_op jit(solution)/shard_map/ppermute | solution.py:312
  144.6 27.0 %collective-permute-done.5 = bf16[256,1280]{1,0:T(8,128)(2,1)S(1)} collective-permute-done((bf16[256,1280]{1,0:T(8,128)(2,1)S(1)}, bf16[256,1280]{1,0:T(8,128)(2,1)S(1)}, u32[]{:S(2)}, u32[]{:S(2)}) %collective-permute-start.5) | collective-permute-done | bytes 655392 | tf_op jit(solution)/shard_map/ppermute | solution.py:312
  174.0 3.5 collective-permute-start.10
  177.5 2.2 collective-permute-start.11
  182.4 5.4 all-gather.6.cloned.1.call-done.refs_0_
  187.9 15.7 %shard_map.101.refs_3_ = f32[2048,1280]{1,0:T(8,128)} custom-call(bf16[2048,2176]{1,0:T(8,128)(2,1)} %all-gather.6.cloned.1.call-done.refs_0_, bf16[1024,1280]{1,0:T(8,128)(2,1)S(1)} %pad_maximum_fusion.refs_1_, bf16[1024,1280]{1,0:T(8,128)(2,1)} %pad_maximum_fusion.1.refs_2_), custom_call_target="tpu_custom_call" | custom-call | flops 1 | bytes 1 | tf_op jit(solution)/shard_map/pallas_call | solution.py:150
  203.6 27.8 %collective-permute-done.12 = bf16[256,4096]{1,0:T(8,128)(2,1)} collective-permute-done((bf16[256,4096]{1,0:T(8,128)(2,1)}, bf16[256,4096]{1,0:T(8,128)(2,1)}, u32[]{:S(2)}, u32[]{:S(2)}) %collective-permute-start.12) | collective-permute-done | bytes 2097184 | tf_op jit(solution)/shard_map/ppermute | solution.py:309
  233.2 7.2 collective-permute-start.13
  240.4 11.5 %collective-permute-start.14 = (bf16[1024,1280]{1,0:T(8,128)(2,1)}, bf16[1024,1280]{1,0:T(8,128)(2,1)S(1)}, u32[]{:S(2)}, u32[]{:S(2)}) collective-permute-start(bf16[1024,1280]{1,0:T(8,128)(2,1)} %collective-permute-done.10.refs_1_), channel_id=1, source_target_pairs={{2,1},{1,2},{6,5},{5,6},{10,9},{9,10},{14,13},{13,14},{18,17},{17,... | collective-permute-start | bytes 7864328 | tf_op jit(solution)/shard_map/ppermute | solution.py:309
  252.4 43.0 %collective-permute-done.13.refs_2_ = bf16[1024,1280]{1,0:T(8,128)(2,1)} collective-permute-done((bf16[1024,1280]{1,0:T(8,128)(2,1)}, bf16[1024,1280]{1,0:T(8,128)(2,1)}, u32[]{:S(2)}, u32[]{:S(2)}) %collective-permute-start.13) | collective-permute-done | bytes 2621472 | tf_op jit(solution)/shard_map/ppermute | solution.py:309
  295.4 2.7 fusion.22
  298.2 2.4 maximum_select_fusion.2
  302.5 2.2 maximum_select_fusion
  304.7 2.2 collective-permute-start.15
  306.9 9.7 %slice.571 = bf16[2048,2048]{1,0:T(8,128)(2,1)} slice(bf16[2048,2176]{1,0:T(8,128)(2,1)} %all-gather.6.cloned.1.call-done.refs_0_), slice={[0:2048], [0:2048]} | slice | bytes 16777216 | tf_op jit(solution)/shard_map/slice | solution.py:367
  316.6 3.1 constant_dynamic-slice_fusion.3
  319.7 7.9 collective-permute-start.16
  329.6 3.1 constant_dynamic-slice_fusion.2
  332.7 2.6 collective-permute-start.19
  337.1 5.6 fusion.3
  342.7 17.8 %shard_map.102.refs_3_ = f32[2048,1280]{1,0:T(8,128)} custom-call(bf16[2048,2048]{1,0:T(8,128)(2,1)} %all-gather.12.cloned.1.call-done.refs_0_, bf16[1024,1280]{1,0:T(8,128)(2,1)} %collective-permute-done.10.refs_1_, bf16[1024,1280]{1,0:T(8,128)(2,1)} %collective-permute-done.13.refs_2_, f32[2048,1280]{1,0:T(8,128)} %shard_map.101.refs_3_), custom_call_target="tpu_custom_call", output_to_operand_aliasing={{}: (3, {})} | custom-call | flops 1 | bytes 1 | tf_op jit(solution)/shard_map/pallas_call | solution.py:150
  362.6 17.9 %shard_map.103.refs_3_ = f32[2048,1280]{1,0:T(8,128)} custom-call(bf16[2048,2048]{1,0:T(8,128)(2,1)} %all-gather.10.cloned.1.call-done.refs_0_, bf16[1024,1280]{1,0:T(8,128)(2,1)S(1)} %copy-done.7, bf16[1024,1280]{1,0:T(8,128)(2,1)} %collective-permute-done.11.refs_2_, f32[2048,1280]{1,0:T(8,128)} %shard_map.102.refs_3_), custom_call_target="tpu_custom_call", output_to_operand_aliasing={{}: (3, {})} | custom-call | flops 1 | bytes 1 | tf_op jit(solution)/shard_map/pallas_call | solution.py:150
  380.5 40.1 %all-gather.8.cloned.1.call-done.refs_0_ = bf16[2048,2048]{1,0:T(8,128)(2,1)} async-done(((bf16[512,2048]{1,0:T(8,128)(2,1)}), bf16[2048,2048]{1,0:T(8,128)(2,1)}) %all-gather.8.cloned.1.call-update) | async-done | bytes 8388624 | tf_op jit(solution)/shard_map/all_gather | solution.py:364
  422.4 16.8 %shard_map.104.refs_0_ = f32[2048,1280]{1,0:T(8,128)} custom-call(bf16[2048,2048]{1,0:T(8,128)(2,1)} %all-gather.8.cloned.1.call-done.refs_0_, bf16[1024,1280]{1,0:T(8,128)(2,1)S(1)} %copy-done.9, bf16[1024,1280]{1,0:T(8,128)(2,1)} %collective-permute-done.15.refs_2_, f32[2048,1280]{1,0:T(8,128)} %shard_map.103.refs_3_), custom_call_target="tpu_custom_call", output_to_operand_aliasing={{}: (3, {})} | custom-call | flops 1 | bytes 1 | tf_op jit(solution)/shard_map/pallas_call | solution.py:150
  448.1 7.4 collective-permute-start.21
  461.7 23.8 %shard_map.106.b_ref = bf16[1024,1024]{1,0:T(8,128)(2,1)} custom-call(s32[1]{0:T(128)} %bitcast.5.f_ref, f32[2048,1280]{1,0:T(8,128)} %shard_map.104.refs_0_, f32[1,1024]{1,0:T(1,128)S(1)} %bitcast.101, f32[2048,128]{1,0:T(8,128)S(1)} %get-tuple-element.299.refs_2_, f32[2048,128]{1,0:T(8,128)S(1)} %get-tuple-element.256.refs_3_, ...), custom_call_target="tpu_custom_call" | custom-call | flops 1 | bytes 1 | tf_op jit(solution)/shard_map/pallas_call | solution.py:110
  485.6 23.9 %shard_map.105.a_ref = bf16[1024,1024]{1,0:T(8,128)(2,1)} custom-call(s32[1]{0:T(128)} %bitcast.5.f_ref, f32[2048,1280]{1,0:T(8,128)} %shard_map.104.refs_0_, f32[1,1024]{1,0:T(1,128)S(1)} %bitcast.102, f32[2048,128]{1,0:T(8,128)S(1)} %get-tuple-element.299.refs_2_, f32[2048,128]{1,0:T(8,128)S(1)} %get-tuple-element.256.refs_3_, ...), custom_call_target="tpu_custom_call" | custom-call | flops 1 | bytes 1 | tf_op jit(solution)/shard_map/pallas_call | solution.py:110
  509.7 2.1 copy-done.2
  511.8 4.9 shard_map.109
  518.1 3.1 constant_dynamic-slice_fusion
  521.3 44.9 %collective-permute-start.30 = (bf16[1024,1024]{1,0:T(8,128)(2,1)}, bf16[1024,1024]{1,0:T(8,128)(2,1)}, u32[]{:S(2)}, u32[]{:S(2)}) collective-permute-start(bf16[1024,1024]{1,0:T(8,128)(2,1)} %bitcast.20.second_ref), channel_id=1, source_target_pairs={{0,1},{3,2},{4,5},{7,6},{8,9},{11,10},{12,13},{15,14},{16,17},{19,... | collective-permute-start | bytes 6291464 | tf_op jit(solution)/shard_map/ppermute | solution.py:309
  566.1 5.8 shard_map.108
  575.5 2.1 collective-permute-start.29
  577.5 5.8 shard_map.107
  591.9 13.0 %collective-permute-done.28 = bf16[1024,1024]{1,0:T(8,128)(2,1)} collective-permute-done((bf16[1024,1024]{1,0:T(8,128)(2,1)}, bf16[1024,1024]{1,0:T(8,128)(2,1)}, u32[]{:S(2)}, u32[]{:S(2)}) %collective-permute-start.28) | collective-permute-done | bytes 2097184 | tf_op jit(solution)/shard_map/ppermute | solution.py:309
  616.4 7.3 collective-permute-done.23
  625.2 6.0 shard_map.116
  634.7 6.0 shard_map.115
  641.2 5.8 shard_map.114
  647.1 5.2 shard_map.113
  666.3 5.8 shard_map.122
  676.8 5.8 shard_map.121
  683.9 11.0 %collective-permute-done.37.refs_2_ = bf16[256,1024]{1,0:T(8,128)(2,1)} collective-permute-done((bf16[256,1024]{1,0:T(8,128)(2,1)}, bf16[256,1024]{1,0:T(8,128)(2,1)}, u32[]{:S(2)}, u32[]{:S(2)}) %collective-permute-start.37) | collective-permute-done | bytes 524320 | tf_op jit(solution)/shard_map/ppermute | solution.py:312
  696.1 9.4 %collective-permute-done.35.refs_2_ = bf16[256,1024]{1,0:T(8,128)(2,1)} collective-permute-done((bf16[256,1024]{1,0:T(8,128)(2,1)}, bf16[256,1024]{1,0:T(8,128)(2,1)}, u32[]{:S(2)}, u32[]{:S(2)}) %collective-permute-start.35) | collective-permute-done | bytes 524320 | tf_op jit(solution)/shard_map/ppermute | solution.py:312
  707.2 6.0 shard_map.124
  715.2 5.9 shard_map.123
  731.5 2.4 slice.537
  750.9 2.4 shard_map.112.result_ref
  755.6 4.0 shard_map.117.result_ref
  759.6 4.1 shard_map.118.result_ref
  763.7 4.0 shard_map.119.result_ref
  767.7 3.8 shard_map.120.result_ref
  774.4 10.4 %collective-permute-done.48 = bf16[2,256,512]{2,1,0:T(8,128)(2,1)} collective-permute-done((bf16[2,256,512]{2,1,0:T(8,128)(2,1)}, bf16[2,256,512]{2,1,0:T(8,128)(2,1)}, u32[]{:S(2)}, u32[]{:S(2)}) %collective-permute-start.48) | collective-permute-done | bytes 524320 | tf_op jit(solution)/shard_map/ppermute | solution.py:312
  784.7 4.8 shard_map.129
  805.3 22.1 %collective-permute-done.52.refs_3_ = bf16[256,512]{1,0:T(8,128)(2,1)S(1)} collective-permute-done((bf16[256,512]{1,0:T(8,128)(2,1)S(1)}, bf16[256,512]{1,0:T(8,128)(2,1)S(1)}, u32[]{:S(2)}, u32[]{:S(2)}) %collective-permute-start.52) | collective-permute-done | bytes 262176 | tf_op jit(solution)/shard_map/ppermute | solution.py:309
  835.2 8.4 collective-permute-done.58.refs_3_
  (402 shorter events, 178.4 us)
Async XLA Ops:
  6.5 181.3 %all-gather.6.cloned.1.call-start = ((), (), s32[]{:S(2)}) async-start(), calls=%async_computation | async-start | bytes 11141120 | tf_op jit(solution)/shard_map/all_gather | solution.py:364
  26.2 17.3 %collective-permute-start = (bf16[256,1280]{1,0:T(8,128)(2,1)}, bf16[256,1280]{1,0:T(8,128)(2,1)}, u32[]{:S(2)}, u32[]{:S(2)}) collective-permute-start(bf16[256,1280]{1,0:T(8,128)(2,1)} %pad_maximum_fusion.10), channel_id=1, source_target_pairs={{0,12},{1,13},{2,14},{3,15},{4,8},{5,9},{6,10},{7,11},{8,4},{9,5},... | collective-permute-start | bytes 1966088 | tf_op jit(solution)/shard_map/ppermute | solution.py:312
  35.7 54.5 %collective-permute-start.3 = (bf16[256,4224]{1,0:T(8,128)(2,1)}, bf16[256,4224]{1,0:T(8,128)(2,1)}, u32[]{:S(2)}, u32[]{:S(2)}) collective-permute-start(bf16[256,4224]{1,0:T(8,128)(2,1)} %pad_maximum_fusion.2), channel_id=1, source_target_pairs={{0,1},{3,2},{4,5},{7,6},{8,9},{11,10},{12,13},{15,14},{16,17},{19,... | collective-permute-start | bytes 6488072 | tf_op jit(solution)/shard_map/ppermute | solution.py:309
  40.0 50.3 %collective-permute-start.4 = (bf16[256,4096]{1,0:T(8,128)(2,1)}, bf16[256,4096]{1,0:T(8,128)(2,1)}, u32[]{:S(2)}, u32[]{:S(2)}) collective-permute-start(bf16[256,4096]{1,0:T(8,128)(2,1)} %slice.439), channel_id=1, source_target_pairs={{1,0},{2,3},{5,4},{6,7},{9,8},{10,11},{13,12},{14,15},{17,16},{18,... | collective-permute-start | bytes 6291464 | tf_op jit(solution)/shard_map/ppermute | solution.py:309
  41.5 17.1 %collective-permute-start.1 = (bf16[256,1280]{1,0:T(8,128)(2,1)S(1)}, bf16[256,1280]{1,0:T(8,128)(2,1)S(1)}, u32[]{:S(2)}, u32[]{:S(2)}) collective-permute-start(bf16[256,1280]{1,0:T(8,128)(2,1)S(1)} %pad_maximum_fusion.11), channel_id=1, source_target_pairs={{0,8},{1,9},{2,10},{3,11},{4,12},{5,13},{6,14},{7,15},{8,0},{9,1},... | collective-permute-start | bytes 1966088 | tf_op jit(solution)/shard_map/ppermute | solution.py:312
  43.1 15.5 %collective-permute-start.2 = (bf16[256,1280]{1,0:T(8,128)(2,1)S(1)}, bf16[256,1280]{1,0:T(8,128)(2,1)S(1)}, u32[]{:S(2)}, u32[]{:S(2)}) collective-permute-start(bf16[256,1280]{1,0:T(8,128)(2,1)S(1)} %pad_maximum_fusion.12), channel_id=1, source_target_pairs={{0,4},{1,5},{2,6},{3,7},{4,0},{5,1},{6,2},{7,3},{8,12},{9,13},{10,... | collective-permute-start | bytes 1966088 | tf_op jit(solution)/shard_map/ppermute | solution.py:312
  99.0 230.5 %all-gather.12.cloned.1.call-start = ((), (), s32[]{:S(2)}) async-start(), calls=%async_computation.3 | async-start | bytes 10485760 | tf_op jit(solution)/shard_map/all_gather | solution.py:364
  103.6 257.3 %all-gather.10.cloned.1.call-start = ((), (), s32[]{:S(2)}) async-start(), calls=%async_computation.2 | async-start | bytes 10485760 | tf_op jit(solution)/shard_map/all_gather | solution.py:364
  103.6 70.4 %collective-permute-start.8 = (bf16[1024,1280]{1,0:T(8,128)(2,1)S(1)}, bf16[1024,1280]{1,0:T(8,128)(2,1)S(1)}, u32[]{:S(2)}, u32[]{:S(2)}) collective-permute-start(bf16[1024,1280]{1,0:T(8,128)(2,1)S(1)} %pad_maximum_fusion.refs_1_), channel_id=1, source_target_pairs={{2,1},{1,2},{6,5},{5,6},{10,9},{9,10},{14,13},{13,14},{18,17},{17,... | collective-permute-start | bytes 7864328 | tf_op jit(solution)/shard_map/ppermute | solution.py:309
  108.9 5.7 collective-permute-start.7
  109.4 64.6 %collective-permute-start.9 = (bf16[256,4096]{1,0:T(8,128)(2,1)S(1)}, bf16[256,4096]{1,0:T(8,128)(2,1)S(1)}, u32[]{:S(2)}, u32[]{:S(2)}) collective-permute-start(bf16[256,4096]{1,0:T(8,128)(2,1)S(1)} %slice.443), channel_id=1, source_target_pairs={{0,1},{3,2},{4,5},{7,6},{8,9},{11,10},{12,13},{15,14},{16,17},{19,... | collective-permute-start | bytes 6291464 | tf_op jit(solution)/shard_map/ppermute | solution.py:309
  112.9 31.7 %collective-permute-start.6 = (bf16[256,1280]{1,0:T(8,128)(2,1)S(1)}, bf16[256,1280]{1,0:T(8,128)(2,1)S(1)}, u32[]{:S(2)}, u32[]{:S(2)}) collective-permute-start(bf16[256,1280]{1,0:T(8,128)(2,1)S(1)} %pad_maximum_fusion.15), channel_id=1, source_target_pairs={{0,8},{1,9},{2,10},{3,11},{4,12},{5,13},{6,14},{7,15},{8,0},{9,1},... | collective-permute-start | bytes 1966088 | tf_op jit(solution)/shard_map/ppermute | solution.py:312
  114.1 57.5 %collective-permute-start.5 = (bf16[256,1280]{1,0:T(8,128)(2,1)S(1)}, bf16[256,1280]{1,0:T(8,128)(2,1)S(1)}, u32[]{:S(2)}, u32[]{:S(2)}) collective-permute-start(bf16[256,1280]{1,0:T(8,128)(2,1)S(1)} %pad_maximum_fusion.14), channel_id=1, source_target_pairs={{0,12},{1,13},{2,14},{3,15},{4,8},{5,9},{6,10},{7,11},{8,4},{9,5},... | collective-permute-start | bytes 1966088 | tf_op jit(solution)/shard_map/ppermute | solution.py:312
  174.0 59.2 %collective-permute-start.10 = (bf16[1024,1280]{1,0:T(8,128)(2,1)S(1)}, bf16[1024,1280]{1,0:T(8,128)(2,1)}, u32[]{:S(2)}, u32[]{:S(2)}) collective-permute-start(bf16[1024,1280]{1,0:T(8,128)(2,1)S(1)} %pad_maximum_fusion.refs_1_), channel_id=1, source_target_pairs={{0,1},{3,2},{4,5},{7,6},{8,9},{11,10},{12,13},{15,14},{16,17},{19,... | collective-permute-start | bytes 7864328 | tf_op jit(solution)/shard_map/ppermute | solution.py:309
  177.5 55.7 %collective-permute-start.11 = (bf16[1024,1280]{1,0:T(8,128)(2,1)}, bf16[1024,1280]{1,0:T(8,128)(2,1)}, u32[]{:S(2)}, u32[]{:S(2)}) collective-permute-start(bf16[1024,1280]{1,0:T(8,128)(2,1)} %pad_maximum_fusion.1.refs_2_), channel_id=1, source_target_pairs={{2,1},{1,2},{6,5},{5,6},{10,9},{9,10},{14,13},{13,14},{18,17},{17,... | collective-permute-start | bytes 7864328 | tf_op jit(solution)/shard_map/ppermute | solution.py:309
  181.2 50.2 %collective-permute-start.12 = (bf16[256,4096]{1,0:T(8,128)(2,1)}, bf16[256,4096]{1,0:T(8,128)(2,1)}, u32[]{:S(2)}, u32[]{:S(2)}) collective-permute-start(bf16[256,4096]{1,0:T(8,128)(2,1)} %slice.446), channel_id=1, source_target_pairs={{1,0},{2,3},{5,4},{6,7},{9,8},{10,11},{13,12},{14,15},{17,16},{18,... | collective-permute-start | bytes 6291464 | tf_op jit(solution)/shard_map/ppermute | solution.py:309
  233.2 62.3 %collective-permute-start.13 = (bf16[1024,1280]{1,0:T(8,128)(2,1)}, bf16[1024,1280]{1,0:T(8,128)(2,1)}, u32[]{:S(2)}, u32[]{:S(2)}) collective-permute-start(bf16[1024,1280]{1,0:T(8,128)(2,1)} %pad_maximum_fusion.1.refs_2_), channel_id=1, source_target_pairs={{0,1},{3,2},{4,5},{7,6},{8,9},{11,10},{12,13},{15,14},{16,17},{19,... | collective-permute-start | bytes 7864328 | tf_op jit(solution)/shard_map/ppermute | solution.py:309
  240.4 55.0 %collective-permute-start.14 = (bf16[1024,1280]{1,0:T(8,128)(2,1)}, bf16[1024,1280]{1,0:T(8,128)(2,1)S(1)}, u32[]{:S(2)}, u32[]{:S(2)}) collective-permute-start(bf16[1024,1280]{1,0:T(8,128)(2,1)} %collective-permute-done.10.refs_1_), channel_id=1, source_target_pairs={{2,1},{1,2},{6,5},{5,6},{10,9},{9,10},{14,13},{13,14},{18,17},{17,... | collective-permute-start | bytes 7864328 | tf_op jit(solution)/shard_map/ppermute | solution.py:309
  300.6 120.0 %all-gather.8.cloned.1.call-start = ((), (), s32[]{:S(2)}) async-start(), calls=%async_computation.1 | async-start | bytes 10485760 | tf_op jit(solution)/shard_map/all_gather | solution.py:364
  304.7 75.8 %collective-permute-start.15 = (bf16[1024,1280]{1,0:T(8,128)(2,1)}, bf16[1024,1280]{1,0:T(8,128)(2,1)}, u32[]{:S(2)}, u32[]{:S(2)}) collective-permute-start(bf16[1024,1280]{1,0:T(8,128)(2,1)} %collective-permute-done.13.refs_2_), channel_id=1, source_target_pairs={{2,1},{1,2},{6,5},{5,6},{10,9},{9,10},{14,13},{13,14},{18,17},{17,... | collective-permute-start | bytes 7864328 | tf_op jit(solution)/shard_map/ppermute | solution.py:309
  319.7 60.8 %collective-permute-start.16 = (bf16[1024,1024]{1,0:T(8,128)(2,1)}, bf16[1024,1024]{1,0:T(8,128)(2,1)}, u32[]{:S(2)}, u32[]{:S(2)}) collective-permute-start(bf16[1024,1024]{1,0:T(8,128)(2,1)} %bitcast.10.second_ref), channel_id=1, source_target_pairs={{0,1},{3,2},{4,5},{7,6},{8,9},{11,10},{12,13},{15,14},{16,17},{19,... | collective-permute-start | bytes 6291464 | tf_op jit(solution)/shard_map/ppermute | solution.py:309
  332.7 124.3 %collective-permute-start.19 = (bf16[1024,1024]{1,0:T(8,128)(2,1)}, bf16[1024,1024]{1,0:T(8,128)(2,1)}, u32[]{:S(2)}, u32[]{:S(2)}) collective-permute-start(bf16[1024,1024]{1,0:T(8,128)(2,1)} %bitcast.16.second_ref), channel_id=1, source_target_pairs={{0,1},{3,2},{4,5},{7,6},{8,9},{11,10},{12,13},{15,14},{16,17},{19,... | collective-permute-start | bytes 6291464 | tf_op jit(solution)/shard_map/ppermute | solution.py:309
  443.5 12.0 %collective-permute-start.17 = (bf16[4,512,256]{2,1,0:T(8,128)(2,1)S(1)}, bf16[4,512,256]{2,1,0:T(8,128)(2,1)S(1)}, u32[]{:S(2)}, u32[]{:S(2)}) collective-permute-start(bf16[4,512,256]{2,1,0:T(8,128)(2,1)S(1)} %pad_maximum_fusion.9), channel_id=1, source_target_pairs={{1,2},{5,6},{9,10},{13,14},{17,18},{21,22},{25,26},{29,30}} | collective-permute-start | bytes 3145736 | tf_op jit(solution)/shard_map/ppermute | solution.py:309
  445.5 11.5 %collective-permute-start.18 = (bf16[512,1024]{1,0:T(8,128)(2,1)S(1)}, bf16[512,1024]{1,0:T(8,128)(2,1)S(1)}, u32[]{:S(2)}, u32[]{:S(2)}) collective-permute-start(bf16[512,1024]{1,0:T(8,128)(2,1)S(1)} %slice.470), channel_id=1, source_target_pairs={{2,1},{1,2},{6,5},{5,6},{10,9},{9,10},{14,13},{13,14},{18,17},{17,... | collective-permute-start | bytes 3145736 | tf_op jit(solution)/shard_map/ppermute | solution.py:309
  448.1 61.4 %collective-permute-start.21 = (bf16[1024,1024]{1,0:T(8,128)(2,1)S(1)}, bf16[1024,1024]{1,0:T(8,128)(2,1)S(1)}, u32[]{:S(2)}, u32[]{:S(2)}) collective-permute-start(bf16[1024,1024]{1,0:T(8,128)(2,1)S(1)} %bitcast.110), channel_id=1, source_target_pairs={{0,1},{3,2},{4,5},{7,6},{8,9},{11,10},{12,13},{15,14},{16,17},{19,... | collective-permute-start | bytes 6291464 | tf_op jit(solution)/shard_map/ppermute | solution.py:309
  459.8 49.7 %collective-permute-start.20 = (bf16[1024,1024]{1,0:T(8,128)(2,1)S(1)}, bf16[1024,1024]{1,0:T(8,128)(2,1)S(1)}, u32[]{:S(2)}, u32[]{:S(2)}) collective-permute-start(bf16[1024,1024]{1,0:T(8,128)(2,1)S(1)} %pad_maximum_fusion.4), channel_id=1, source_target_pairs={{2,1},{1,2},{6,5},{5,6},{10,9},{9,10},{14,13},{13,14},{18,17},{17,... | collective-permute-start | bytes 6291464 | tf_op jit(solution)/shard_map/ppermute | solution.py:309
  509.5 64.1 %copy-start.45 = (bf16[1024,1024]{1,0:T(8,128)(2,1)}, bf16[1024,1024]{1,0:T(8,128)(2,1)S(1)}, u32[]{:S(2)}) copy-start(bf16[1024,1024]{1,0:T(8,128)(2,1)S(1)} %collective-permute-done.21.first_ref) | copy-start | bytes 6291460
  516.8 67.6 %collective-permute-start.26 = (bf16[2,512,512]{2,1,0:T(8,128)(2,1)S(1)}, bf16[2,512,512]{2,1,0:T(8,128)(2,1)S(1)}, u32[]{:S(2)}, u32[]{:S(2)}) collective-permute-start(bf16[2,512,512]{2,1,0:T(8,128)(2,1)S(1)} %get-tuple-element.184), channel_id=1, source_target_pairs={{0,4},{1,5},{2,6},{3,7},{4,0},{5,1},{6,2},{7,3},{8,12},{9,13},{10,... | collective-permute-start | bytes 3145736 | tf_op jit(solution)/shard_map/ppermute | solution.py:312
  516.8 88.1 %collective-permute-start.28 = (bf16[1024,1024]{1,0:T(8,128)(2,1)}, bf16[1024,1024]{1,0:T(8,128)(2,1)}, u32[]{:S(2)}, u32[]{:S(2)}) collective-permute-start(bf16[1024,1024]{1,0:T(8,128)(2,1)} %shard_map.106.b_ref), channel_id=1, source_target_pairs={{1,0},{2,3},{5,4},{6,7},{9,8},{10,11},{13,12},{14,15},{17,16},{18,... | collective-permute-start | bytes 6291464 | tf_op jit(solution)/shard_map/ppermute | solution.py:309
  521.3 95.0 %collective-permute-start.30 = (bf16[1024,1024]{1,0:T(8,128)(2,1)}, bf16[1024,1024]{1,0:T(8,128)(2,1)}, u32[]{:S(2)}, u32[]{:S(2)}) collective-permute-start(bf16[1024,1024]{1,0:T(8,128)(2,1)} %bitcast.20.second_ref), channel_id=1, source_target_pairs={{0,1},{3,2},{4,5},{7,6},{8,9},{11,10},{12,13},{15,14},{16,17},{19,... | collective-permute-start | bytes 6291464 | tf_op jit(solution)/shard_map/ppermute | solution.py:309
  573.7 13.4 %collective-permute-start.24 = (bf16[2,512,512]{2,1,0:T(8,128)(2,1)}, bf16[2,512,512]{2,1,0:T(8,128)(2,1)}, u32[]{:S(2)}, u32[]{:S(2)}) collective-permute-start(bf16[2,512,512]{2,1,0:T(8,128)(2,1)} %get-tuple-element.182), channel_id=1, source_target_pairs={{0,4},{1,5},{2,6},{3,7},{4,0},{5,1},{6,2},{7,3},{8,12},{9,13},{10,... | collective-permute-start | bytes 3145736 | tf_op jit(solution)/shard_map/ppermute | solution.py:312
  575.5 48.2 %collective-permute-start.29 = (bf16[1024,1024]{1,0:T(8,128)(2,1)}, bf16[1024,1024]{1,0:T(8,128)(2,1)}, u32[]{:S(2)}, u32[]{:S(2)}) collective-permute-start(bf16[1024,1024]{1,0:T(8,128)(2,1)} %pad_maximum_fusion.5), channel_id=1, source_target_pairs={{2,1},{1,2},{6,5},{5,6},{10,9},{9,10},{14,13},{13,14},{18,17},{17,... | collective-permute-start | bytes 6291464 | tf_op jit(solution)/shard_map/ppermute | solution.py:309
  585.3 3.8 collective-permute-start.22
  587.1 29.2 %collective-permute-start.27 = (bf16[2,256,512]{2,1,0:T(8,128)(2,1)S(1)}, bf16[2,256,512]{2,1,0:T(8,128)(2,1)S(1)}, u32[]{:S(2)}, u32[]{:S(2)}) collective-permute-start(bf16[2,256,512]{2,1,0:T(8,128)(2,1)S(1)} %add_convert_fusion.9), channel_id=1, source_target_pairs={{0,8},{1,9},{2,10},{3,11},{4,12},{5,13},{6,14},{7,15},{8,0},{9,1},... | collective-permute-start | bytes 1572872 | tf_op jit(solution)/shard_map/ppermute | solution.py:312
  589.1 27.3 %collective-permute-start.25 = (bf16[2,256,512]{2,1,0:T(8,128)(2,1)S(1)}, bf16[2,256,512]{2,1,0:T(8,128)(2,1)S(1)}, u32[]{:S(2)}, u32[]{:S(2)}) collective-permute-start(bf16[2,256,512]{2,1,0:T(8,128)(2,1)S(1)} %add_convert_fusion.10), channel_id=1, source_target_pairs={{0,8},{1,9},{2,10},{3,11},{4,12},{5,13},{6,14},{7,15},{8,0},{9,1},... | collective-permute-start | bytes 1572872 | tf_op jit(solution)/shard_map/ppermute | solution.py:312
  604.9 18.7 %collective-permute-start.23 = (bf16[2,256,512]{2,1,0:T(8,128)(2,1)S(1)}, bf16[2,256,512]{2,1,0:T(8,128)(2,1)S(1)}, u32[]{:S(2)}, u32[]{:S(2)}) collective-permute-start(bf16[2,256,512]{2,1,0:T(8,128)(2,1)S(1)} %add_convert_fusion.11), channel_id=1, source_target_pairs={{0,8},{1,9},{2,10},{3,11},{4,12},{5,13},{6,14},{7,15},{8,0},{9,1},... | collective-permute-start | bytes 1572872 | tf_op jit(solution)/shard_map/ppermute | solution.py:312
  631.2 25.2 %collective-permute-start.40 = (bf16[512,1024]{1,0:T(8,128)(2,1)}, bf16[512,1024]{1,0:T(8,128)(2,1)S(1)}, u32[]{:S(2)}, u32[]{:S(2)}) collective-permute-start(bf16[512,1024]{1,0:T(8,128)(2,1)} %get-tuple-element.216), channel_id=1, source_target_pairs={{0,4},{1,5},{2,6},{3,7},{4,0},{5,1},{6,2},{7,3},{8,12},{9,13},{10,... | collective-permute-start | bytes 3145736 | tf_op jit(solution)/shard_map/ppermute | solution.py:312
  632.7 72.8 %collective-permute-start.42 = (bf16[1024,1024]{1,0:T(8,128)(2,1)}, bf16[1024,1024]{1,0:T(8,128)(2,1)}, u32[]{:S(2)}, u32[]{:S(2)}) collective-permute-start(bf16[1024,1024]{1,0:T(8,128)(2,1)} %pad_maximum_fusion.6), channel_id=1, source_target_pairs={{2,1},{1,2},{6,5},{5,6},{10,9},{9,10},{14,13},{13,14},{18,17},{17,... | collective-permute-start | bytes 6291464 | tf_op jit(solution)/shard_map/ppermute | solution.py:309
  640.7 17.2 %collective-permute-start.38 = (bf16[512,1024]{1,0:T(8,128)(2,1)}, bf16[512,1024]{1,0:T(8,128)(2,1)S(1)}, u32[]{:S(2)}, u32[]{:S(2)}) collective-permute-start(bf16[512,1024]{1,0:T(8,128)(2,1)} %get-tuple-element.212), channel_id=1, source_target_pairs={{0,4},{1,5},{2,6},{3,7},{4,0},{5,1},{6,2},{7,3},{8,12},{9,13},{10,... | collective-permute-start | bytes 3145736 | tf_op jit(solution)/shard_map/ppermute | solution.py:312
  647.1 13.3 %collective-permute-start.36 = (bf16[512,1024]{1,0:T(8,128)(2,1)}, bf16[512,1024]{1,0:T(8,128)(2,1)}, u32[]{:S(2)}, u32[]{:S(2)}) collective-permute-start(bf16[512,1024]{1,0:T(8,128)(2,1)} %get-tuple-element.208), channel_id=1, source_target_pairs={{0,4},{1,5},{2,6},{3,7},{4,0},{5,1},{6,2},{7,3},{8,12},{9,13},{10,... | collective-permute-start | bytes 3145736 | tf_op jit(solution)/shard_map/ppermute | solution.py:312
  652.4 10.6 %collective-permute-start.34 = (bf16[512,1024]{1,0:T(8,128)(2,1)S(1)}, bf16[512,1024]{1,0:T(8,128)(2,1)S(1)}, u32[]{:S(2)}, u32[]{:S(2)}) collective-permute-start(bf16[512,1024]{1,0:T(8,128)(2,1)S(1)} %get-tuple-element.204), channel_id=1, source_target_pairs={{0,4},{1,5},{2,6},{3,7},{4,0},{5,1},{6,2},{7,3},{8,12},{9,13},{10,... | collective-permute-start | bytes 3145736 | tf_op jit(solution)/shard_map/ppermute | solution.py:312
  657.3 17.6 %collective-permute-start.41 = (bf16[256,1024]{1,0:T(8,128)(2,1)}, bf16[256,1024]{1,0:T(8,128)(2,1)S(1)}, u32[]{:S(2)}, u32[]{:S(2)}) collective-permute-start(bf16[256,1024]{1,0:T(8,128)(2,1)} %add_convert_fusion.5), channel_id=1, source_target_pairs={{0,8},{1,9},{2,10},{3,11},{4,12},{5,13},{6,14},{7,15},{8,0},{9,1},... | collective-permute-start | bytes 1572872 | tf_op jit(solution)/shard_map/ppermute | solution.py:312
  658.9 24.7 %collective-permute-start.39 = (bf16[256,1024]{1,0:T(8,128)(2,1)}, bf16[256,1024]{1,0:T(8,128)(2,1)}, u32[]{:S(2)}, u32[]{:S(2)}) collective-permute-start(bf16[256,1024]{1,0:T(8,128)(2,1)} %add_convert_fusion.6), channel_id=1, source_target_pairs={{0,8},{1,9},{2,10},{3,11},{4,12},{5,13},{6,14},{7,15},{8,0},{9,1},... | collective-permute-start | bytes 1572872 | tf_op jit(solution)/shard_map/ppermute | solution.py:312
  662.4 32.5 %collective-permute-start.37 = (bf16[256,1024]{1,0:T(8,128)(2,1)}, bf16[256,1024]{1,0:T(8,128)(2,1)}, u32[]{:S(2)}, u32[]{:S(2)}) collective-permute-start(bf16[256,1024]{1,0:T(8,128)(2,1)} %add_convert_fusion.7), channel_id=1, source_target_pairs={{0,8},{1,9},{2,10},{3,11},{4,12},{5,13},{6,14},{7,15},{8,0},{9,1},... | collective-permute-start | bytes 1572872 | tf_op jit(solution)/shard_map/ppermute | solution.py:312
  664.1 41.4 %collective-permute-start.35 = (bf16[256,1024]{1,0:T(8,128)(2,1)}, bf16[256,1024]{1,0:T(8,128)(2,1)}, u32[]{:S(2)}, u32[]{:S(2)}) collective-permute-start(bf16[256,1024]{1,0:T(8,128)(2,1)} %add_convert_fusion.8), channel_id=1, source_target_pairs={{0,8},{1,9},{2,10},{3,11},{4,12},{5,13},{6,14},{7,15},{8,0},{9,1},... | collective-permute-start | bytes 1572872 | tf_op jit(solution)/shard_map/ppermute | solution.py:312
  674.9 49.9 %collective-permute-start.45 = (bf16[2,512,512]{2,1,0:T(8,128)(2,1)}, bf16[2,512,512]{2,1,0:T(8,128)(2,1)}, u32[]{:S(2)}, u32[]{:S(2)}) collective-permute-start(bf16[2,512,512]{2,1,0:T(8,128)(2,1)} %get-tuple-element.233), channel_id=1, source_target_pairs={{0,4},{1,5},{2,6},{3,7},{4,0},{5,1},{6,2},{7,3},{8,12},{9,13},{10,... | collective-permute-start | bytes 3145736 | tf_op jit(solution)/shard_map/ppermute | solution.py:312
  683.6 44.5 %collective-permute-start.43 = (bf16[2,512,512]{2,1,0:T(8,128)(2,1)}, bf16[2,512,512]{2,1,0:T(8,128)(2,1)}, u32[]{:S(2)}, u32[]{:S(2)}) collective-permute-start(bf16[2,512,512]{2,1,0:T(8,128)(2,1)} %get-tuple-element.231), channel_id=1, source_target_pairs={{0,4},{1,5},{2,6},{3,7},{4,0},{5,1},{6,2},{7,3},{8,12},{9,13},{10,... | collective-permute-start | bytes 3145736 | tf_op jit(solution)/shard_map/ppermute | solution.py:312
  694.9 43.4 %collective-permute-start.33 = (bf16[256,512]{1,0:T(8,128)(2,1)}, bf16[256,512]{1,0:T(8,128)(2,1)}, u32[]{:S(2)}, u32[]{:S(2)}) collective-permute-start(bf16[256,512]{1,0:T(8,128)(2,1)} %fusion.6), channel_id=1, source_target_pairs={{1,0},{2,3},{5,4},{6,7},{9,8},{10,11},{13,12},{14,15},{17,16},{18,... | collective-permute-start | bytes 786440 | tf_op jit(solution)/shard_map/ppermute | solution.py:309
  714.2 19.7 %collective-permute-start.49 = (bf16[2,512,512]{2,1,0:T(8,128)(2,1)}, bf16[2,512,512]{2,1,0:T(8,128)(2,1)}, u32[]{:S(2)}, u32[]{:S(2)}) collective-permute-start(bf16[2,512,512]{2,1,0:T(8,128)(2,1)} %get-tuple-element.238), channel_id=1, source_target_pairs={{0,4},{1,5},{2,6},{3,7},{4,0},{5,1},{6,2},{7,3},{8,12},{9,13},{10,... | collective-permute-start | bytes 3145736 | tf_op jit(solution)/shard_map/ppermute | solution.py:312
  722.1 14.7 %collective-permute-start.47 = (bf16[2,512,512]{2,1,0:T(8,128)(2,1)}, bf16[2,512,512]{2,1,0:T(8,128)(2,1)S(1)}, u32[]{:S(2)}, u32[]{:S(2)}) collective-permute-start(bf16[2,512,512]{2,1,0:T(8,128)(2,1)} %get-tuple-element.236), channel_id=1, source_target_pairs={{0,4},{1,5},{2,6},{3,7},{4,0},{5,1},{6,2},{7,3},{8,12},{9,13},{10,... | collective-permute-start | bytes 3145736 | tf_op jit(solution)/shard_map/ppermute | solution.py:312
  724.8 15.0 %collective-permute-start.32 = (bf16[256,512]{1,0:T(8,128)(2,1)}, bf16[256,512]{1,0:T(8,128)(2,1)S(1)}, u32[]{:S(2)}, u32[]{:S(2)}) collective-permute-start(bf16[256,512]{1,0:T(8,128)(2,1)} %fusion.5), channel_id=1, source_target_pairs={{1,0},{2,3},{5,4},{6,7},{9,8},{10,11},{13,12},{14,15},{17,16},{18,... | collective-permute-start | bytes 786440 | tf_op jit(solution)/shard_map/ppermute | solution.py:309
  728.1 12.7 %collective-permute-start.31 = (bf16[256,512]{1,0:T(8,128)(2,1)S(1)}, bf16[256,512]{1,0:T(8,128)(2,1)S(1)}, u32[]{:S(2)}, u32[]{:S(2)}) collective-permute-start(bf16[256,512]{1,0:T(8,128)(2,1)S(1)} %fusion.4), channel_id=1, source_target_pairs={{1,0},{2,3},{5,4},{6,7},{9,8},{10,11},{13,12},{14,15},{17,16},{18,... | collective-permute-start | bytes 786440 | tf_op jit(solution)/shard_map/ppermute | solution.py:309
  733.9 39.1 %collective-permute-start.51 = (bf16[512,1024]{1,0:T(8,128)(2,1)}, bf16[512,1024]{1,0:T(8,128)(2,1)S(1)}, u32[]{:S(2)}, u32[]{:S(2)}) collective-permute-start(bf16[512,1024]{1,0:T(8,128)(2,1)} %slice.537), channel_id=1, source_target_pairs={{2,1},{1,2},{6,5},{5,6},{10,9},{9,10},{14,13},{13,14},{18,17},{17,... | collective-permute-start | bytes 3145736 | tf_op jit(solution)/shard_map/ppermute | solution.py:309
  736.8 36.1 %collective-permute-start.46 = (bf16[2,256,512]{2,1,0:T(8,128)(2,1)}, bf16[2,256,512]{2,1,0:T(8,128)(2,1)}, u32[]{:S(2)}, u32[]{:S(2)}) collective-permute-start(bf16[2,256,512]{2,1,0:T(8,128)(2,1)} %add_convert_fusion.3), channel_id=1, source_target_pairs={{0,8},{1,9},{2,10},{3,11},{4,12},{5,13},{6,14},{7,15},{8,0},{9,1},... | collective-permute-start | bytes 1572872 | tf_op jit(solution)/shard_map/ppermute | solution.py:312
  738.3 34.6 %collective-permute-start.44 = (bf16[2,256,512]{2,1,0:T(8,128)(2,1)}, bf16[2,256,512]{2,1,0:T(8,128)(2,1)}, u32[]{:S(2)}, u32[]{:S(2)}) collective-permute-start(bf16[2,256,512]{2,1,0:T(8,128)(2,1)} %add_convert_fusion.4), channel_id=1, source_target_pairs={{0,8},{1,9},{2,10},{3,11},{4,12},{5,13},{6,14},{7,15},{8,0},{9,1},... | collective-permute-start | bytes 1572872 | tf_op jit(solution)/shard_map/ppermute | solution.py:312
  739.8 34.6 %collective-permute-start.50 = (bf16[2,256,512]{2,1,0:T(8,128)(2,1)}, bf16[2,256,512]{2,1,0:T(8,128)(2,1)}, u32[]{:S(2)}, u32[]{:S(2)}) collective-permute-start(bf16[2,256,512]{2,1,0:T(8,128)(2,1)} %add_convert_fusion.1), channel_id=1, source_target_pairs={{0,8},{1,9},{2,10},{3,11},{4,12},{5,13},{6,14},{7,15},{8,0},{9,1},... | collective-permute-start | bytes 1572872 | tf_op jit(solution)/shard_map/ppermute | solution.py:312
  740.8 43.9 %collective-permute-start.48 = (bf16[2,256,512]{2,1,0:T(8,128)(2,1)}, bf16[2,256,512]{2,1,0:T(8,128)(2,1)}, u32[]{:S(2)}, u32[]{:S(2)}) collective-permute-start(bf16[2,256,512]{2,1,0:T(8,128)(2,1)} %add_convert_fusion.2), channel_id=1, source_target_pairs={{0,8},{1,9},{2,10},{3,11},{4,12},{5,13},{6,14},{7,15},{8,0},{9,1},... | collective-permute-start | bytes 1572872 | tf_op jit(solution)/shard_map/ppermute | solution.py:312
  789.6 7.8 collective-permute-start.56
  797.5 36.2 %collective-permute-start.57 = (bf16[2,256,512]{2,1,0:T(8,128)(2,1)S(1)}, bf16[2,256,512]{2,1,0:T(8,128)(2,1)S(1)}, u32[]{:S(2)}, u32[]{:S(2)}) collective-permute-start(bf16[2,256,512]{2,1,0:T(8,128)(2,1)S(1)} %add_convert_fusion), channel_id=1, source_target_pairs={{0,8},{1,9},{2,10},{3,11},{4,12},{5,13},{6,14},{7,15},{8,0},{9,1},... | collective-permute-start | bytes 1572872 | tf_op jit(solution)/shard_map/ppermute | solution.py:312
  799.1 33.0 %collective-permute-start.55 = (bf16[256,512]{1,0:T(8,128)(2,1)S(1)}, bf16[256,512]{1,0:T(8,128)(2,1)S(1)}, u32[]{:S(2)}, u32[]{:S(2)}) collective-permute-start(bf16[256,512]{1,0:T(8,128)(2,1)S(1)} %fusion.10), channel_id=1, source_target_pairs={{1,0},{2,3},{5,4},{6,7},{9,8},{10,11},{13,12},{14,15},{17,16},{18,... | collective-permute-start | bytes 786440 | tf_op jit(solution)/shard_map/ppermute | solution.py:309
  800.4 30.2 %collective-permute-start.54 = (bf16[256,512]{1,0:T(8,128)(2,1)S(1)}, bf16[256,512]{1,0:T(8,128)(2,1)S(1)}, u32[]{:S(2)}, u32[]{:S(2)}) collective-permute-start(bf16[256,512]{1,0:T(8,128)(2,1)S(1)} %fusion.9), channel_id=1, source_target_pairs={{1,0},{2,3},{5,4},{6,7},{9,8},{10,11},{13,12},{14,15},{17,16},{18,... | collective-permute-start | bytes 786440 | tf_op jit(solution)/shard_map/ppermute | solution.py:309
  801.7 27.3 %collective-permute-start.53 = (bf16[256,512]{1,0:T(8,128)(2,1)S(1)}, bf16[256,512]{1,0:T(8,128)(2,1)S(1)}, u32[]{:S(2)}, u32[]{:S(2)}) collective-permute-start(bf16[256,512]{1,0:T(8,128)(2,1)S(1)} %fusion.8), channel_id=1, source_target_pairs={{1,0},{2,3},{5,4},{6,7},{9,8},{10,11},{13,12},{14,15},{17,16},{18,... | collective-permute-start | bytes 786440 | tf_op jit(solution)/shard_map/ppermute | solution.py:309
  803.0 24.4 %collective-permute-start.52 = (bf16[256,512]{1,0:T(8,128)(2,1)S(1)}, bf16[256,512]{1,0:T(8,128)(2,1)S(1)}, u32[]{:S(2)}, u32[]{:S(2)}) collective-permute-start(bf16[256,512]{1,0:T(8,128)(2,1)S(1)} %fusion.7), channel_id=1, source_target_pairs={{1,0},{2,3},{5,4},{6,7},{9,8},{10,11},{13,12},{14,15},{17,16},{18,... | collective-permute-start | bytes 786440 | tf_op jit(solution)/shard_map/ppermute | solution.py:309
  833.8 9.8 %collective-permute-start.58 = (bf16[256,512]{1,0:T(8,128)(2,1)S(1)}, bf16[256,512]{1,0:T(8,128)(2,1)S(1)}, u32[]{:S(2)}, u32[]{:S(2)}) collective-permute-start(bf16[256,512]{1,0:T(8,128)(2,1)S(1)} %fusion.11), channel_id=1, source_target_pairs={{1,0},{2,3},{5,4},{6,7},{9,8},{10,11},{13,12},{14,15},{17,16},{18,... | collective-permute-start | bytes 786440 | tf_op jit(solution)/shard_map/ppermute | solution.py:309
  (78 other events, 580.7 us)
Sparse Core Ops, SparseCore 0:
  99.1 88.6 all-gather.5
  189.4 58.2 all-gather.11
  300.8 60.0 all-gather.9
  362.3 58.2 all-gather.7

commit v2 on v1

--- a/solution.py
+++ b/solution.py
@@ -12,6 +12,7 @@
 rope_base = 1000000.0
 norm_eps = 1e-06
 MASKED = -1e30
+LOG2E = 1.4426950408889634
 NOWHERE = 1 << 20
 LEVEL = ("fsdp", "tp")
 
@@ -87,10 +88,12 @@
         scores = lax.dot_general(
             query.astype(jnp.bfloat16), keys, (((1,), (1,)), ((), ())),
             preferred_element_type=jnp.float32,
-        ) * scale
+        )
         scores = jnp.where(allowed, scores, MASKED)
-        weights = jnp.exp(scores - jnp.max(scores, axis=-1, keepdims=True))
-        probs = (weights / jnp.sum(weights, axis=-1, keepdims=True)).astype(jnp.bfloat16)
+        highest = jnp.max(scores, axis=-1, keepdims=True)
+        weights = jnp.exp2((scores - highest) * (scale * LOG2E))
+        share = 1.0 / jnp.sum(weights, axis=-1, keepdims=True)
+        probs = (weights * share).astype(jnp.bfloat16)
         mixed = jnp.dot(probs, values, preferred_element_type=jnp.float32)
         out_ref[:, span] = mixed.astype(jnp.bfloat16)
 
@@ -210,7 +213,7 @@
         for place, mixed_ref in enumerate((a_ref, b_ref)):
             for half, out_ref in enumerate((given_ref, kept_ref)):
                 def multiply(mixed_ref=mixed_ref, out_ref=out_ref):
-                    out_ref[0] = times_transposed(mixed_ref[...], weight_ref[...])
+                    out_ref[...] = times_transposed(mixed_ref[...], weight_ref[...])
 
                 pl.when(step == 2 * half + place)(multiply)
 
@@ -220,23 +223,22 @@
         grid=(4,),
         in_specs=[rows, rows, pl.BlockSpec((width, depth), lambda m: (0, 0))],
         out_specs=[
-            pl.BlockSpec((1, block, width), lambda m: (jnp.maximum(m - 2, 0), 0, 0)),
-            pl.BlockSpec((1, block, width), lambda m: (jnp.minimum(m, 1), 0, 0)),
+            pl.BlockSpec((block, width), lambda m: (0, jnp.maximum(m - 2, 0))),
+            pl.BlockSpec((block, width), lambda m: (0, jnp.minimum(m, 1))),
         ],
-        out_shape=[jax.ShapeDtypeStruct((2, block, width), jnp.bfloat16)] * 2,
+        out_shape=[jax.ShapeDtypeStruct((block, 2 * width), jnp.bfloat16)] * 2,
         compiler_params=ROOM,
         cost_estimate=LIGHT,
     )(mixed_a, mixed_b, weight)
 
 
-def add_up(result, hidden, terms, other, use_terms, level, n_t, cuts, cut, h, first):
+def add_up(result, hidden, terms, item, other, other_item, use_terms, count, level, n_t, cuts, cut, h, first):
     rows = result.shape[0]
-    count = terms[-1].shape[1] // cut
     wide = lambda term: term.astype(jnp.float32)
     if cut % 128:
-        total = sum(wide(term[:rows]) for term in terms)
+        total = sum(wide(term[item, :rows, :count * cut]) for term in terms)
         if other is not None:
-            total = jnp.where(use_terms, total, wide(other))
+            total = jnp.where(use_terms, total, wide(other[other_item]))
         for i in range(count):
             column = ((first + i) * n_t + level) * cuts * cut + h * cut
             before = wide(lax.dynamic_slice_in_dim(hidden, column, cut, 1))
@@ -252,6 +254,7 @@
 
     place = pl.BlockSpec(
         (rows, cut), lambda i, at_ref: (0, ((first + i) * n_t + at_ref[0]) * cuts + h))
+    one = lambda item: pl.BlockSpec((None, rows, cut), lambda i, at_ref: (item, 0, i))
     extra = [] if other is None else [other]
     return pl.pallas_call(
         kernel,
@@ -259,7 +262,7 @@
             num_scalar_prefetch=1,
             grid=(count,),
             in_specs=[pl.BlockSpec(memory_space=pl.ANY), place]
-            + [pl.BlockSpec((rows, cut), lambda i, at_ref: (0, i))] * (len(terms) + len(extra)),
+            + [one(item)] * len(terms) + [one(other_item)] * len(extra),
             out_specs=place,
         ),
         out_shape=jax.ShapeDtypeStruct(result.shape, result.dtype),
@@ -364,55 +367,56 @@
         return lax.all_gather(payload, "fsdp", axis=0, tiled=True)
 
     def output_rows(gathered, count):
-        blocks = gathered[:, :part].reshape(n_f, -1, count, part)
+        blocks = gathered.reshape(n_f, -1, count, gathered.shape[1])
         column = f * q_cols
         blocks = lax.dynamic_slice(
             blocks, (0, column // part, 0, column % part), (n_f, 1, count, q_cols))
         return blocks.reshape(n_f, count, q_cols)
 
     count = 2 * rows * part // output_weight.shape[1]
-    early = max(width // 2, part)
+    early = max(width * 3 // 8, part)
 
     own = [level_exchange(projection_block(weights, 0), every)]
     head = send(jnp.concatenate([mine[:, :early], digits], axis=1), inward)
-    raw = [send(output_weight[:cut], outward)]
-    own, head, raw, mine, weights, output_weight = tie(
-        (own, head, raw, mine, weights, output_weight))
+    own, head, mine, weights, output_weight = tie((own, head, mine, weights, output_weight))
     their_digits = head[:, early:]
+    raw = []
 
     def source(k):
         runs = cut // count
         run, at = k // runs, (k % runs) * count
-        h, level = run // 2, run % 2
-        if h >= cuts:
+        if run >= 2 * cuts:
             return jnp.zeros((count, output_weight.shape[1]), output_weight.dtype)
-        some = raw[h] if level == 0 else output_weight[h * cut:(h + 1) * cut]
+        some = raw[run - cuts] if run >= cuts else output_weight[run * cut:(run + 1) * cut]
         return some[at:at + count]
 
     across = [send(own[0], shift(1))] if n_pairs > 1 else []
     own += [level_exchange(projection_block(weights, h), every) for h in range(1, cuts)]
     tail = send(mine[:, early:], inward)
-    ahead = max(1, n_t // 2)
-    gathered = [gather(k, head[:, k * part:(k + 1) * part], source(k)) for k in range(ahead)]
-    own, across, tail, mine, output_weight, raw = tie((own, across, tail, mine, output_weight, raw))
+    gathered = [gather(0, head[:, :part], source(0))]
+    own, across, tail, mine, output_weight = tie((own, across, tail, mine, output_weight))
     theirs = jnp.concatenate([head[:, :early], tail], axis=1)
 
     beyond = []
     projected = None
     for h in range(cuts):
+        until = min(n_t, (cuts + h) * (cut // count))
+        gathered += [
+            gather(k, theirs[:, k * part:(k + 1) * part], source(k))
+            for k in range(len(gathered), until)
+        ]
         if n_pairs > 1 and h + 1 < cuts:
             across.append(send(own[h + 1], shift(1)))
         elif n_pairs > 1 and h:
             across.append(send(beyond[0], shift(1)))
         beyond.append(send(own[h], inward))
-        if h + 1 < cuts:
-            raw.append(send(output_weight[(h + 1) * cut:(h + 2) * cut], outward))
+        raw.append(send(output_weight[h * cut:(h + 1) * cut], outward))
         if h == 0:
             projected = project(gathered[0], own)
-        own, beyond, across, raw, output_weight, projected = tie(
-            (own, beyond, across, raw, output_weight, projected))
+        own, beyond, across, raw, output_weight, projected, theirs, mine = tie(
+            (own, beyond, across, raw, output_weight, projected, theirs, mine))
     gathered += [
-        gather(k, theirs[:, k * part:(k + 1) * part], source(k)) for k in range(ahead, n_t)
+        gather(k, theirs[:, k * part:(k + 1) * part], source(k)) for k in range(len(gathered), n_t)
     ]
 
     def outer_run(r):
@@ -475,85 +479,115 @@
     key_value = jnp.concatenate(
         [keys.reshape(n_f, pair_rows, HEAD), values.reshape(n_f, pair_rows, HEAD)], axis=-1
     )
-    seen, columns = [key_value], [pair_ids]
-    for s in range(1, min(n_pairs - 1, -(-(LONGEST - 1) // pair_rows)) + 1):
+    seen = [key_value]
+    reach = min(n_t - 1, -(-(LONGEST - 1) // rows))
+    for s in range(1, min(n_pairs - 1, (reach + 1) // 2) + 1):
         seen.append(send(key_value, [(inner[j - s], inner[j]) for j in range(s, n_pairs)]))
-        p = pair - s
-        ids = jnp.concatenate([
-            (2 * p + 1 - p % 2) * rows + level_ids, (2 * p + p % 2) * rows + level_ids
-        ])
-        columns.append(jnp.where(p >= 0, ids, NOWHERE))
-    attend = functools.partial(
-        attention, rows=rows, groups=n_f, width=q_cols, f=f, projected=projected,
-        bias=lax.dynamic_slice_in_dim(query_bias, f * q_cols, q_cols)[None],
-        cosine=cosine, sine=sine, starts=starts[:, None], row_ids=row_ids[:, None],
-        columns=jnp.concatenate(columns)[None], key_value=jnp.concatenate(seen, axis=1),
-    )
-    def between_chips(kept, given):
+
+    def attend(outer_rows):
+        blocks, columns = [], []
+        for d in range(reach + 1):
+            found = []
+            for parity in range(2):
+                offset = (1 - parity) ^ outer_rows
+                s = -((offset - d) // 2)
+                place = ((offset - d) % 2) ^ (1 - (parity + s) % 2)
+                block = seen[s] if s < len(seen) else jnp.zeros_like(key_value)
+                found.append(block[:, place * rows:(place + 1) * rows])
+            blocks.append(jnp.where(pair % 2 == 0, found[0], found[1]))
+            level = (my_outer if outer_rows else my_inner) - d
+            columns.append(jnp.where(level >= 0, level * rows + level_ids, NOWHERE))
+        return attention(
+            outer_rows, rows=rows, groups=n_f, width=q_cols, f=f, projected=projected,
+            bias=lax.dynamic_slice_in_dim(query_bias, f * q_cols, q_cols)[None],
+            cosine=cosine, sine=sine, starts=starts[:, None], row_ids=row_ids[:, None],
+            columns=jnp.concatenate(columns)[None], key_value=jnp.concatenate(blocks, axis=1),
+        )
+
+    wide = lambda value: value.astype(jnp.float32)
+
+    def multiply(item):
+        if item[0] == 0:
+            return partials_of_one(mixed, at_inner[item[1]], at_outer[item[1]], is_inner)
+        return partials_of_two(mixed_inner, mixed_outer, arrived[item])
+
+    def between_cores(items, long_ones):
+        kept, given = zip(*[multiply(item) for item in items])
+        given = tie((jnp.stack(given), long_ones))[0]
+        return items, jnp.stack(kept), swap(given, 1, every)
+
+    def between_chips(items, kept, given):
         crossed = []
         for d in range(2, n_f, 2):
             span = slice(d // 2 * rows, (d // 2 + 1) * rows)
-            share = kept[..., span, :].astype(jnp.float32) + given[..., span, :].astype(jnp.float32)
+            share = wide(kept[:, span]) + wide(given[:, span])
             crossed.append(swap(share.astype(jnp.bfloat16), d, every))
-        return crossed
-
-    def own_pair(result, r):
-        kept, given = partials_of_one(mixed, at_inner[r], at_outer[r], is_inner)
-        given = swap(given, 1, every)
-        return [kept, given] + between_chips(kept, given)
-
-    def other_pair(half_run):
-        kept, given = partials_of_two(mixed_inner, mixed_outer, arrived[half_run])
-        given = swap(given, 1, every)
-        crossed = between_chips(kept, given)
-        return [kept[:, :rows], given[:, :rows]] + crossed
-
-    def put_own(result, r, terms):
-        return add_up(result, hidden_in, terms, None, is_inner, order[r % 2], n_t, cuts, cut, r // 2, 0)
-
-    def put_other(result, half_run, terms):
-        s, r, p = half_run
-        sums = sum(term[1].astype(jnp.float32) for term in terms).astype(jnp.bfloat16)
-        return add_up(
-            result, hidden_in, [term[0] for term in terms], send(sums, outward), is_inner,
-            order[2 * s + r % 2], n_t, cuts, cut, r // 2, p * half)
-
-    result = hidden_in
-    key_value, got, at_inner, at_outer = tie((attend.keywords["key_value"], got, at_inner, at_outer))
-    attend.keywords["key_value"] = key_value
+        return items, [kept, given] + crossed
+
+    def between_levels(items, terms):
+        others = [i for i, item in enumerate(items) if item[0]]
+        if not others:
+            return items, terms, None
+        sums = [
+            sum(wide(term[i, :rows, half * cut:]) for term in terms).astype(jnp.bfloat16)
+            for i in others
+        ]
+        return items, terms, send(jnp.stack(sums), outward)
+
+    def put(result, items, terms, other):
+        n_other = 0
+        for i, item in enumerate(items):
+            level, h = 1 - item[1] // cuts, item[1] % cuts
+            if item[0] == 0:
+                result = add_up(
+                    result, hidden_in, terms, i, None, 0, is_inner, n_f, order[level],
+                    n_t, cuts, cut, h, 0)
+            else:
+                result = add_up(
+                    result, hidden_in, terms, i, other, n_other, is_inner, half,
+                    order[2 * item[0] + level], n_t, cuts, cut, h, item[2] * half)
+                n_other += 1
+        return result
+
+    mixed_outer = attend(1)
+    mixed_outer, got, at_inner, at_outer, projected, seen = tie(
+        (mixed_outer, got, at_inner, at_outer, projected, seen))
     if groups:
         arrive(groups[0], got)
-    mixed, waiting = None, list(groups[:1])
-    phase = 1
-    while phase < max(len(groups), 4):
+    runs = [(0, r) for r in range(2 * cuts)]
+    result, phase, from_cores, from_chips, from_levels = hidden_in, 1, None, None, None
+    while phase <= max(len(groups), 3) or from_cores or from_chips or from_levels:
         got = send_group(groups[phase]) if phase < len(groups) else None
         if len(at_inner) < 2 * cuts:
             at_outer.append(outer_run(len(at_inner)))
             at_inner.append(send(at_outer[-1], inward))
+        received = from_levels
+        from_levels = between_levels(*from_chips) if from_chips else None
+        from_chips = between_chips(*from_cores) if from_cores else None
         if phase == 1:
-            mixed_outer = attend(1)
+            there = send(mixed_outer, outward)
             mixed_inner = attend(0)
-            mixed_inner, mixed_outer, got, at_inner, at_outer = tie(
-                (mixed_inner, mixed_outer, got, at_inner, at_outer))
-        else:
-            done = {}
-            if phase == 2:
-                mixed = jnp.where(is_inner, mixed_inner, send(mixed_outer, outward))
-            if phase == 3:
-                done = {r: own_pair(result, r) for r in range(2 * cuts)}
-            else:
-                done = {item: other_pair(item) for group in waiting for item in group}
-                waiting = []
-            done, mixed, got, at_inner, at_outer = tie((done, mixed, got, at_inner, at_outer))
-            for item, terms in done.items():
-                result = (put_own if phase == 3 else put_other)(result, item, terms)
+        if phase == 2:
+            mixed = jnp.where(is_inner, mixed_inner, there)
+        items = list(groups[phase - 1]) if phase <= len(groups) else []
+        if phase >= 2:
+            ready = runs[:cuts]
+            items, runs = items + ready, runs[cuts:]
+        long_ones = (got, at_inner[-1:], from_chips and from_chips[1], from_levels and from_levels[2], there)
+        from_cores = between_cores(items, long_ones) if items else None
+        if received:
+            result = put(result, *received)
+        moving = [None if x is None else x[1:] for x in (from_cores, from_chips, from_levels)]
+        if phase == 1:
+            mixed_inner, there = tie((mixed_inner, there))
+        moving, got, at_inner, at_outer, result = tie((moving, got, at_inner, at_outer, result))
+        from_cores, from_chips, from_levels = [
+            None if x is None else (x[0],) + tuple(y)
+            for x, y in zip((from_cores, from_chips, from_levels), moving)
+        ]
         if got is not None:
             arrive(groups[phase], got)
-            waiting.append(groups[phase])
         phase += 1
-    for group in waiting:
-        for item in group:
-            result = put_other(result, item, other_pair(item))
     return result
 
 

time: 864 us -> 750 us (0.87)
  starting transfers between devices: 136 us -> 68 us
  local copies, waits for them, and re-layouts: 107 us -> 73.6 us
    ppermute x29 -> x26, starting transfers between devices: 119 us -> 62.8 us  [send(): return lax.ppermute(value, 'tp', pairs)]
    all_gather x4, waiting for transfers between devices: 46 us -> 0.03 us  [gather(): return lax.all_gather(payload, 'fsdp', axis=0, tiled=True)]
    ppermute x29 -> x26, waiting for transfers between devices: 146 us -> 191 us  [send(): return lax.ppermute(value, 'tp', pairs)]
    slice x17 -> x4, local copies, waits for them, and re-layouts: 23.4 us -> 5.23 us  [the longest x2 4.92 us: per_device(): raw.append(send(output_weight[h * cut:(h + 1) * cut], outward))]
    squeeze x24 -> x0, local copies, waits for them, and re-layouts: 12.6 us -> none  [put_other(): term[0]]
    ppermute x30 -> x16, starting transfers between devices: 17.6 us -> 5.12 us  [swap(): lax.ppermute(value, LEVEL, [(i * n_t + z, (i ^ d) * n_t + z) for i in ran...]
    unnamed x152 -> x94, local copies, waits for them, and re-layouts: 21.1 us -> 26.1 us
    ppermute x30 -> x16, waiting for transfers between devices: 112 us -> 107 us  [swap(): lax.ppermute(value, LEVEL, [(i * n_t + z, (i ^ d) * n_t + z) for i in ran...]
  transfers between devices with their start and end apart: 63 -> 46, of which waited for: 20 -> 19; matrix products, arithmetic and copies ran while one was open for 15% -> 13% of each run, Pallas kernels for 23% -> 28%
where the time goes in v2:
time: 750 us; the launch traced here: 740 us
  waiting for transfers between devices  298 us (40%)
  Pallas kernels  209 us (28%)
  local copies, waits for them, and re-layouts  73.6 us (10%)
  starting transfers between devices  68 us (9%)
  other arithmetic  62.8 us (8%)
  between operations  14.8 us (2%)
  blocking collectives  12.8 us (2%)
    ppermute x26, waiting for transfers between devices, send(): return lax.ppermute(value, 'tp', pairs)  191 us
    ppermute x16, waiting for transfers between devices, swap(): lax.ppermute(value, LEVEL, [(i * n_t + z, (i ^ d) * n_t + z) for i in ran...  107 us
    pallas_call x4, Pallas kernels, project(): pl.pallas_call(kernel, grid=(n_rows // block,), in_specs=[pl.BlockSpec((b...  65.9 us
    ppermute x26, starting transfers between devices, send(): return lax.ppermute(value, 'tp', pairs)  62.8 us
    pallas_call x2, Pallas kernels, attention(): pl.pallas_call(kernel, grid_spec=pltpu.PrefetchScalarGridSpec(num_scalar_...  42.3 us
    pallas_call x8, Pallas kernels, partials_of_two(): pl.pallas_call(kernel, grid=(4,), in_specs=[rows, rows, pl.BlockSpec((wid...  40.8 us
    pallas_call x12, Pallas kernels, add_up(): pl.pallas_call(kernel, grid_spec=pltpu.PrefetchScalarGridSpec(num_scalar_...  35.8 us
    unnamed x94, local copies, waits for them, and re-layouts  26.1 us
  transfers between devices with their start and end apart: 46, of which 19 were waited for; matrix products, arithmetic and copies ran while one was open for 13% of the time, Pallas kernels for 28%

profile of v2, /device:TPU:0, one launch (start us, length us, event | category | flops | bytes accessed | tf_op | source)
XLA Modules:
  0.0 739.9 jit_solution(14346743664577922565)
XLA Ops:
  6.5 12.8 %all-gather = s32[4,1,256]{2,1,0:T(1,128)S(1)} all-gather(s32[1,1,256]{2,1,0:T(1,128)} %bitcast.103), channel_id=1, replica_groups=mesh['groups'=2,'fsdp'=4,'tp'=4] {'tp'}, dimensions={0}, use_global_device_ids=true | all-gather | bytes 5120 | tf_op jit(solution)/shard_map/all_gather | solution.py:348
  28.0 4.6 shard_map.100
  38.5 3.5 collective-permute-done.1
  42.0 9.8 %collective-permute-done = bf16[256,1280]{1,0:T(8,128)(2,1)} collective-permute-done((bf16[256,1280]{1,0:T(8,128)(2,1)}, bf16[256,1280]{1,0:T(8,128)(2,1)}, u32[]{:S(2)}, u32[]{:S(2)}) %collective-permute-start) | collective-permute-done | bytes 655392 | tf_op jit(solution)/shard_map/ppermute | solution.py:315
  55.7 18.5 %collective-permute-done.3 = bf16[256,3200]{1,0:T(8,128)(2,1)S(1)} collective-permute-done((bf16[256,3200]{1,0:T(8,128)(2,1)}, bf16[256,3200]{1,0:T(8,128)(2,1)S(1)}, u32[]{:S(2)}, u32[]{:S(2)}) %collective-permute-start.3) | collective-permute-done | bytes 1638432 | tf_op jit(solution)/shard_map/ppermute | solution.py:312
  80.9 4.6 collective-permute-start.8
  89.1 29.4 %collective-permute-done.5 = bf16[256,1280]{1,0:T(8,128)(2,1)S(1)} collective-permute-done((bf16[256,1280]{1,0:T(8,128)(2,1)S(1)}, bf16[256,1280]{1,0:T(8,128)(2,1)S(1)}, u32[]{:S(2)}, u32[]{:S(2)}) %collective-permute-start.5) | collective-permute-done | bytes 655392 | tf_op jit(solution)/shard_map/ppermute | solution.py:315
  118.5 26.7 %collective-permute-done.4 = bf16[256,1280]{1,0:T(8,128)(2,1)S(1)} collective-permute-done((bf16[256,1280]{1,0:T(8,128)(2,1)S(1)}, bf16[256,1280]{1,0:T(8,128)(2,1)S(1)}, u32[]{:S(2)}, u32[]{:S(2)}) %collective-permute-start.4) | collective-permute-done | bytes 655392 | tf_op jit(solution)/shard_map/ppermute | solution.py:315
  157.5 5.7 collective-permute-start.9
  163.2 3.2 slice.309
  168.2 2.4 pad_maximum_fusion
  172.3 14.7 %shard_map.101.refs_3_ = f32[2048,1280]{1,0:T(8,128)} custom-call(bf16[2048,2176]{1,0:T(8,128)(2,1)} %all-gather.6.cloned.1.call-done.refs_0_, bf16[1024,1280]{1,0:T(8,128)(2,1)S(1)} %copy-done.4, bf16[1024,1280]{1,0:T(8,128)(2,1)S(1)} %copy-done.5), custom_call_target="tpu_custom_call" | custom-call | flops 1 | bytes 1 | tf_op jit(solution)/shard_map/pallas_call | solution.py:153
  187.0 29.4 %collective-permute-done.11 = bf16[256,4096]{1,0:T(8,128)(2,1)} collective-permute-done((bf16[256,4096]{1,0:T(8,128)(2,1)}, bf16[256,4096]{1,0:T(8,128)(2,1)}, u32[]{:S(2)}, u32[]{:S(2)}) %collective-permute-start.11) | collective-permute-done | bytes 2097184 | tf_op jit(solution)/shard_map/ppermute | solution.py:312
  222.9 6.0 collective-permute-start.12
  232.8 47.3 %collective-permute-done.14 = bf16[256,4096]{1,0:T(8,128)(2,1)S(1)} collective-permute-done((bf16[256,4096]{1,0:T(8,128)(2,1)S(1)}, bf16[256,4096]{1,0:T(8,128)(2,1)S(1)}, u32[]{:S(2)}, u32[]{:S(2)}) %collective-permute-start.14) | collective-permute-done | bytes 2097184 | tf_op jit(solution)/shard_map/ppermute | solution.py:312
  280.0 3.4 collective-permute-done.12.refs_2_
  292.2 7.1 collective-permute-start.16
  303.9 5.7 fusion.7
  309.6 3.1 constant_dynamic-slice_fusion.2
  312.7 3.0 collective-permute-start.19
  315.7 17.6 %shard_map.102.refs_3_ = f32[2048,1280]{1,0:T(8,128)} custom-call(bf16[2048,2048]{1,0:T(8,128)(2,1)} %all-gather.12.cloned.1.call-done.refs_0_, bf16[1024,1280]{1,0:T(8,128)(2,1)} %collective-permute-done.9.refs_1_, bf16[1024,1280]{1,0:T(8,128)(2,1)} %collective-permute-done.12.refs_2_, f32[2048,1280]{1,0:T(8,128)} %shard_map.101.refs_3_), custom_call_target="tpu_custom_call", output_to_operand_aliasing={{}: (3, {})} | custom-call | flops 1 | bytes 1 | tf_op jit(solution)/shard_map/pallas_call | solution.py:153
  335.0 16.9 %shard_map.103.refs_3_ = f32[2048,1280]{1,0:T(8,128)} custom-call(bf16[2048,2048]{1,0:T(8,128)(2,1)} %all-gather.10.cloned.1.call-done.refs_0_, bf16[1024,1280]{1,0:T(8,128)(2,1)S(1)} %copy-done.11, bf16[1024,1280]{1,0:T(8,128)(2,1)} %collective-permute-done.10.refs_2_, f32[2048,1280]{1,0:T(8,128)} %shard_map.102.refs_3_), custom_call_target="tpu_custom_call", output_to_operand_aliasing={{}: (3, {})} | custom-call | flops 1 | bytes 1 | tf_op jit(solution)/shard_map/pallas_call | solution.py:153
  353.6 16.8 %shard_map.104.refs_0_ = f32[2048,1280]{1,0:T(8,128)} custom-call(bf16[2048,2048]{1,0:T(8,128)(2,1)} %all-gather.8.cloned.1.call-done.refs_0_, bf16[1024,1280]{1,0:T(8,128)(2,1)S(1)} %copy-done.13, bf16[1024,1280]{1,0:T(8,128)(2,1)} %collective-permute-done.15.refs_2_, f32[2048,1280]{1,0:T(8,128)} %shard_map.103.refs_3_), custom_call_target="tpu_custom_call", output_to_operand_aliasing={{}: (3, {})} | custom-call | flops 1 | bytes 1 | tf_op jit(solution)/shard_map/pallas_call | solution.py:153
  383.4 3.1 constant_dynamic-slice_fusion.1
  386.5 5.1 collective-permute-start.22
  393.2 21.1 %shard_map.105.b_ref = bf16[1024,1024]{1,0:T(8,128)(2,1)} custom-call(s32[1]{0:T(128)} %bitcast.2.f_ref, f32[2048,1280]{1,0:T(8,128)} %shard_map.104.refs_0_, f32[1,1024]{1,0:T(1,128)S(1)} %bitcast.86, f32[2048,128]{1,0:T(8,128)S(1)} %get-tuple-element.353.refs_2_, f32[2048,128]{1,0:T(8,128)S(1)} %get-tuple-element.306.refs_3_, s32[2048,1]{1,0:T(8,128)S(1)} %copy-done.6, ...), custom_call_target="tpu_custom_call" | custom-call | flops 1 | bytes 1 | tf_op jit(solution)/shard_map/pallas_call | solution.py:113
  423.6 21.2 %shard_map.106.a_ref = bf16[1024,1024]{1,0:T(8,128)(2,1)} custom-call(s32[1]{0:T(128)} %bitcast.2.f_ref, f32[2048,1280]{1,0:T(8,128)} %shard_map.104.refs_0_, f32[1,1024]{1,0:T(1,128)S(1)} %bitcast.87, f32[2048,128]{1,0:T(8,128)S(1)} %get-tuple-element.353.refs_2_, f32[2048,128]{1,0:T(8,128)S(1)} %get-tuple-element.306.refs_3_, s32[2048,1]{1,0:T(8,128)S(1)} %copy-done.7, ...), custom_call_target="tpu_custom_call" | custom-call | flops 1 | bytes 1 | tf_op jit(solution)/shard_map/pallas_call | solution.py:113
  446.4 5.3 shard_map.107
  451.7 28.1 %collective-permute-done.20 = bf16[1024,1024]{1,0:T(8,128)(2,1)} collective-permute-done((bf16[1024,1024]{1,0:T(8,128)(2,1)}, bf16[1024,1024]{1,0:T(8,128)(2,1)}, u32[]{:S(2)}, u32[]{:S(2)}) %collective-permute-start.20) | collective-permute-done | bytes 2097184 | tf_op jit(solution)/shard_map/ppermute | solution.py:312
  479.9 3.1 constant_dynamic-slice_fusion
  483.0 2.8 collective-permute-start.25
  497.2 5.0 shard_map.108
  502.3 5.0 shard_map.109
  507.3 4.9 shard_map.111
  512.2 5.3 shard_map.110
  518.0 12.4 %collective-permute-done.25.first_ref = bf16[1024,1024]{1,0:T(8,128)(2,1)} collective-permute-done((bf16[1024,1024]{1,0:T(8,128)(2,1)}, bf16[1024,1024]{1,0:T(8,128)(2,1)}, u32[]{:S(2)}, u32[]{:S(2)}) %collective-permute-start.25) | collective-permute-done | bytes 2097184 | tf_op jit(solution)/shard_map/ppermute | solution.py:312
  531.0 6.6 collective-permute-done.27.refs_1_
  537.6 2.7 add_convert_fusion.1
  550.3 5.2 shard_map.112
  556.5 5.0 shard_map.113
  562.6 4.8 shard_map.114
  568.4 5.2 shard_map.115
  575.4 12.7 %collective-permute-done.29.refs_2_ = bf16[4,256,1024]{2,1,0:T(8,128)(2,1)S(1)} collective-permute-done((bf16[4,256,1024]{2,1,0:T(8,128)(2,1)}, bf16[4,256,1024]{2,1,0:T(8,128)(2,1)S(1)}, u32[]{:S(2)}, u32[]{:S(2)}) %collective-permute-start.29) | collective-permute-done | bytes 2097184 | tf_op jit(solution)/shard_map/ppermute | solution.py:315
  588.7 6.6 collective-permute-done.31.refs_1_
  595.3 2.7 add_convert_fusion
  604.9 5.3 shard_map.116
  611.2 5.0 shard_map.117
  617.8 15.1 %collective-permute-done.34.refs_3_ = bf16[2,256,512]{2,1,0:T(8,128)(2,1)S(1)} collective-permute-done((bf16[2,256,512]{2,1,0:T(8,128)(2,1)S(1)}, bf16[2,256,512]{2,1,0:T(8,128)(2,1)S(1)}, u32[]{:S(2)}, u32[]{:S(2)}) %collective-permute-start.34) | collective-permute-done | bytes 524320 | tf_op jit(solution)/shard_map/ppermute | solution.py:312
  633.9 12.0 %collective-permute-done.33.refs_2_ = bf16[4,256,1024]{2,1,0:T(8,128)(2,1)S(1)} collective-permute-done((bf16[4,256,1024]{2,1,0:T(8,128)(2,1)}, bf16[4,256,1024]{2,1,0:T(8,128)(2,1)S(1)}, u32[]{:S(2)}, u32[]{:S(2)}) %collective-permute-start.33) | collective-permute-done | bytes 2097184 | tf_op jit(solution)/shard_map/ppermute | solution.py:315
  655.0 5.0 shard_map.119
  661.1 22.0 %collective-permute-done.37.refs_3_ = bf16[2,256,512]{2,1,0:T(8,128)(2,1)S(1)} collective-permute-done((bf16[2,256,512]{2,1,0:T(8,128)(2,1)S(1)}, bf16[2,256,512]{2,1,0:T(8,128)(2,1)S(1)}, u32[]{:S(2)}, u32[]{:S(2)}) %collective-permute-start.37) | collective-permute-done | bytes 524320 | tf_op jit(solution)/shard_map/ppermute | solution.py:312
  683.1 2.5 shard_map.120.result_ref
  685.7 2.5 shard_map.121.result_ref
  688.3 4.1 shard_map.122.result_ref
  692.4 4.1 shard_map.123.result_ref
  698.8 2.5 shard_map.124.result_ref
  701.3 2.5 shard_map.125.result_ref
  703.8 4.1 shard_map.126.result_ref
  707.9 4.1 shard_map.127.result_ref
  712.0 7.7 %collective-permute-done.40.refs_3_ = bf16[2,256,512]{2,1,0:T(8,128)(2,1)S(1)} collective-permute-done((bf16[2,256,512]{2,1,0:T(8,128)(2,1)S(1)}, bf16[2,256,512]{2,1,0:T(8,128)(2,1)S(1)}, u32[]{:S(2)}, u32[]{:S(2)}) %collective-permute-start.40) | collective-permute-done | bytes 524320 | tf_op jit(solution)/shard_map/ppermute | solution.py:312
  721.1 2.3 shard_map.128.result_ref
  723.4 2.3 shard_map.129.result_ref
  725.8 4.8 collective-permute-done.41.refs_3_
  730.6 2.3 shard_map.130
  (288 shorter events, 148.7 us)
Async XLA Ops:
  6.5 164.0 %all-gather.6.cloned.1.call-start = ((), (), s32[]{:S(2)}) async-start(), calls=%async_computation | async-start | bytes 11141120 | tf_op jit(solution)/shard_map/all_gather | solution.py:367
  24.0 18.0 %collective-permute-start.1 = (bf16[256,1280]{1,0:T(8,128)(2,1)}, bf16[256,1280]{1,0:T(8,128)(2,1)}, u32[]{:S(2)}, u32[]{:S(2)}) collective-permute-start(bf16[256,1280]{1,0:T(8,128)(2,1)} %pad_maximum_fusion.19), channel_id=1, source_target_pairs={{0,8},{1,9},{2,10},{3,11},{4,12},{5,13},{6,14},{7,15},{8,0},{9,1},... | collective-permute-start | bytes 1966088 | tf_op jit(solution)/shard_map/ppermute | solution.py:315
  26.4 15.6 %collective-permute-start.2 = (bf16[256,1280]{1,0:T(8,128)(2,1)}, bf16[256,1280]{1,0:T(8,128)(2,1)}, u32[]{:S(2)}, u32[]{:S(2)}) collective-permute-start(bf16[256,1280]{1,0:T(8,128)(2,1)} %pad_maximum_fusion.20), channel_id=1, source_target_pairs={{0,4},{1,5},{2,6},{3,7},{4,0},{5,1},{6,2},{7,3},{8,12},{9,13},{10,... | collective-permute-start | bytes 1966088 | tf_op jit(solution)/shard_map/ppermute | solution.py:315
  27.3 24.5 %collective-permute-start = (bf16[256,1280]{1,0:T(8,128)(2,1)}, bf16[256,1280]{1,0:T(8,128)(2,1)}, u32[]{:S(2)}, u32[]{:S(2)}) collective-permute-start(bf16[256,1280]{1,0:T(8,128)(2,1)} %pad_maximum_fusion.18), channel_id=1, source_target_pairs={{0,12},{1,13},{2,14},{3,15},{4,8},{5,9},{6,10},{7,11},{8,4},{9,5},... | collective-permute-start | bytes 1966088 | tf_op jit(solution)/shard_map/ppermute | solution.py:315
  37.1 37.1 %collective-permute-start.3 = (bf16[256,3200]{1,0:T(8,128)(2,1)}, bf16[256,3200]{1,0:T(8,128)(2,1)S(1)}, u32[]{:S(2)}, u32[]{:S(2)}) collective-permute-start(bf16[256,3200]{1,0:T(8,128)(2,1)} %pad_maximum_fusion.12), channel_id=1, source_target_pairs={{0,1},{3,2},{4,5},{7,6},{8,9},{11,10},{12,13},{15,14},{16,17},{19,... | collective-permute-start | bytes 4915208 | tf_op jit(solution)/shard_map/ppermute | solution.py:312
  54.0 20.3 %copy-start.29 = (bf16[512,4096]{1,0:T(8,128)(2,1)S(1)}, bf16[512,4096]{1,0:T(8,128)(2,1)}, u32[]{:S(2)}) copy-start(bf16[512,4096]{1,0:T(8,128)(2,1)} %param.16) | copy-start | bytes 12582916
  78.7 6.8 copy-start.3
  78.7 7.6 %slice-start.9 = ((bf16[512,512]{1,0:T(8,128)(2,1)}), bf16[256,512]{1,0:T(8,128)(2,1)S(1)}, s32[]{:S(2)}) async-start(bf16[512,512]{1,0:T(8,128)(2,1)} %param.14), calls=%async_computation.13 | async-start | bytes 524288 | tf_op jit(solution)/shard_map/slice | solution.py:343
  78.7 7.6 %slice-start.10 = ((bf16[512,512]{1,0:T(8,128)(2,1)}), bf16[256,512]{1,0:T(8,128)(2,1)S(1)}, s32[]{:S(2)}) async-start(bf16[512,512]{1,0:T(8,128)(2,1)} %param.15), calls=%async_computation.14 | async-start | bytes 524288 | tf_op jit(solution)/shard_map/slice | solution.py:344
  78.7 230.9 %all-gather.12.cloned.1.call-start = ((), (), s32[]{:S(2)}) async-start(), calls=%async_computation.3 | async-start | bytes 10485760 | tf_op jit(solution)/shard_map/all_gather | solution.py:367
  80.9 5.6 slice-start.7
  80.9 66.7 %collective-permute-start.8 = (bf16[256,5120]{1,0:T(8,128)(2,1)S(1)}, bf16[256,5120]{1,0:T(8,128)(2,1)S(1)}, u32[]{:S(2)}, u32[]{:S(2)}) collective-permute-start(bf16[256,5120]{1,0:T(8,128)(2,1)S(1)} %slice.308), channel_id=1, source_target_pairs={{0,1},{3,2},{4,5},{7,6},{8,9},{11,10},{12,13},{15,14},{16,17},{19,... | collective-permute-start | bytes 7864328 | tf_op jit(solution)/shard_map/ppermute | solution.py:312
  85.5 62.1 %collective-permute-start.7 = (bf16[1024,1280]{1,0:T(8,128)(2,1)S(1)}, bf16[1024,1280]{1,0:T(8,128)(2,1)S(1)}, u32[]{:S(2)}, u32[]{:S(2)}) collective-permute-start(bf16[1024,1280]{1,0:T(8,128)(2,1)S(1)} %copy-done.3), channel_id=1, source_target_pairs={{2,1},{1,2},{6,5},{5,6},{10,9},{9,10},{14,13},{13,14},{18,17},{17,... | collective-permute-start | bytes 7864328 | tf_op jit(solution)/shard_map/ppermute | solution.py:312
  86.8 2.4 collective-permute-start.6
  86.9 31.6 %collective-permute-start.5 = (bf16[256,1280]{1,0:T(8,128)(2,1)S(1)}, bf16[256,1280]{1,0:T(8,128)(2,1)S(1)}, u32[]{:S(2)}, u32[]{:S(2)}) collective-permute-start(bf16[256,1280]{1,0:T(8,128)(2,1)S(1)} %pad_maximum_fusion.23), channel_id=1, source_target_pairs={{0,8},{1,9},{2,10},{3,11},{4,12},{5,13},{6,14},{7,15},{8,0},{9,1},... | collective-permute-start | bytes 1966088 | tf_op jit(solution)/shard_map/ppermute | solution.py:315
  88.5 56.7 %collective-permute-start.4 = (bf16[256,1280]{1,0:T(8,128)(2,1)S(1)}, bf16[256,1280]{1,0:T(8,128)(2,1)S(1)}, u32[]{:S(2)}, u32[]{:S(2)}) collective-permute-start(bf16[256,1280]{1,0:T(8,128)(2,1)S(1)} %pad_maximum_fusion.22), channel_id=1, source_target_pairs={{0,12},{1,13},{2,14},{3,15},{4,8},{5,9},{6,10},{7,11},{8,4},{9,5},... | collective-permute-start | bytes 1966088 | tf_op jit(solution)/shard_map/ppermute | solution.py:315
  89.1 58.4 %copy-start.31 = (bf16[256,3072]{1,0:T(8,128)(2,1)}, bf16[256,3072]{1,0:T(8,128)(2,1)S(1)}, u32[]{:S(2)}) copy-start(bf16[256,3072]{1,0:T(8,128)(2,1)S(1)} %slice.315) | copy-start | bytes 4718596
  155.1 178.1 %all-gather.10.cloned.1.call-start = ((), (), s32[]{:S(2)}) async-start(), calls=%async_computation.2 | async-start | bytes 10485760 | tf_op jit(solution)/shard_map/all_gather | solution.py:367
  155.2 13.0 %copy-start.32 = (bf16[256,3072]{1,0:T(8,128)(2,1)S(1)}, bf16[256,3072]{1,0:T(8,128)(2,1)}, u32[]{:S(2)}) copy-start(bf16[256,3072]{1,0:T(8,128)(2,1)} %copy-done.31) | copy-start | bytes 4718596
  155.2 13.0 %copy-start.34 = (bf16[256,5120]{1,0:T(8,128)(2,1)S(1)}, bf16[256,5120]{1,0:T(8,128)(2,1)}, u32[]{:S(2)}) copy-start(bf16[256,5120]{1,0:T(8,128)(2,1)} %copy-done.33) | copy-start | bytes 7864324
  155.2 61.2 %collective-permute-start.10 = (bf16[1024,1280]{1,0:T(8,128)(2,1)}, bf16[1024,1280]{1,0:T(8,128)(2,1)}, u32[]{:S(2)}, u32[]{:S(2)}) collective-permute-start(bf16[1024,1280]{1,0:T(8,128)(2,1)} %pad_maximum_fusion.6.refs_2_), channel_id=1, source_target_pairs={{2,1},{1,2},{6,5},{5,6},{10,9},{9,10},{14,13},{13,14},{18,17},{17,... | collective-permute-start | bytes 7864328 | tf_op jit(solution)/shard_map/ppermute | solution.py:312
  157.5 61.0 %collective-permute-start.9 = (bf16[1024,1280]{1,0:T(8,128)(2,1)}, bf16[1024,1280]{1,0:T(8,128)(2,1)}, u32[]{:S(2)}, u32[]{:S(2)}) collective-permute-start(bf16[1024,1280]{1,0:T(8,128)(2,1)} %pad_maximum_fusion.5.refs_1_), channel_id=1, source_target_pairs={{0,1},{3,2},{4,5},{7,6},{8,9},{11,10},{12,13},{15,14},{16,17},{19,... | collective-permute-start | bytes 7864328 | tf_op jit(solution)/shard_map/ppermute | solution.py:312
  166.4 50.0 %collective-permute-start.11 = (bf16[256,4096]{1,0:T(8,128)(2,1)}, bf16[256,4096]{1,0:T(8,128)(2,1)}, u32[]{:S(2)}, u32[]{:S(2)}) collective-permute-start(bf16[256,4096]{1,0:T(8,128)(2,1)} %slice.309), channel_id=1, source_target_pairs={{1,0},{2,3},{5,4},{6,7},{9,8},{10,11},{13,12},{14,15},{17,16},{18,... | collective-permute-start | bytes 6291464 | tf_op jit(solution)/shard_map/ppermute | solution.py:312
  222.9 129.0 %all-gather.8.cloned.1.call-start = ((), (), s32[]{:S(2)}) async-start(), calls=%async_computation.1 | async-start | bytes 10485760 | tf_op jit(solution)/shard_map/all_gather | solution.py:367
  222.9 60.5 %collective-permute-start.12 = (bf16[1024,1280]{1,0:T(8,128)(2,1)}, bf16[1024,1280]{1,0:T(8,128)(2,1)}, u32[]{:S(2)}, u32[]{:S(2)}) collective-permute-start(bf16[1024,1280]{1,0:T(8,128)(2,1)} %pad_maximum_fusion.6.refs_2_), channel_id=1, source_target_pairs={{0,1},{3,2},{4,5},{7,6},{8,9},{11,10},{12,13},{15,14},{16,17},{19,... | collective-permute-start | bytes 7864328 | tf_op jit(solution)/shard_map/ppermute | solution.py:312
  228.9 54.5 %collective-permute-start.13 = (bf16[1024,1280]{1,0:T(8,128)(2,1)}, bf16[1024,1280]{1,0:T(8,128)(2,1)S(1)}, u32[]{:S(2)}, u32[]{:S(2)}) collective-permute-start(bf16[1024,1280]{1,0:T(8,128)(2,1)} %collective-permute-done.9.refs_1_), channel_id=1, source_target_pairs={{2,1},{1,2},{6,5},{5,6},{10,9},{9,10},{14,13},{13,14},{18,17},{17,... | collective-permute-start | bytes 7864328 | tf_op jit(solution)/shard_map/ppermute | solution.py:312
  231.5 48.6 %collective-permute-start.14 = (bf16[256,4096]{1,0:T(8,128)(2,1)S(1)}, bf16[256,4096]{1,0:T(8,128)(2,1)S(1)}, u32[]{:S(2)}, u32[]{:S(2)}) collective-permute-start(bf16[256,4096]{1,0:T(8,128)(2,1)S(1)} %slice.316), channel_id=1, source_target_pairs={{1,0},{2,3},{5,4},{6,7},{9,8},{10,11},{13,12},{14,15},{17,16},{18,... | collective-permute-start | bytes 6291464 | tf_op jit(solution)/shard_map/ppermute | solution.py:312
  288.2 63.6 %collective-permute-start.15 = (bf16[1024,1280]{1,0:T(8,128)(2,1)}, bf16[1024,1280]{1,0:T(8,128)(2,1)}, u32[]{:S(2)}, u32[]{:S(2)}) collective-permute-start(bf16[1024,1280]{1,0:T(8,128)(2,1)} %collective-permute-done.12.refs_2_), channel_id=1, source_target_pairs={{2,1},{1,2},{6,5},{5,6},{10,9},{9,10},{14,13},{13,14},{18,17},{17,... | collective-permute-start | bytes 7864328 | tf_op jit(solution)/shard_map/ppermute | solution.py:312
  292.2 11.8 %copy-start.35 = (bf16[4,1,256,1024]{3,2,1,0:T(8,128)(2,1)}, bf16[4,1,256,1024]{3,2,1,0:T(8,128)(2,1)S(1)}, u32[]{:S(2)}) copy-start(bf16[4,1,256,1024]{3,2,1,0:T(8,128)(2,1)S(1)} %constant_dynamic-slice_fusion.3) | copy-start | bytes 6291460
  292.2 59.7 %collective-permute-start.16 = (bf16[1024,1024]{1,0:T(8,128)(2,1)S(1)}, bf16[1024,1024]{1,0:T(8,128)(2,1)}, u32[]{:S(2)}, u32[]{:S(2)}) collective-permute-start(bf16[1024,1024]{1,0:T(8,128)(2,1)S(1)} %bitcast.95), channel_id=1, source_target_pairs={{0,1},{3,2},{4,5},{7,6},{8,9},{11,10},{12,13},{15,14},{16,17},{19,... | collective-permute-start | bytes 6291464 | tf_op jit(solution)/shard_map/ppermute | solution.py:312
  312.7 101.6 %collective-permute-start.19 = (bf16[1024,1024]{1,0:T(8,128)(2,1)}, bf16[1024,1024]{1,0:T(8,128)(2,1)}, u32[]{:S(2)}, u32[]{:S(2)}) collective-permute-start(bf16[1024,1024]{1,0:T(8,128)(2,1)} %bitcast.15.second_ref), channel_id=1, source_target_pairs={{0,1},{3,2},{4,5},{7,6},{8,9},{11,10},{12,13},{15,14},{16,17},{19,... | collective-permute-start | bytes 6291464 | tf_op jit(solution)/shard_map/ppermute | solution.py:312
  377.0 14.6 %collective-permute-start.17 = (bf16[4,512,256]{2,1,0:T(8,128)(2,1)}, bf16[4,512,256]{2,1,0:T(8,128)(2,1)}, u32[]{:S(2)}, u32[]{:S(2)}) collective-permute-start(bf16[4,512,256]{2,1,0:T(8,128)(2,1)} %pad_maximum_fusion.15), channel_id=1, source_target_pairs={{1,2},{5,6},{9,10},{13,14},{17,18},{21,22},{25,26},{29,30}} | collective-permute-start | bytes 3145736 | tf_op jit(solution)/shard_map/ppermute | solution.py:312
  380.9 33.4 %collective-permute-start.18 = (bf16[512,1024]{1,0:T(8,128)(2,1)}, bf16[512,1024]{1,0:T(8,128)(2,1)}, u32[]{:S(2)}, u32[]{:S(2)}) collective-permute-start(bf16[512,1024]{1,0:T(8,128)(2,1)} %slice.340), channel_id=1, source_target_pairs={{2,1},{1,2},{6,5},{5,6},{10,9},{9,10},{14,13},{13,14},{18,17},{17,... | collective-permute-start | bytes 3145736 | tf_op jit(solution)/shard_map/ppermute | solution.py:312
  382.6 9.0 %copy-start.37 = (bf16[2048,128]{1,0:T(8,128)(2,1)S(1)}, bf16[2048,128]{1,0:T(8,128)(2,1)}, u32[]{:S(2)}) copy-start(bf16[2048,128]{1,0:T(8,128)(2,1)} %copy-done.36) | copy-start | bytes 1572868
  382.6 9.1 %copy-start.39 = (bf16[2048,128]{1,0:T(8,128)(2,1)S(1)}, bf16[2048,128]{1,0:T(8,128)(2,1)}, u32[]{:S(2)}) copy-start(bf16[2048,128]{1,0:T(8,128)(2,1)} %copy-done.38) | copy-start | bytes 1572868
  386.5 6.7 copy-start.6
  386.5 65.2 %collective-permute-start.22 = (bf16[1024,1024]{1,0:T(8,128)(2,1)}, bf16[1024,1024]{1,0:T(8,128)(2,1)}, u32[]{:S(2)}, u32[]{:S(2)}) collective-permute-start(bf16[1024,1024]{1,0:T(8,128)(2,1)} %bitcast.19.second_ref), channel_id=1, source_target_pairs={{0,1},{3,2},{4,5},{7,6},{8,9},{11,10},{12,13},{15,14},{16,17},{19,... | collective-permute-start | bytes 6291464 | tf_op jit(solution)/shard_map/ppermute | solution.py:312
  418.5 33.3 %collective-permute-start.21 = (bf16[1024,1024]{1,0:T(8,128)(2,1)}, bf16[1024,1024]{1,0:T(8,128)(2,1)}, u32[]{:S(2)}, u32[]{:S(2)}) collective-permute-start(bf16[1024,1024]{1,0:T(8,128)(2,1)} %pad_maximum_fusion.7), channel_id=1, source_target_pairs={{2,1},{1,2},{6,5},{5,6},{10,9},{9,10},{14,13},{13,14},{18,17},{17,... | collective-permute-start | bytes 6291464 | tf_op jit(solution)/shard_map/ppermute | solution.py:312
  420.4 59.4 %collective-permute-start.20 = (bf16[1024,1024]{1,0:T(8,128)(2,1)}, bf16[1024,1024]{1,0:T(8,128)(2,1)}, u32[]{:S(2)}, u32[]{:S(2)}) collective-permute-start(bf16[1024,1024]{1,0:T(8,128)(2,1)} %shard_map.105.b_ref), channel_id=1, source_target_pairs={{1,0},{2,3},{5,4},{6,7},{9,8},{10,11},{13,12},{14,15},{17,16},{18,... | collective-permute-start | bytes 6291464 | tf_op jit(solution)/shard_map/ppermute | solution.py:312
  479.9 5.9 collective-permute-start.23
  483.0 47.4 %collective-permute-start.25 = (bf16[1024,1024]{1,0:T(8,128)(2,1)}, bf16[1024,1024]{1,0:T(8,128)(2,1)}, u32[]{:S(2)}, u32[]{:S(2)}) collective-permute-start(bf16[1024,1024]{1,0:T(8,128)(2,1)} %bitcast.29.second_ref), channel_id=1, source_target_pairs={{0,1},{3,2},{4,5},{7,6},{8,9},{11,10},{12,13},{15,14},{16,17},{19,... | collective-permute-start | bytes 6291464 | tf_op jit(solution)/shard_map/ppermute | solution.py:312
  490.4 40.0 %collective-permute-start.24 = (bf16[1024,1024]{1,0:T(8,128)(2,1)}, bf16[1024,1024]{1,0:T(8,128)(2,1)}, u32[]{:S(2)}, u32[]{:S(2)}) collective-permute-start(bf16[1024,1024]{1,0:T(8,128)(2,1)} %pad_maximum_fusion.8), channel_id=1, source_target_pairs={{2,1},{1,2},{6,5},{5,6},{10,9},{9,10},{14,13},{13,14},{18,17},{17,... | collective-permute-start | bytes 6291464 | tf_op jit(solution)/shard_map/ppermute | solution.py:312
  495.5 34.9 %collective-permute-start.26 = (bf16[1,256,1024]{2,1,0:T(8,128)(2,1)}, bf16[1,256,1024]{2,1,0:T(8,128)(2,1)S(1)}, u32[]{:S(2)}, u32[]{:S(2)}) collective-permute-start(bf16[1,256,1024]{2,1,0:T(8,128)(2,1)} %add_convert_fusion.4), channel_id=1, source_target_pairs={{0,8},{1,9},{2,10},{3,11},{4,12},{5,13},{6,14},{7,15},{8,0},{9,1},... | collective-permute-start | bytes 1572872 | tf_op jit(solution)/shard_map/ppermute | solution.py:315
  530.4 7.2 collective-permute-start.27
  531.0 9.3 %copy-start.25 = (bf16[4,512,1024]{2,1,0:T(8,128)(2,1)}, bf16[4,512,1024]{2,1,0:T(8,128)(2,1)S(1)}, u32[]{:S(2)}) copy-start(bf16[4,512,1024]{2,1,0:T(8,128)(2,1)S(1)} %pad_maximum_fusion.1.refs_0_) | copy-start | bytes 12582916
  537.6 9.7 %copy-start.27 = (bf16[4,512,1024]{2,1,0:T(8,128)(2,1)}, bf16[4,512,1024]{2,1,0:T(8,128)(2,1)S(1)}, u32[]{:S(2)}) copy-start(bf16[4,512,1024]{2,1,0:T(8,128)(2,1)S(1)} %collective-permute-done.27.refs_1_) | copy-start | bytes 12582916
  540.3 47.9 %collective-permute-start.29 = (bf16[4,256,1024]{2,1,0:T(8,128)(2,1)}, bf16[4,256,1024]{2,1,0:T(8,128)(2,1)S(1)}, u32[]{:S(2)}, u32[]{:S(2)}) collective-permute-start(bf16[4,256,1024]{2,1,0:T(8,128)(2,1)} %add_convert_fusion.1), channel_id=1, source_target_pairs={{0,8},{1,9},{2,10},{3,11},{4,12},{5,13},{6,14},{7,15},{8,0},{9,1},... | collective-permute-start | bytes 6291464 | tf_op jit(solution)/shard_map/ppermute | solution.py:315
  544.4 43.8 %collective-permute-start.28 = (bf16[1024,1024]{1,0:T(8,128)(2,1)}, bf16[1024,1024]{1,0:T(8,128)(2,1)}, u32[]{:S(2)}, u32[]{:S(2)}) collective-permute-start(bf16[1024,1024]{1,0:T(8,128)(2,1)} %pad_maximum_fusion.9), channel_id=1, source_target_pairs={{2,1},{1,2},{6,5},{5,6},{10,9},{9,10},{14,13},{13,14},{18,17},{17,... | collective-permute-start | bytes 6291464 | tf_op jit(solution)/shard_map/ppermute | solution.py:312
  547.3 28.1 %collective-permute-start.30 = (bf16[1,256,512]{2,1,0:T(8,128)(2,1)}, bf16[1,256,512]{2,1,0:T(8,128)(2,1)S(1)}, u32[]{:S(2)}, u32[]{:S(2)}) collective-permute-start(bf16[1,256,512]{2,1,0:T(8,128)(2,1)} %add_convert_fusion.12), channel_id=1, source_target_pairs={{1,0},{2,3},{5,4},{6,7},{9,8},{10,11},{13,12},{14,15},{17,16},{18,... | collective-permute-start | bytes 786440 | tf_op jit(solution)/shard_map/ppermute | solution.py:312
  568.4 5.2 copy-start.19
  588.2 7.2 collective-permute-start.31
  588.7 9.3 %copy-start.26 = (bf16[4,512,1024]{2,1,0:T(8,128)(2,1)}, bf16[4,512,1024]{2,1,0:T(8,128)(2,1)S(1)}, u32[]{:S(2)}) copy-start(bf16[4,512,1024]{2,1,0:T(8,128)(2,1)S(1)} %pad_maximum_fusion.3.refs_0_) | copy-start | bytes 12582916
  595.3 9.5 %copy-start.28 = (bf16[4,512,1024]{2,1,0:T(8,128)(2,1)}, bf16[4,512,1024]{2,1,0:T(8,128)(2,1)S(1)}, u32[]{:S(2)}) copy-start(bf16[4,512,1024]{2,1,0:T(8,128)(2,1)S(1)} %collective-permute-done.31.refs_1_) | copy-start | bytes 12582916
  598.0 47.9 %collective-permute-start.33 = (bf16[4,256,1024]{2,1,0:T(8,128)(2,1)}, bf16[4,256,1024]{2,1,0:T(8,128)(2,1)S(1)}, u32[]{:S(2)}, u32[]{:S(2)}) collective-permute-start(bf16[4,256,1024]{2,1,0:T(8,128)(2,1)} %add_convert_fusion), channel_id=1, source_target_pairs={{0,8},{1,9},{2,10},{3,11},{4,12},{5,13},{6,14},{7,15},{8,0},{9,1},... | collective-permute-start | bytes 6291464 | tf_op jit(solution)/shard_map/ppermute | solution.py:315
  599.6 33.3 %collective-permute-start.32 = (bf16[512,1024]{1,0:T(8,128)(2,1)S(1)}, bf16[512,1024]{1,0:T(8,128)(2,1)S(1)}, u32[]{:S(2)}, u32[]{:S(2)}) collective-permute-start(bf16[512,1024]{1,0:T(8,128)(2,1)S(1)} %slice.364), channel_id=1, source_target_pairs={{2,1},{1,2},{6,5},{5,6},{10,9},{9,10},{14,13},{13,14},{18,17},{17,... | collective-permute-start | bytes 3145736 | tf_op jit(solution)/shard_map/ppermute | solution.py:312
  601.8 31.1 %collective-permute-start.34 = (bf16[2,256,512]{2,1,0:T(8,128)(2,1)S(1)}, bf16[2,256,512]{2,1,0:T(8,128)(2,1)S(1)}, u32[]{:S(2)}, u32[]{:S(2)}) collective-permute-start(bf16[2,256,512]{2,1,0:T(8,128)(2,1)S(1)} %pad_maximum_fusion.26), channel_id=1, source_target_pairs={{1,0},{2,3},{5,4},{6,7},{9,8},{10,11},{13,12},{14,15},{17,16},{18,... | collective-permute-start | bytes 1572872 | tf_op jit(solution)/shard_map/ppermute | solution.py:312
  616.2 29.8 %copy-start.24 = (bf16[256,8192]{1,0:T(8,128)(2,1)S(1)}, bf16[256,8192]{1,0:T(8,128)(2,1)}, u32[]{:S(2)}) copy-start(bf16[256,8192]{1,0:T(8,128)(2,1)} %hidden_ref.24) | copy-start | bytes 12582916
  645.9 4.6 collective-permute-start.35
  652.0 31.1 %collective-permute-start.36 = (bf16[2,256,1024]{2,1,0:T(8,128)(2,1)}, bf16[2,256,1024]{2,1,0:T(8,128)(2,1)S(1)}, u32[]{:S(2)}, u32[]{:S(2)}) collective-permute-start(bf16[2,256,1024]{2,1,0:T(8,128)(2,1)} %add_convert_fusion.2), channel_id=1, source_target_pairs={{0,8},{1,9},{2,10},{3,11},{4,12},{5,13},{6,14},{7,15},{8,0},{9,1},... | collective-permute-start | bytes 3145736 | tf_op jit(solution)/shard_map/ppermute | solution.py:315
  653.7 29.4 %collective-permute-start.37 = (bf16[2,256,512]{2,1,0:T(8,128)(2,1)S(1)}, bf16[2,256,512]{2,1,0:T(8,128)(2,1)S(1)}, u32[]{:S(2)}, u32[]{:S(2)}) collective-permute-start(bf16[2,256,512]{2,1,0:T(8,128)(2,1)S(1)} %pad_maximum_fusion.27), channel_id=1, source_target_pairs={{1,0},{2,3},{5,4},{6,7},{9,8},{10,11},{13,12},{14,15},{17,16},{18,... | collective-permute-start | bytes 1572872 | tf_op jit(solution)/shard_map/ppermute | solution.py:312
  683.1 13.3 %collective-permute-start.38 = (bf16[1,512,1024]{2,1,0:T(8,128)(2,1)}, bf16[1,512,1024]{2,1,0:T(8,128)(2,1)S(1)}, u32[]{:S(2)}, u32[]{:S(2)}) collective-permute-start(bf16[1,512,1024]{2,1,0:T(8,128)(2,1)} %bitcast.89), channel_id=1, source_target_pairs={{0,4},{1,5},{2,6},{3,7},{4,0},{5,1},{6,2},{7,3},{8,12},{9,13},{10,... | collective-permute-start | bytes 3145736 | tf_op jit(solution)/shard_map/ppermute | solution.py:315
  696.8 22.8 %collective-permute-start.40 = (bf16[2,256,512]{2,1,0:T(8,128)(2,1)S(1)}, bf16[2,256,512]{2,1,0:T(8,128)(2,1)S(1)}, u32[]{:S(2)}, u32[]{:S(2)}) collective-permute-start(bf16[2,256,512]{2,1,0:T(8,128)(2,1)S(1)} %pad_maximum_fusion.28), channel_id=1, source_target_pairs={{1,0},{2,3},{5,4},{6,7},{9,8},{10,11},{13,12},{14,15},{17,16},{18,... | collective-permute-start | bytes 1572872 | tf_op jit(solution)/shard_map/ppermute | solution.py:312
  698.3 21.3 %collective-permute-start.39 = (bf16[1,256,1024]{2,1,0:T(8,128)(2,1)S(1)}, bf16[1,256,1024]{2,1,0:T(8,128)(2,1)S(1)}, u32[]{:S(2)}, u32[]{:S(2)}) collective-permute-start(bf16[1,256,1024]{2,1,0:T(8,128)(2,1)S(1)} %add_convert_fusion.3), channel_id=1, source_target_pairs={{0,8},{1,9},{2,10},{3,11},{4,12},{5,13},{6,14},{7,15},{8,0},{9,1},... | collective-permute-start | bytes 1572872 | tf_op jit(solution)/shard_map/ppermute | solution.py:315
  719.8 10.8 %collective-permute-start.41 = (bf16[1,256,512]{2,1,0:T(8,128)(2,1)S(1)}, bf16[1,256,512]{2,1,0:T(8,128)(2,1)S(1)}, u32[]{:S(2)}, u32[]{:S(2)}) collective-permute-start(bf16[1,256,512]{2,1,0:T(8,128)(2,1)S(1)} %add_convert_fusion.5), channel_id=1, source_target_pairs={{1,0},{2,3},{5,4},{6,7},{9,8},{10,11},{13,12},{14,15},{17,16},{18,... | collective-permute-start | bytes 786440 | tf_op jit(solution)/shard_map/ppermute | solution.py:312
  (38 other events, 76.3 us)
Sparse Core Ops, SparseCore 0:
  78.8 88.8 all-gather.5
  169.2 57.6 all-gather.11
  228.5 58.2 all-gather.9
  288.4 60.6 all-gather.7

commit v3 on v2

--- a/solution.py
+++ b/solution.py
@@ -135,9 +135,11 @@
       key_value, key_value)
 
 
-def project(tokens, weights, total=None):
+def project(tokens, weights, total=None, columns=None):
     n_rows, width = tokens.shape[0], weights[0].shape[1]
     block, n_w = min(512, n_rows), len(weights)
+    first, width = (0, width) if columns is None else columns
+    at = first // width
 
     def kernel(*refs):
         part, done = None, 0
@@ -149,16 +151,16 @@
             part, done = more if part is None else part + more, done + depth
         refs[-1][...] = part if total is None else part + refs[1 + n_w][...]
 
-    sums = pl.BlockSpec((block, width), lambda m: (m, 0))
+    sums = pl.BlockSpec((block, width), lambda m: (m, at))
     return pl.pallas_call(
         kernel,
         grid=(n_rows // block,),
         in_specs=[pl.BlockSpec((block, tokens.shape[1]), lambda m: (m, 0))]
-        + [pl.BlockSpec(w.shape, lambda m: (0, 0)) for w in weights]
+        + [pl.BlockSpec((w.shape[0], width), lambda m: (0, at)) for w in weights]
         + ([] if total is None else [sums]),
-        out_specs=sums,
+        out_specs=pl.BlockSpec((block, width), lambda m: (m, 0)),
         out_shape=jax.ShapeDtypeStruct((n_rows, width), jnp.float32),
-        input_output_aliases={} if total is None else {1 + n_w: 0},
+        input_output_aliases={1 + n_w: 0} if total is not None and columns is None else {},
         compiler_params=ROOM,
         cost_estimate=LIGHT,
     )(tokens, *weights, *([] if total is None else [total]))
@@ -374,11 +376,12 @@
         return blocks.reshape(n_f, count, q_cols)
 
     count = 2 * rows * part // output_weight.shape[1]
-    early = max(width * 3 // 8, part)
+    early = part
 
     own = [level_exchange(projection_block(weights, 0), every)]
     head = send(jnp.concatenate([mine[:, :early], digits], axis=1), inward)
-    own, head, mine, weights, output_weight = tie((own, head, mine, weights, output_weight))
+    tail = send(mine[:, early:], inward)
+    own, weights = tie((own, weights))
     their_digits = head[:, early:]
     raw = []
 
@@ -392,8 +395,7 @@
 
     across = [send(own[0], shift(1))] if n_pairs > 1 else []
     own += [level_exchange(projection_block(weights, h), every) for h in range(1, cuts)]
-    tail = send(mine[:, early:], inward)
-    gathered = [gather(0, head[:, :part], source(0))]
+    gathered = [gather(0, tie((head, own[0]))[0][:, :part], source(0))]
     own, across, tail, mine, output_weight = tie((own, across, tail, mine, output_weight))
     theirs = jnp.concatenate([head[:, :early], tail], axis=1)
 
@@ -429,17 +431,18 @@
     at_inner = [send(at_outer[0], inward)]
     if n_pairs > 1:
         across += [send(w, shift(1)) for w in beyond[len(across) - cuts:]]
-    projected = project(gathered[1], beyond, projected)
+    waiting = [(1, beyond)]
     if n_pairs > 1:
+        projected = project(gathered[1], beyond, projected)
         projected = project(gathered[2], across[:cuts], projected)
+        waiting = [(3, across[cuts:])]
     projected, across, at_inner, at_outer = tie((projected, across, at_inner, at_outer))
 
     groups = []
     half = n_f // 2
     for s in range(1, n_pairs):
         halves = [(s, r, p) for r in range(2 * cuts) for p in range(2)]
-        inside = halves[1:-1]
-        groups += [halves[:1]] + [inside[i:i + 2] for i in range(0, len(inside), 2)] + [halves[-1:]]
+        groups += [halves[i:i + 2] for i in range(0, len(halves), 2)]
 
     def send_group(group):
         return send(jnp.concatenate([
@@ -452,15 +455,14 @@
         for place, (s, r, p) in enumerate(group):
             arrived[s, r, p] = got[place * half * cut:(place + 1) * half * cut]
 
-    got = send_group(groups[0]) if groups else None
-    if len(at_inner) < 2 * cuts:
-        at_outer.append(outer_run(1))
-        at_inner.append(send(at_outer[1], inward))
-    for s in range(1, n_pairs):
-        if s > 1:
-            across = [send(w, shift(s)) for w in own + beyond]
-            projected = project(gathered[2 * s], across[:cuts], projected)
-        projected = project(gathered[2 * s + 1], across[cuts:], projected)
+    for s in range(2, n_pairs):
+        across = [send(w, shift(s)) for w in own + beyond]
+        waiting += [(2 * s, across[:cuts]), (2 * s + 1, across[cuts:])]
+    for k, some in waiting[:-1]:
+        projected = project(gathered[k], some, projected)
+    k, some = waiting[-1]
+    projected_pair = project(gathered[k], some, projected, (q_cols, 2 * HEAD))
+    projected_queries = project(gathered[k], some, projected, (0, q_cols))
 
     level_ids = jnp.arange(rows, dtype=jnp.int32)
     pair_ids = jnp.concatenate([my_inner * rows + level_ids, my_outer * rows + level_ids])
@@ -469,11 +471,11 @@
     starts = digits[:, 0] * 256 + digits[:, 1]
     cosine, sine = rotary_tables((row_ids - starts).astype(jnp.float32))
 
-    key_rows = projected[:, q_cols:q_cols + HEAD]
+    key_rows = projected_pair[:, :HEAD]
     key_rows = key_rows + lax.dynamic_slice_in_dim(key_bias, kv_head * HEAD, HEAD)
     turned = jnp.concatenate([key_rows[:, HEAD // 2:], key_rows[:, :HEAD // 2]], axis=-1)
     keys = (key_rows * cosine + turned * sine).astype(jnp.bfloat16)
-    values = projected[:, q_cols + HEAD:] + lax.dynamic_slice_in_dim(value_bias, kv_head * HEAD, HEAD)
+    values = projected_pair[:, HEAD:] + lax.dynamic_slice_in_dim(value_bias, kv_head * HEAD, HEAD)
     values = values.astype(jnp.bfloat16)
     pair_rows = 2 * rows
     key_value = jnp.concatenate(
@@ -483,6 +485,12 @@
     reach = min(n_t - 1, -(-(LONGEST - 1) // rows))
     for s in range(1, min(n_pairs - 1, (reach + 1) // 2) + 1):
         seen.append(send(key_value, [(inner[j - s], inner[j]) for j in range(s, n_pairs)]))
+    if groups:
+        at_inner[0] = tie((at_inner[0], seen[1]))[0]
+    got = send_group(groups[0]) if groups else None
+    if len(at_inner) < 2 * cuts:
+        at_outer.append(outer_run(1))
+        at_inner.append(send(at_outer[1], inward))
 
     def attend(outer_rows):
         blocks, columns = [], []
@@ -498,7 +506,7 @@
             level = (my_outer if outer_rows else my_inner) - d
             columns.append(jnp.where(level >= 0, level * rows + level_ids, NOWHERE))
         return attention(
-            outer_rows, rows=rows, groups=n_f, width=q_cols, f=f, projected=projected,
+            outer_rows, rows=rows, groups=n_f, width=q_cols, f=f, projected=projected_queries,
             bias=lax.dynamic_slice_in_dim(query_bias, f * q_cols, q_cols)[None],
             cosine=cosine, sine=sine, starts=starts[:, None], row_ids=row_ids[:, None],
             columns=jnp.concatenate(columns)[None], key_value=jnp.concatenate(blocks, axis=1),
@@ -512,7 +520,12 @@
         return partials_of_two(mixed_inner, mixed_outer, arrived[item])
 
     def between_cores(items, long_ones):
-        kept, given = zip(*[multiply(item) for item in items])
+        kept, given = [], []
+        for item in items:
+            if item == (0, 2 * cuts - 1) and kept:
+                at_inner[-1], kept[-1] = tie((at_inner[-1], kept[-1]))
+            a, b = multiply(item)
+            kept, given = kept + [a], given + [b]
         given = tie((jnp.stack(given), long_ones))[0]
         return items, jnp.stack(kept), swap(given, 1, every)
 
@@ -550,13 +563,13 @@
         return result
 
     mixed_outer = attend(1)
-    mixed_outer, got, at_inner, at_outer, projected, seen = tie(
-        (mixed_outer, got, at_inner, at_outer, projected, seen))
+    mixed_outer, at_inner, at_outer, projected_queries, seen = tie(
+        (mixed_outer, at_inner, at_outer, projected_queries, seen))
     if groups:
         arrive(groups[0], got)
     runs = [(0, r) for r in range(2 * cuts)]
     result, phase, from_cores, from_chips, from_levels = hidden_in, 1, None, None, None
-    while phase <= max(len(groups), 3) or from_cores or from_chips or from_levels:
+    while phase <= len(groups) or runs or from_cores or from_chips or from_levels:
         got = send_group(groups[phase]) if phase < len(groups) else None
         if len(at_inner) < 2 * cuts:
             at_outer.append(outer_run(len(at_inner)))
@@ -567,19 +580,15 @@
         if phase == 1:
             there = send(mixed_outer, outward)
             mixed_inner = attend(0)
-        if phase == 2:
             mixed = jnp.where(is_inner, mixed_inner, there)
         items = list(groups[phase - 1]) if phase <= len(groups) else []
-        if phase >= 2:
-            ready = runs[:cuts]
-            items, runs = items + ready, runs[cuts:]
+        ready = runs[:cuts]
+        items, runs = items + ready, runs[cuts:]
         long_ones = (got, at_inner[-1:], from_chips and from_chips[1], from_levels and from_levels[2], there)
         from_cores = between_cores(items, long_ones) if items else None
         if received:
             result = put(result, *received)
         moving = [None if x is None else x[1:] for x in (from_cores, from_chips, from_levels)]
-        if phase == 1:
-            mixed_inner, there = tie((mixed_inner, there))
         moving, got, at_inner, at_outer, result = tie((moving, got, at_inner, at_outer, result))
         from_cores, from_chips, from_levels = [
             None if x is None else (x[0],) + tuple(y)

time: 750 us -> 699 us (0.932)
  waiting for transfers between devices: 298 us -> 244 us
  starting transfers between devices: 68 us -> 85 us
  other arithmetic: 62.8 us -> 50.3 us
    ppermute x26 -> x24, waiting for transfers between devices: 191 us -> 130 us  [send(): return lax.ppermute(value, 'tp', pairs)]
    ppermute x26 -> x24, starting transfers between devices: 62.8 us -> 79.5 us  [send(): return lax.ppermute(value, 'tp', pairs)]
    slice x10 -> x1, local copies, waits for them, and re-layouts: 12 us -> 1.32 us  [per_device(): gathered = [gather(0, tie((head, own[0]))[0][:, :part], source(0))]]
    ppermute x16 -> x14, waiting for transfers between devices: 107 us -> 114 us  [swap(): lax.ppermute(value, LEVEL, [(i * n_t + z, (i ^ d) * n_t + z) for i in ran...]
    pallas_call x4 -> x5, Pallas kernels: 65.9 us -> 69.8 us  [project(): pl.pallas_call(kernel, grid=(n_rows // block,), in_specs=[pl.BlockSpec((b...]
    unnamed x94 -> x90, local copies, waits for them, and re-layouts: 26.1 us -> 23.5 us
  transfers between devices with their start and end apart: 46 -> 42, of which waited for: 19 -> 21; matrix products, arithmetic and copies ran while one was open for 13% -> 12% of each run, Pallas kernels for 28% -> 30%
where the time goes in v3:
time: 699 us; the launch traced here: 689 us
  waiting for transfers between devices  244 us (35%)
  Pallas kernels  214 us (31%)
  starting transfers between devices  85 us (12%)
  local copies, waits for them, and re-layouts  69.1 us (10%)
  other arithmetic  50.3 us (7%)
  between operations  14.5 us (2%)
  blocking collectives  12.8 us (2%)
    ppermute x24, waiting for transfers between devices, send(): return lax.ppermute(value, 'tp', pairs)  130 us
    ppermute x14, waiting for transfers between devices, swap(): lax.ppermute(value, LEVEL, [(i * n_t + z, (i ^ d) * n_t + z) for i in ran...  114 us
    ppermute x24, starting transfers between devices, send(): return lax.ppermute(value, 'tp', pairs)  79.5 us
    pallas_call x5, Pallas kernels, project(): pl.pallas_call(kernel, grid=(n_rows // block,), in_specs=[pl.BlockSpec((b...  69.8 us
    pallas_call x2, Pallas kernels, attention(): pl.pallas_call(kernel, grid_spec=pltpu.PrefetchScalarGridSpec(num_scalar_...  42.3 us
    pallas_call x8, Pallas kernels, partials_of_two(): pl.pallas_call(kernel, grid=(4,), in_specs=[rows, rows, pl.BlockSpec((wid...  40.8 us
    pallas_call x12, Pallas kernels, add_up(): pl.pallas_call(kernel, grid_spec=pltpu.PrefetchScalarGridSpec(num_scalar_...  36.1 us
    unnamed x90, local copies, waits for them, and re-layouts  23.5 us
  transfers between devices with their start and end apart: 42, of which 21 were waited for; matrix products, arithmetic and copies ran while one was open for 12% of the time, Pallas kernels for 30%

profile of v3, /device:TPU:0, one launch (start us, length us, event | category | flops | bytes accessed | tf_op | source)
XLA Modules:
  0.0 689.0 jit_solution(3267776494734158339)
XLA Ops:
  6.5 12.8 %all-gather = s32[4,1,256]{2,1,0:T(1,128)S(1)} all-gather(s32[1,1,256]{2,1,0:T(1,128)} %bitcast.99), channel_id=1, replica_groups=mesh['groups'=2,'fsdp'=4,'tp'=4] {'tp'}, dimensions={0}, use_global_device_ids=true | all-gather | bytes 5120 | tf_op jit(solution)/shard_map/all_gather | solution.py:350
  27.9 4.6 shard_map.100
  36.7 2.3 collective-permute-start.11
  39.0 3.1 fusion.10
  42.4 9.8 %collective-permute-done = bf16[256,1280]{1,0:T(8,128)(2,1)} collective-permute-done((bf16[256,1280]{1,0:T(8,128)(2,1)}, bf16[256,1280]{1,0:T(8,128)(2,1)}, u32[]{:S(2)}, u32[]{:S(2)}) %collective-permute-start) | collective-permute-done | bytes 655392 | tf_op jit(solution)/shard_map/ppermute | solution.py:317
  54.7 7.9 %collective-permute-done.11 = bf16[256,2176]{1,0:T(8,128)(2,1)} collective-permute-done((bf16[256,2176]{1,0:T(8,128)(2,1)}, bf16[256,2176]{1,0:T(8,128)(2,1)}, u32[]{:S(2)}, u32[]{:S(2)}) %collective-permute-start.11) | collective-permute-done | bytes 1114144 | tf_op jit(solution)/shard_map/ppermute | solution.py:314
  69.7 4.6 collective-permute-start.7
  79.7 29.6 %collective-permute-done.4 = bf16[256,1280]{1,0:T(8,128)(2,1)S(1)} collective-permute-done((bf16[256,1280]{1,0:T(8,128)(2,1)S(1)}, bf16[256,1280]{1,0:T(8,128)(2,1)S(1)}, u32[]{:S(2)}, u32[]{:S(2)}) %collective-permute-start.4) | collective-permute-done | bytes 655392 | tf_op jit(solution)/shard_map/ppermute | solution.py:317
  109.2 27.3 %collective-permute-done.3 = bf16[256,1280]{1,0:T(8,128)(2,1)S(1)} collective-permute-done((bf16[256,1280]{1,0:T(8,128)(2,1)S(1)}, bf16[256,1280]{1,0:T(8,128)(2,1)S(1)}, u32[]{:S(2)}, u32[]{:S(2)}) %collective-permute-start.3) | collective-permute-done | bytes 655392 | tf_op jit(solution)/shard_map/ppermute | solution.py:317
  145.9 6.2 collective-permute-start.8
  154.2 3.2 slice.294
  165.0 15.0 %shard_map.101.refs_3_ = f32[2048,1280]{1,0:T(8,128)} custom-call(bf16[2048,2176]{1,0:T(8,128)(2,1)} %all-gather.6.cloned.1.call-done.refs_0_, bf16[1024,1280]{1,0:T(8,128)(2,1)S(1)} %copy-done.3, bf16[1024,1280]{1,0:T(8,128)(2,1)S(1)} %copy-done.4), custom_call_target="tpu_custom_call" | custom-call | flops 1 | bytes 1 | tf_op jit(solution)/shard_map/pallas_call | solution.py:155
  180.0 25.4 %collective-permute-done.10 = bf16[256,4096]{1,0:T(8,128)(2,1)} collective-permute-done((bf16[256,4096]{1,0:T(8,128)(2,1)}, bf16[256,4096]{1,0:T(8,128)(2,1)}, u32[]{:S(2)}, u32[]{:S(2)}) %collective-permute-start.10) | collective-permute-done | bytes 2097184 | tf_op jit(solution)/shard_map/ppermute | solution.py:314
  210.3 7.2 %collective-permute-start.12 = (bf16[1024,1280]{1,0:T(8,128)(2,1)}, bf16[1024,1280]{1,0:T(8,128)(2,1)}, u32[]{:S(2)}, u32[]{:S(2)}) collective-permute-start(bf16[1024,1280]{1,0:T(8,128)(2,1)} %pad_maximum_fusion.6.refs_2_), channel_id=1, source_target_pairs={{0,1},{3,2},{4,5},{7,6},{8,9},{11,10},{12,13},{15,14},{16,17},{19,... | collective-permute-start | bytes 7864328 | tf_op jit(solution)/shard_map/ppermute | solution.py:314
  221.3 45.6 %collective-permute-done.14 = bf16[256,4096]{1,0:T(8,128)(2,1)S(1)} collective-permute-done((bf16[256,4096]{1,0:T(8,128)(2,1)S(1)}, bf16[256,4096]{1,0:T(8,128)(2,1)S(1)}, u32[]{:S(2)}, u32[]{:S(2)}) %collective-permute-start.14) | collective-permute-done | bytes 2097184 | tf_op jit(solution)/shard_map/ppermute | solution.py:314
  266.9 3.4 collective-permute-done.12.refs_2_
  279.1 8.1 %collective-permute-start.16 = (bf16[1024,1024]{1,0:T(8,128)(2,1)S(1)}, bf16[1024,1024]{1,0:T(8,128)(2,1)}, u32[]{:S(2)}, u32[]{:S(2)}) collective-permute-start(bf16[1024,1024]{1,0:T(8,128)(2,1)S(1)} %bitcast.91), channel_id=1, source_target_pairs={{0,1},{3,2},{4,5},{7,6},{8,9},{11,10},{12,13},{15,14},{16,17},{19,... | collective-permute-start | bytes 6291464 | tf_op jit(solution)/shard_map/ppermute | solution.py:314
  291.7 5.8 fusion.6
  297.4 3.1 constant_dynamic-slice_fusion.2
  300.5 3.0 collective-permute-start.18
  303.6 17.5 %shard_map.102.refs_3_ = f32[2048,1280]{1,0:T(8,128)} custom-call(bf16[2048,2048]{1,0:T(8,128)(2,1)} %all-gather.12.cloned.1.call-done.refs_0_, bf16[1024,1280]{1,0:T(8,128)(2,1)} %collective-permute-done.8.refs_1_, bf16[1024,1280]{1,0:T(8,128)(2,1)} %collective-permute-done.12.refs_2_, f32[2048,1280]{1,0:T(8,128)} %shard_map.101.refs_3_), custom_call_target="tpu_custom_call", output_to_operand_aliasing={{}: (3, {})} | custom-call | flops 1 | bytes 1 | tf_op jit(solution)/shard_map/pallas_call | solution.py:155
  322.9 16.9 %shard_map.103.refs_3_ = f32[2048,1280]{1,0:T(8,128)} custom-call(bf16[2048,2048]{1,0:T(8,128)(2,1)} %all-gather.10.cloned.1.call-done.refs_0_, bf16[1024,1280]{1,0:T(8,128)(2,1)S(1)} %copy-done.11, bf16[1024,1280]{1,0:T(8,128)(2,1)} %collective-permute-done.9.refs_2_, f32[2048,1280]{1,0:T(8,128)} %shard_map.102.refs_3_), custom_call_target="tpu_custom_call", output_to_operand_aliasing={{}: (3, {})} | custom-call | flops 1 | bytes 1 | tf_op jit(solution)/shard_map/pallas_call | solution.py:155
  341.5 6.0 shard_map.105
  356.6 14.5 %shard_map.104.refs_0_ = f32[2048,1024]{1,0:T(8,128)} custom-call(bf16[2048,2048]{1,0:T(8,128)(2,1)} %all-gather.8.cloned.1.call-done.refs_0_, bf16[1024,1280]{1,0:T(8,128)(2,1)S(1)} %copy-done.7, bf16[1024,1280]{1,0:T(8,128)(2,1)} %collective-permute-done.15.refs_2_, f32[2048,1280]{1,0:T(8,128)} %shard_map.103.refs_3_), custom_call_target="tpu_custom_call" | custom-call | flops 1 | bytes 1 | tf_op jit(solution)/shard_map/pallas_call | solution.py:155
  375.7 21.2 %shard_map.106.b_ref = bf16[1024,1024]{1,0:T(8,128)(2,1)} custom-call(s32[1]{0:T(128)} %bitcast.2.f_ref, f32[2048,1024]{1,0:T(8,128)} %shard_map.104.refs_0_, f32[1,1024]{1,0:T(1,128)S(1)} %bitcast.84, f32[2048,128]{1,0:T(8,128)S(1)} %get-tuple-element.309.refs_2_, f32[2048,128]{1,0:T(8,128)S(1)} %get-tuple-element.258.refs_3_, s32[2048,1]{1,0:T(8,128)S(1)} %copy-done.8, ...), custom_call_target="tpu_custom_call" | custom-call | flops 1 | bytes 1 | tf_op jit(solution)/shard_map/pallas_call | solution.py:113
  398.3 3.1 constant_dynamic-slice_fusion.1
  401.4 13.2 %collective-permute-start.22 = (bf16[1024,1024]{1,0:T(8,128)(2,1)}, bf16[1024,1024]{1,0:T(8,128)(2,1)}, u32[]{:S(2)}, u32[]{:S(2)}) collective-permute-start(bf16[1024,1024]{1,0:T(8,128)(2,1)} %bitcast.25.second_ref), channel_id=1, source_target_pairs={{0,1},{3,2},{4,5},{7,6},{8,9},{11,10},{12,13},{15,14},{16,17},{19,... | collective-permute-start | bytes 6291464 | tf_op jit(solution)/shard_map/ppermute | solution.py:314
  419.5 21.1 %shard_map.107.a_ref = bf16[1024,1024]{1,0:T(8,128)(2,1)} custom-call(s32[1]{0:T(128)} %bitcast.2.f_ref, f32[2048,1024]{1,0:T(8,128)} %shard_map.104.refs_0_, f32[1,1024]{1,0:T(1,128)S(1)} %bitcast.85, f32[2048,128]{1,0:T(8,128)S(1)} %get-tuple-element.309.refs_2_, f32[2048,128]{1,0:T(8,128)S(1)} %get-tuple-element.258.refs_3_, s32[2048,1]{1,0:T(8,128)S(1)} %copy-done.9, ...), custom_call_target="tpu_custom_call" | custom-call | flops 1 | bytes 1 | tf_op jit(solution)/shard_map/pallas_call | solution.py:113
  442.9 5.0 shard_map.108
  447.9 5.0 shard_map.109
  454.7 5.1 shard_map.111
  459.8 4.9 shard_map.110
  465.4 3.2 constant_dynamic-slice_fusion
  468.5 10.0 %collective-permute-start.24 = (bf16[1024,1024]{1,0:T(8,128)(2,1)}, bf16[1024,1024]{1,0:T(8,128)(2,1)}, u32[]{:S(2)}, u32[]{:S(2)}) collective-permute-start(bf16[1024,1024]{1,0:T(8,128)(2,1)} %bitcast.29.second_ref), channel_id=1, source_target_pairs={{0,1},{3,2},{4,5},{7,6},{8,9},{11,10},{12,13},{15,14},{16,17},{19,... | collective-permute-start | bytes 6291464 | tf_op jit(solution)/shard_map/ppermute | solution.py:314
  479.1 2.9 add_convert_fusion.1
  485.8 5.3 shard_map.112
  491.0 5.0 shard_map.113
  496.1 4.9 shard_map.114
  500.9 22.1 %collective-permute-done.24.first_ref = bf16[1024,1024]{1,0:T(8,128)(2,1)} collective-permute-done((bf16[1024,1024]{1,0:T(8,128)(2,1)}, bf16[1024,1024]{1,0:T(8,128)(2,1)}, u32[]{:S(2)}, u32[]{:S(2)}) %collective-permute-start.24) | collective-permute-done | bytes 2097184 | tf_op jit(solution)/shard_map/ppermute | solution.py:314
  523.1 5.3 shard_map.115
  530.6 6.6 collective-permute-done.27.refs_1_
  545.2 5.2 shard_map.116
  550.4 5.0 shard_map.117
  555.6 4.3 collective-permute-done.30.refs_3_
  559.9 26.1 %collective-permute-done.29.refs_2_ = bf16[4,256,1024]{2,1,0:T(8,128)(2,1)S(1)} collective-permute-done((bf16[4,256,1024]{2,1,0:T(8,128)(2,1)S(1)}, bf16[4,256,1024]{2,1,0:T(8,128)(2,1)S(1)}, u32[]{:S(2)}, u32[]{:S(2)}) %collective-permute-start.29) | collective-permute-done | bytes 2097184 | tf_op jit(solution)/shard_map/ppermute | solution.py:317
  586.2 4.0 collective-permute-done.31.refs_1_
  596.3 5.2 shard_map.118
  603.5 5.1 shard_map.119
  612.7 4.3 collective-permute-done.32.refs_2_
  619.2 2.5 shard_map.120.result_ref
  621.7 2.5 shard_map.121.result_ref
  624.2 4.1 shard_map.122.result_ref
  628.3 4.2 shard_map.123.result_ref
  636.1 2.5 shard_map.124.result_ref
  638.7 2.5 shard_map.125.result_ref
  641.3 4.1 shard_map.126.result_ref
  645.4 4.1 shard_map.127.result_ref
  649.5 4.4 collective-permute-done.36.refs_3_
  653.9 4.9 collective-permute-done.35.refs_2_
  660.5 2.4 shard_map.128.result_ref
  662.9 2.4 shard_map.129.result_ref
  665.4 12.2 %collective-permute-done.37.refs_3_ = bf16[2,256,512]{2,1,0:T(8,128)(2,1)S(1)} collective-permute-done((bf16[2,256,512]{2,1,0:T(8,128)(2,1)S(1)}, bf16[2,256,512]{2,1,0:T(8,128)(2,1)S(1)}, u32[]{:S(2)}, u32[]{:S(2)}) %collective-permute-start.37) | collective-permute-done | bytes 524320 | tf_op jit(solution)/shard_map/ppermute | solution.py:314
  677.6 2.3 shard_map.130.result_ref
  679.9 2.3 shard_map.131
  (267 shorter events, 131.2 us)
Async XLA Ops:
  6.5 155.9 %all-gather.6.cloned.1.call-start = ((), (), s32[]{:S(2)}) async-start(), calls=%async_computation | async-start | bytes 11141120 | tf_op jit(solution)/shard_map/all_gather | solution.py:369
  24.5 3.4 copy-start.20
  24.6 17.8 %collective-permute-start.1 = (bf16[256,1280]{1,0:T(8,128)(2,1)S(1)}, bf16[256,1280]{1,0:T(8,128)(2,1)}, u32[]{:S(2)}, u32[]{:S(2)}) collective-permute-start(bf16[256,1280]{1,0:T(8,128)(2,1)S(1)} %pad_maximum_fusion.18), channel_id=1, source_target_pairs={{0,8},{1,9},{2,10},{3,11},{4,12},{5,13},{6,14},{7,15},{8,0},{9,1},... | collective-permute-start | bytes 1966088 | tf_op jit(solution)/shard_map/ppermute | solution.py:317
  26.2 16.2 %collective-permute-start.2 = (bf16[256,1280]{1,0:T(8,128)(2,1)S(1)}, bf16[256,1280]{1,0:T(8,128)(2,1)}, u32[]{:S(2)}, u32[]{:S(2)}) collective-permute-start(bf16[256,1280]{1,0:T(8,128)(2,1)S(1)} %pad_maximum_fusion.19), channel_id=1, source_target_pairs={{0,4},{1,5},{2,6},{3,7},{4,0},{5,1},{6,2},{7,3},{8,12},{9,13},{10,... | collective-permute-start | bytes 1966088 | tf_op jit(solution)/shard_map/ppermute | solution.py:317
  27.1 25.1 %collective-permute-start = (bf16[256,1280]{1,0:T(8,128)(2,1)}, bf16[256,1280]{1,0:T(8,128)(2,1)}, u32[]{:S(2)}, u32[]{:S(2)}) collective-permute-start(bf16[256,1280]{1,0:T(8,128)(2,1)} %pad_maximum_fusion.17), channel_id=1, source_target_pairs={{0,12},{1,13},{2,14},{3,15},{4,8},{5,9},{6,10},{7,11},{8,4},{9,5},... | collective-permute-start | bytes 1966088 | tf_op jit(solution)/shard_map/ppermute | solution.py:317
  34.5 7.6 %copy-start.27 = (bf16[256,2048]{1,0:T(8,128)(2,1)}, bf16[256,2048]{1,0:T(8,128)(2,1)S(1)}, u32[]{:S(2)}) copy-start(bf16[256,2048]{1,0:T(8,128)(2,1)S(1)} %slice.370) | copy-start | bytes 3145732
  36.7 25.9 %collective-permute-start.11 = (bf16[256,2176]{1,0:T(8,128)(2,1)}, bf16[256,2176]{1,0:T(8,128)(2,1)}, u32[]{:S(2)}, u32[]{:S(2)}) collective-permute-start(bf16[256,2176]{1,0:T(8,128)(2,1)} %pad_maximum_fusion.14), channel_id=1, source_target_pairs={{0,1},{3,2},{4,5},{7,6},{8,9},{11,10},{12,13},{15,14},{16,17},{19,... | collective-permute-start | bytes 3342344 | tf_op jit(solution)/shard_map/ppermute | solution.py:314
  54.4 9.5 %copy-start.40 = (bf16[256,2048]{1,0:T(8,128)(2,1)S(1)}, bf16[256,2048]{1,0:T(8,128)(2,1)}, u32[]{:S(2)}) copy-start(bf16[256,2048]{1,0:T(8,128)(2,1)} %get-tuple-element.272) | copy-start | bytes 3145732
  54.7 19.6 %copy-start.2 = (bf16[1024,1280]{1,0:T(8,128)(2,1)}, bf16[1024,1280]{1,0:T(8,128)(2,1)S(1)}, u32[]{:S(2)}) copy-start(bf16[1024,1280]{1,0:T(8,128)(2,1)S(1)} %pad_maximum_fusion.5.refs_1_) | copy-start | bytes 7864324
  54.7 9.2 %copy-start.28 = (bf16[256,2048]{1,0:T(8,128)(2,1)S(1)}, bf16[256,2048]{1,0:T(8,128)(2,1)}, u32[]{:S(2)}) copy-start(bf16[256,2048]{1,0:T(8,128)(2,1)} %copy-done.27) | copy-start | bytes 3145732
  54.7 9.2 %copy-start.39 = (bf16[256,2048]{1,0:T(8,128)(2,1)S(1)}, bf16[256,2048]{1,0:T(8,128)(2,1)}, u32[]{:S(2)}) copy-start(bf16[256,2048]{1,0:T(8,128)(2,1)} %get-tuple-element.271) | copy-start | bytes 3145732
  67.4 7.7 %slice-start.7 = ((bf16[512,512]{1,0:T(8,128)(2,1)}), bf16[256,512]{1,0:T(8,128)(2,1)S(1)}, s32[]{:S(2)}) async-start(bf16[512,512]{1,0:T(8,128)(2,1)} %param.14), calls=%async_computation.11 | async-start | bytes 524288 | tf_op jit(solution)/shard_map/slice | solution.py:345
  67.5 7.7 %slice-start.8 = ((bf16[512,512]{1,0:T(8,128)(2,1)}), bf16[256,512]{1,0:T(8,128)(2,1)S(1)}, s32[]{:S(2)}) async-start(bf16[512,512]{1,0:T(8,128)(2,1)} %param.15), calls=%async_computation.12 | async-start | bytes 524288 | tf_op jit(solution)/shard_map/slice | solution.py:346
  67.5 230.0 %all-gather.12.cloned.1.call-start = ((), (), s32[]{:S(2)}) async-start(), calls=%async_computation.3 | async-start | bytes 10485760 | tf_op jit(solution)/shard_map/all_gather | solution.py:369
  69.7 71.4 %collective-permute-start.7 = (bf16[256,6144]{1,0:T(8,128)(2,1)S(1)}, bf16[256,6144]{1,0:T(8,128)(2,1)S(1)}, u32[]{:S(2)}, u32[]{:S(2)}) collective-permute-start(bf16[256,6144]{1,0:T(8,128)(2,1)S(1)} %slice.369), channel_id=1, source_target_pairs={{0,1},{3,2},{4,5},{7,6},{8,9},{11,10},{12,13},{15,14},{16,17},{19,... | collective-permute-start | bytes 9437192 | tf_op jit(solution)/shard_map/ppermute | solution.py:314
  74.3 66.8 %collective-permute-start.6 = (bf16[1024,1280]{1,0:T(8,128)(2,1)S(1)}, bf16[1024,1280]{1,0:T(8,128)(2,1)S(1)}, u32[]{:S(2)}, u32[]{:S(2)}) collective-permute-start(bf16[1024,1280]{1,0:T(8,128)(2,1)S(1)} %pad_maximum_fusion.5.refs_1_), channel_id=1, source_target_pairs={{2,1},{1,2},{6,5},{5,6},{10,9},{9,10},{14,13},{13,14},{18,17},{17,... | collective-permute-start | bytes 7864328 | tf_op jit(solution)/shard_map/ppermute | solution.py:314
  77.5 2.2 collective-permute-start.5
  77.6 31.6 %collective-permute-start.4 = (bf16[256,1280]{1,0:T(8,128)(2,1)S(1)}, bf16[256,1280]{1,0:T(8,128)(2,1)S(1)}, u32[]{:S(2)}, u32[]{:S(2)}) collective-permute-start(bf16[256,1280]{1,0:T(8,128)(2,1)S(1)} %pad_maximum_fusion.22), channel_id=1, source_target_pairs={{0,8},{1,9},{2,10},{3,11},{4,12},{5,13},{6,14},{7,15},{8,0},{9,1},... | collective-permute-start | bytes 1966088 | tf_op jit(solution)/shard_map/ppermute | solution.py:317
  79.2 57.3 %collective-permute-start.3 = (bf16[256,1280]{1,0:T(8,128)(2,1)S(1)}, bf16[256,1280]{1,0:T(8,128)(2,1)S(1)}, u32[]{:S(2)}, u32[]{:S(2)}) collective-permute-start(bf16[256,1280]{1,0:T(8,128)(2,1)S(1)} %pad_maximum_fusion.21), channel_id=1, source_target_pairs={{0,12},{1,13},{2,14},{3,15},{4,8},{5,9},{6,10},{7,11},{8,4},{9,5},... | collective-permute-start | bytes 1966088 | tf_op jit(solution)/shard_map/ppermute | solution.py:317
  137.3 3.9 copy-start.26
  145.8 175.3 %all-gather.10.cloned.1.call-start = ((), (), s32[]{:S(2)}) async-start(), calls=%async_computation.2 | async-start | bytes 10485760 | tf_op jit(solution)/shard_map/all_gather | solution.py:369
  145.9 14.3 %copy-start.31 = (bf16[256,6144]{1,0:T(8,128)(2,1)S(1)}, bf16[256,6144]{1,0:T(8,128)(2,1)}, u32[]{:S(2)}) copy-start(bf16[256,6144]{1,0:T(8,128)(2,1)} %copy-done.30) | copy-start | bytes 9437188
  145.9 59.9 %collective-permute-start.8 = (bf16[1024,1280]{1,0:T(8,128)(2,1)}, bf16[1024,1280]{1,0:T(8,128)(2,1)}, u32[]{:S(2)}, u32[]{:S(2)}) collective-permute-start(bf16[1024,1280]{1,0:T(8,128)(2,1)} %copy-done.2), channel_id=1, source_target_pairs={{0,1},{3,2},{4,5},{7,6},{8,9},{11,10},{12,13},{15,14},{16,17},{19,... | collective-permute-start | bytes 7864328 | tf_op jit(solution)/shard_map/ppermute | solution.py:314
  152.1 53.7 %collective-permute-start.9 = (bf16[1024,1280]{1,0:T(8,128)(2,1)}, bf16[1024,1280]{1,0:T(8,128)(2,1)}, u32[]{:S(2)}, u32[]{:S(2)}) collective-permute-start(bf16[1024,1280]{1,0:T(8,128)(2,1)} %pad_maximum_fusion.6.refs_2_), channel_id=1, source_target_pairs={{2,1},{1,2},{6,5},{5,6},{10,9},{9,10},{14,13},{13,14},{18,17},{17,... | collective-permute-start | bytes 7864328 | tf_op jit(solution)/shard_map/ppermute | solution.py:314
  157.4 48.1 %collective-permute-start.10 = (bf16[256,4096]{1,0:T(8,128)(2,1)}, bf16[256,4096]{1,0:T(8,128)(2,1)}, u32[]{:S(2)}, u32[]{:S(2)}) collective-permute-start(bf16[256,4096]{1,0:T(8,128)(2,1)} %slice.294), channel_id=1, source_target_pairs={{1,0},{2,3},{5,4},{6,7},{9,8},{10,11},{13,12},{14,15},{17,16},{18,... | collective-permute-start | bytes 6291464 | tf_op jit(solution)/shard_map/ppermute | solution.py:314
  210.3 129.5 %all-gather.8.cloned.1.call-start = ((), (), s32[]{:S(2)}) async-start(), calls=%async_computation.1 | async-start | bytes 10485760 | tf_op jit(solution)/shard_map/all_gather | solution.py:369
  210.3 60.0 %collective-permute-start.12 = (bf16[1024,1280]{1,0:T(8,128)(2,1)}, bf16[1024,1280]{1,0:T(8,128)(2,1)}, u32[]{:S(2)}, u32[]{:S(2)}) collective-permute-start(bf16[1024,1280]{1,0:T(8,128)(2,1)} %pad_maximum_fusion.6.refs_2_), channel_id=1, source_target_pairs={{0,1},{3,2},{4,5},{7,6},{8,9},{11,10},{12,13},{15,14},{16,17},{19,... | collective-permute-start | bytes 7864328 | tf_op jit(solution)/shard_map/ppermute | solution.py:314
  217.5 52.9 %collective-permute-start.13 = (bf16[1024,1280]{1,0:T(8,128)(2,1)}, bf16[1024,1280]{1,0:T(8,128)(2,1)S(1)}, u32[]{:S(2)}, u32[]{:S(2)}) collective-permute-start(bf16[1024,1280]{1,0:T(8,128)(2,1)} %collective-permute-done.8.refs_1_), channel_id=1, source_target_pairs={{2,1},{1,2},{6,5},{5,6},{10,9},{9,10},{14,13},{13,14},{18,17},{17,... | collective-permute-start | bytes 7864328 | tf_op jit(solution)/shard_map/ppermute | solution.py:314
  220.0 46.9 %collective-permute-start.14 = (bf16[256,4096]{1,0:T(8,128)(2,1)S(1)}, bf16[256,4096]{1,0:T(8,128)(2,1)S(1)}, u32[]{:S(2)}, u32[]{:S(2)}) collective-permute-start(bf16[256,4096]{1,0:T(8,128)(2,1)S(1)} %slice.301), channel_id=1, source_target_pairs={{1,0},{2,3},{5,4},{6,7},{9,8},{10,11},{13,12},{14,15},{17,16},{18,... | collective-permute-start | bytes 6291464 | tf_op jit(solution)/shard_map/ppermute | solution.py:314
  275.2 64.6 %collective-permute-start.15 = (bf16[1024,1280]{1,0:T(8,128)(2,1)}, bf16[1024,1280]{1,0:T(8,128)(2,1)}, u32[]{:S(2)}, u32[]{:S(2)}) collective-permute-start(bf16[1024,1280]{1,0:T(8,128)(2,1)} %collective-permute-done.12.refs_2_), channel_id=1, source_target_pairs={{2,1},{1,2},{6,5},{5,6},{10,9},{9,10},{14,13},{13,14},{18,17},{17,... | collective-permute-start | bytes 7864328 | tf_op jit(solution)/shard_map/ppermute | solution.py:314
  279.1 12.6 %copy-start.29 = (bf16[4,1,256,1024]{3,2,1,0:T(8,128)(2,1)}, bf16[4,1,256,1024]{3,2,1,0:T(8,128)(2,1)S(1)}, u32[]{:S(2)}) copy-start(bf16[4,1,256,1024]{3,2,1,0:T(8,128)(2,1)S(1)} %constant_dynamic-slice_fusion.3) | copy-start | bytes 6291460
  279.1 60.6 %collective-permute-start.16 = (bf16[1024,1024]{1,0:T(8,128)(2,1)S(1)}, bf16[1024,1024]{1,0:T(8,128)(2,1)}, u32[]{:S(2)}, u32[]{:S(2)}) collective-permute-start(bf16[1024,1024]{1,0:T(8,128)(2,1)S(1)} %bitcast.91), channel_id=1, source_target_pairs={{0,1},{3,2},{4,5},{7,6},{8,9},{11,10},{12,13},{15,14},{16,17},{19,... | collective-permute-start | bytes 6291464 | tf_op jit(solution)/shard_map/ppermute | solution.py:314
  300.5 96.3 %collective-permute-start.18 = (bf16[1024,1024]{1,0:T(8,128)(2,1)}, bf16[1024,1024]{1,0:T(8,128)(2,1)}, u32[]{:S(2)}, u32[]{:S(2)}) collective-permute-start(bf16[1024,1024]{1,0:T(8,128)(2,1)} %bitcast.15.second_ref), channel_id=1, source_target_pairs={{0,1},{3,2},{4,5},{7,6},{8,9},{11,10},{12,13},{15,14},{16,17},{19,... | collective-permute-start | bytes 6291464 | tf_op jit(solution)/shard_map/ppermute | solution.py:314
  352.5 18.6 %collective-permute-start.17 = (bf16[4,512,256]{2,1,0:T(8,128)(2,1)}, bf16[4,512,256]{2,1,0:T(8,128)(2,1)}, u32[]{:S(2)}, u32[]{:S(2)}) collective-permute-start(bf16[4,512,256]{2,1,0:T(8,128)(2,1)} %pad_maximum_fusion.13), channel_id=1, source_target_pairs={{1,2},{5,6},{9,10},{13,14},{17,18},{21,22},{25,26},{29,30}} | collective-permute-start | bytes 3145736 | tf_op jit(solution)/shard_map/ppermute | solution.py:314
  356.6 16.5 %copy-start.33 = (bf16[2048,128]{1,0:T(8,128)(2,1)S(1)}, bf16[2048,128]{1,0:T(8,128)(2,1)}, u32[]{:S(2)}) copy-start(bf16[2048,128]{1,0:T(8,128)(2,1)} %copy-done.32) | copy-start | bytes 1572868
  356.6 16.5 %copy-start.35 = (bf16[2048,128]{1,0:T(8,128)(2,1)S(1)}, bf16[2048,128]{1,0:T(8,128)(2,1)}, u32[]{:S(2)}) copy-start(bf16[2048,128]{1,0:T(8,128)(2,1)} %copy-done.34) | copy-start | bytes 1572868
  371.0 69.6 %collective-permute-start.19 = (bf16[1024,1024]{1,0:T(8,128)(2,1)}, bf16[1024,1024]{1,0:T(8,128)(2,1)}, u32[]{:S(2)}, u32[]{:S(2)}) collective-permute-start(bf16[1024,1024]{1,0:T(8,128)(2,1)} %collective-permute-done.16.first_ref), channel_id=1, source_target_pairs={{2,1},{1,2},{6,5},{5,6},{10,9},{9,10},{14,13},{13,14},{18,17},{17,... | collective-permute-start | bytes 6291464 | tf_op jit(solution)/shard_map/ppermute | solution.py:314
  396.8 56.1 %collective-permute-start.20 = (bf16[1024,1024]{1,0:T(8,128)(2,1)}, bf16[1024,1024]{1,0:T(8,128)(2,1)}, u32[]{:S(2)}, u32[]{:S(2)}) collective-permute-start(bf16[1024,1024]{1,0:T(8,128)(2,1)} %shard_map.106.b_ref), channel_id=1, source_target_pairs={{1,0},{2,3},{5,4},{6,7},{9,8},{10,11},{13,12},{14,15},{17,16},{18,... | collective-permute-start | bytes 6291464 | tf_op jit(solution)/shard_map/ppermute | solution.py:314
  401.4 63.8 %collective-permute-start.22 = (bf16[1024,1024]{1,0:T(8,128)(2,1)}, bf16[1024,1024]{1,0:T(8,128)(2,1)}, u32[]{:S(2)}, u32[]{:S(2)}) collective-permute-start(bf16[1024,1024]{1,0:T(8,128)(2,1)} %bitcast.25.second_ref), channel_id=1, source_target_pairs={{0,1},{3,2},{4,5},{7,6},{8,9},{11,10},{12,13},{15,14},{16,17},{19,... | collective-permute-start | bytes 6291464 | tf_op jit(solution)/shard_map/ppermute | solution.py:314
  414.6 50.6 %collective-permute-start.21 = (bf16[1024,1024]{1,0:T(8,128)(2,1)}, bf16[1024,1024]{1,0:T(8,128)(2,1)}, u32[]{:S(2)}, u32[]{:S(2)}) collective-permute-start(bf16[1024,1024]{1,0:T(8,128)(2,1)} %collective-permute-done.18.first_ref), channel_id=1, source_target_pairs={{2,1},{1,2},{6,5},{5,6},{10,9},{9,10},{14,13},{13,14},{18,17},{17,... | collective-permute-start | bytes 6291464 | tf_op jit(solution)/shard_map/ppermute | solution.py:314
  465.3 13.8 %collective-permute-start.23 = (bf16[4,512,1024]{2,1,0:T(8,128)(2,1)S(1)}, bf16[4,512,1024]{2,1,0:T(8,128)(2,1)S(1)}, u32[]{:S(2)}, u32[]{:S(2)}) collective-permute-start(bf16[4,512,1024]{2,1,0:T(8,128)(2,1)S(1)} %pad_maximum_fusion.2), channel_id=1, source_target_pairs={{0,4},{1,5},{2,6},{3,7},{4,0},{5,1},{6,2},{7,3},{8,12},{9,13},{10,... | collective-permute-start | bytes 12582920 | tf_op jit(solution)/shard_map/ppermute | solution.py:317
  468.5 54.5 %collective-permute-start.24 = (bf16[1024,1024]{1,0:T(8,128)(2,1)}, bf16[1024,1024]{1,0:T(8,128)(2,1)}, u32[]{:S(2)}, u32[]{:S(2)}) collective-permute-start(bf16[1024,1024]{1,0:T(8,128)(2,1)} %bitcast.29.second_ref), channel_id=1, source_target_pairs={{0,1},{3,2},{4,5},{7,6},{8,9},{11,10},{12,13},{15,14},{16,17},{19,... | collective-permute-start | bytes 6291464 | tf_op jit(solution)/shard_map/ppermute | solution.py:314
  479.1 6.6 copy-start.24
  482.1 48.0 %collective-permute-start.26 = (bf16[4,256,1024]{2,1,0:T(8,128)(2,1)}, bf16[4,256,1024]{2,1,0:T(8,128)(2,1)S(1)}, u32[]{:S(2)}, u32[]{:S(2)}) collective-permute-start(bf16[4,256,1024]{2,1,0:T(8,128)(2,1)} %add_convert_fusion.1), channel_id=1, source_target_pairs={{0,8},{1,9},{2,10},{3,11},{4,12},{5,13},{6,14},{7,15},{8,0},{9,1},... | collective-permute-start | bytes 6291464 | tf_op jit(solution)/shard_map/ppermute | solution.py:317
  482.1 48.0 %collective-permute-start.25 = (bf16[1024,1024]{1,0:T(8,128)(2,1)}, bf16[1024,1024]{1,0:T(8,128)(2,1)}, u32[]{:S(2)}, u32[]{:S(2)}) collective-permute-start(bf16[1024,1024]{1,0:T(8,128)(2,1)} %collective-permute-done.22.first_ref), channel_id=1, source_target_pairs={{2,1},{1,2},{6,5},{5,6},{10,9},{9,10},{14,13},{13,14},{18,17},{17,... | collective-permute-start | bytes 6291464 | tf_op jit(solution)/shard_map/ppermute | solution.py:314
  530.0 7.2 %collective-permute-start.27 = (bf16[4,512,1024]{2,1,0:T(8,128)(2,1)S(1)}, bf16[4,512,1024]{2,1,0:T(8,128)(2,1)S(1)}, u32[]{:S(2)}, u32[]{:S(2)}) collective-permute-start(bf16[4,512,1024]{2,1,0:T(8,128)(2,1)S(1)} %pad_maximum_fusion.4), channel_id=1, source_target_pairs={{0,4},{1,5},{2,6},{3,7},{4,0},{5,1},{6,2},{7,3},{8,12},{9,13},{10,... | collective-permute-start | bytes 12582920 | tf_op jit(solution)/shard_map/ppermute | solution.py:317
  530.6 7.7 %copy-start.23 = (bf16[4,512,1024]{2,1,0:T(8,128)(2,1)}, bf16[4,512,1024]{2,1,0:T(8,128)(2,1)S(1)}, u32[]{:S(2)}) copy-start(bf16[4,512,1024]{2,1,0:T(8,128)(2,1)S(1)} %pad_maximum_fusion.3.refs_0_) | copy-start | bytes 12582916
  537.2 8.0 %copy-start.25 = (bf16[4,512,1024]{2,1,0:T(8,128)(2,1)}, bf16[4,512,1024]{2,1,0:T(8,128)(2,1)S(1)}, u32[]{:S(2)}) copy-start(bf16[4,512,1024]{2,1,0:T(8,128)(2,1)S(1)} %collective-permute-done.27.refs_1_) | copy-start | bytes 12582916
  538.3 47.7 %collective-permute-start.29 = (bf16[4,256,1024]{2,1,0:T(8,128)(2,1)S(1)}, bf16[4,256,1024]{2,1,0:T(8,128)(2,1)S(1)}, u32[]{:S(2)}, u32[]{:S(2)}) collective-permute-start(bf16[4,256,1024]{2,1,0:T(8,128)(2,1)S(1)} %add_convert_fusion), channel_id=1, source_target_pairs={{0,8},{1,9},{2,10},{3,11},{4,12},{5,13},{6,14},{7,15},{8,0},{9,1},... | collective-permute-start | bytes 6291464 | tf_op jit(solution)/shard_map/ppermute | solution.py:317
  538.6 47.4 %collective-permute-start.28 = (bf16[1024,1024]{1,0:T(8,128)(2,1)}, bf16[1024,1024]{1,0:T(8,128)(2,1)}, u32[]{:S(2)}, u32[]{:S(2)}) collective-permute-start(bf16[1024,1024]{1,0:T(8,128)(2,1)} %collective-permute-done.24.first_ref), channel_id=1, source_target_pairs={{2,1},{1,2},{6,5},{5,6},{10,9},{9,10},{14,13},{13,14},{18,17},{17,... | collective-permute-start | bytes 6291464 | tf_op jit(solution)/shard_map/ppermute | solution.py:314
  542.1 17.7 %collective-permute-start.30 = (bf16[2,256,512]{2,1,0:T(8,128)(2,1)S(1)}, bf16[2,256,512]{2,1,0:T(8,128)(2,1)S(1)}, u32[]{:S(2)}, u32[]{:S(2)}) collective-permute-start(bf16[2,256,512]{2,1,0:T(8,128)(2,1)S(1)} %pad_maximum_fusion.25), channel_id=1, source_target_pairs={{1,0},{2,3},{5,4},{6,7},{9,8},{10,11},{13,12},{14,15},{17,16},{18,... | collective-permute-start | bytes 1572872 | tf_op jit(solution)/shard_map/ppermute | solution.py:314
  586.0 4.2 collective-permute-start.31
  591.5 25.5 %collective-permute-start.32 = (bf16[2,256,1024]{2,1,0:T(8,128)(2,1)}, bf16[2,256,1024]{2,1,0:T(8,128)(2,1)}, u32[]{:S(2)}, u32[]{:S(2)}) collective-permute-start(bf16[2,256,1024]{2,1,0:T(8,128)(2,1)} %add_convert_fusion.3), channel_id=1, source_target_pairs={{0,8},{1,9},{2,10},{3,11},{4,12},{5,13},{6,14},{7,15},{8,0},{9,1},... | collective-permute-start | bytes 3145736 | tf_op jit(solution)/shard_map/ppermute | solution.py:317
  593.3 18.6 %collective-permute-start.33 = (bf16[2,256,512]{2,1,0:T(8,128)(2,1)S(1)}, bf16[2,256,512]{2,1,0:T(8,128)(2,1)S(1)}, u32[]{:S(2)}, u32[]{:S(2)}) collective-permute-start(bf16[2,256,512]{2,1,0:T(8,128)(2,1)S(1)} %pad_maximum_fusion.26), channel_id=1, source_target_pairs={{1,0},{2,3},{5,4},{6,7},{9,8},{10,11},{13,12},{14,15},{17,16},{18,... | collective-permute-start | bytes 1572872 | tf_op jit(solution)/shard_map/ppermute | solution.py:314
  603.5 5.1 copy-start.19
  608.6 10.5 %copy-start.16 = (bf16[512,1024]{1,0:T(8,128)(2,1)}, bf16[512,1024]{1,0:T(8,128)(2,1)S(1)}, u32[]{:S(2)}) copy-start(bf16[512,1024]{1,0:T(8,128)(2,1)S(1)} %get-tuple-element.219) | copy-start | bytes 3145732
  608.6 8.5 %copy-start.21 = (bf16[256,8192]{1,0:T(8,128)(2,1)S(1)}, bf16[256,8192]{1,0:T(8,128)(2,1)}, u32[]{:S(2)}) copy-start(bf16[256,8192]{1,0:T(8,128)(2,1)} %hidden_ref.24) | copy-start | bytes 12582916
  617.1 15.6 %collective-permute-start.34 = (bf16[2,512,1024]{2,1,0:T(8,128)(2,1)}, bf16[2,512,1024]{2,1,0:T(8,128)(2,1)S(1)}, u32[]{:S(2)}, u32[]{:S(2)}) collective-permute-start(bf16[2,512,1024]{2,1,0:T(8,128)(2,1)} %pad_maximum_fusion.10), channel_id=1, source_target_pairs={{0,4},{1,5},{2,6},{3,7},{4,0},{5,1},{6,2},{7,3},{8,12},{9,13},{10,... | collective-permute-start | bytes 6291464 | tf_op jit(solution)/shard_map/ppermute | solution.py:317
  628.3 4.2 copy-start.15
  628.3 4.2 copy-start.17
  633.1 3.0 copy-start.13
  633.1 25.6 %collective-permute-start.35 = (bf16[2,256,1024]{2,1,0:T(8,128)(2,1)S(1)}, bf16[2,256,1024]{2,1,0:T(8,128)(2,1)S(1)}, u32[]{:S(2)}, u32[]{:S(2)}) collective-permute-start(bf16[2,256,1024]{2,1,0:T(8,128)(2,1)S(1)} %add_convert_fusion.2), channel_id=1, source_target_pairs={{0,8},{1,9},{2,10},{3,11},{4,12},{5,13},{6,14},{7,15},{8,0},{9,1},... | collective-permute-start | bytes 3145736 | tf_op jit(solution)/shard_map/ppermute | solution.py:317
  634.8 19.1 %collective-permute-start.36 = (bf16[2,256,512]{2,1,0:T(8,128)(2,1)S(1)}, bf16[2,256,512]{2,1,0:T(8,128)(2,1)S(1)}, u32[]{:S(2)}, u32[]{:S(2)}) collective-permute-start(bf16[2,256,512]{2,1,0:T(8,128)(2,1)S(1)} %pad_maximum_fusion.27), channel_id=1, source_target_pairs={{1,0},{2,3},{5,4},{6,7},{9,8},{10,11},{13,12},{14,15},{17,16},{18,... | collective-permute-start | bytes 1572872 | tf_op jit(solution)/shard_map/ppermute | solution.py:314
  659.1 18.5 %collective-permute-start.37 = (bf16[2,256,512]{2,1,0:T(8,128)(2,1)S(1)}, bf16[2,256,512]{2,1,0:T(8,128)(2,1)S(1)}, u32[]{:S(2)}, u32[]{:S(2)}) collective-permute-start(bf16[2,256,512]{2,1,0:T(8,128)(2,1)S(1)} %pad_maximum_fusion.28), channel_id=1, source_target_pairs={{1,0},{2,3},{5,4},{6,7},{9,8},{10,11},{13,12},{14,15},{17,16},{18,... | collective-permute-start | bytes 1572872 | tf_op jit(solution)/shard_map/ppermute | solution.py:314
  (30 other events, 55.3 us)
Sparse Core Ops, SparseCore 0:
  67.6 89.4 all-gather.5
  158.6 58.2 all-gather.11
  218.5 58.2 all-gather.9
  278.3 58.2 all-gather.7

commit v4 on v3

--- a/solution.py
+++ b/solution.py
@@ -347,14 +347,8 @@
             ], axis=1)
         return block
 
-    segments = lax.all_gather(segment_ids, "tp", axis=0, tiled=True)
-    segments, hidden, output_weight, weights = tie(
-        (segments, hidden_in, output_weight, (query_weight, key_weight, value_weight)))
-    my_starts = lax.dynamic_slice_in_dim(segment_starts(segments), t * rows, rows)
-    digits = jnp.stack([my_starts // 256, my_starts % 256], axis=1).astype(jnp.bfloat16)
-    digits = jnp.pad(digits, ((0, 0), (0, HEAD - 2)))
-
-    mine = normalize(hidden, norm_gain, order, n_f, depth, cuts)
+    weights = (query_weight, key_weight, value_weight)
+    mine = normalize(hidden_in, norm_gain, order, n_f, depth, cuts)
     part = n_f * depth
 
     def gather(k, theirs, outputs):
@@ -363,9 +357,9 @@
         outputs = jnp.concatenate(
             [outputs[:, c * part:(c + 1) * part] for c in range(chunks)], axis=0)
         payload = jnp.where(is_inner, both, outputs)
-        if k == 0:
+        if k == 1:
             payload = jnp.concatenate(
-                [payload, jnp.concatenate([digits, their_digits], axis=0)], axis=1)
+                [payload, jnp.concatenate([digits, tail[:, width - early:]], axis=0)], axis=1)
         return lax.all_gather(payload, "fsdp", axis=0, tiled=True)
 
     def output_rows(gathered, count):
@@ -379,10 +373,15 @@
     early = part
 
     own = [level_exchange(projection_block(weights, 0), every)]
-    head = send(jnp.concatenate([mine[:, :early], digits], axis=1), inward)
-    tail = send(mine[:, early:], inward)
-    own, weights = tie((own, weights))
-    their_digits = head[:, early:]
+    head = send(mine[:, :early], inward)
+    own, weights, segment_ids = tie((own, weights, segment_ids))
+
+    segments = lax.all_gather(segment_ids, "tp", axis=0, tiled=True)
+    own, segments = tie((own, segments))
+    my_starts = lax.dynamic_slice_in_dim(segment_starts(segments), t * rows, rows)
+    digits = jnp.stack([my_starts // 256, my_starts % 256], axis=1).astype(jnp.bfloat16)
+    digits = jnp.pad(digits, ((0, 0), (0, HEAD - 2)))
+    tail = send(jnp.concatenate([mine[:, early:], digits], axis=1), inward)
     raw = []
 
     def source(k):
@@ -397,7 +396,7 @@
     own += [level_exchange(projection_block(weights, h), every) for h in range(1, cuts)]
     gathered = [gather(0, tie((head, own[0]))[0][:, :part], source(0))]
     own, across, tail, mine, output_weight = tie((own, across, tail, mine, output_weight))
-    theirs = jnp.concatenate([head[:, :early], tail], axis=1)
+    theirs = jnp.concatenate([head, tail[:, :width - early]], axis=1)
 
     beyond = []
     projected = None
@@ -467,7 +466,7 @@
     level_ids = jnp.arange(rows, dtype=jnp.int32)
     pair_ids = jnp.concatenate([my_inner * rows + level_ids, my_outer * rows + level_ids])
     row_ids = jnp.tile(pair_ids, n_f)
-    digits = gathered[0][:, part:part + 2].astype(jnp.int32)
+    digits = gathered[1][:, part:part + 2].astype(jnp.int32)
     starts = digits[:, 0] * 256 + digits[:, 1]
     cosine, sine = rotary_tables((row_ids - starts).astype(jnp.float32))
 
@@ -481,13 +480,17 @@
     key_value = jnp.concatenate(
         [keys.reshape(n_f, pair_rows, HEAD), values.reshape(n_f, pair_rows, HEAD)], axis=-1
     )
+    start = None
+    if groups:
+        start = send(at_inner[0][:cut], shift(1))
+        key_value, start = tie((key_value, start))
     seen = [key_value]
     reach = min(n_t - 1, -(-(LONGEST - 1) // rows))
     for s in range(1, min(n_pairs - 1, (reach + 1) // 2) + 1):
         seen.append(send(key_value, [(inner[j - s], inner[j]) for j in range(s, n_pairs)]))
     if groups:
-        at_inner[0] = tie((at_inner[0], seen[1]))[0]
-    got = send_group(groups[0]) if groups else None
+        rest, projected_queries = tie((at_inner[0][cut:], projected_queries, seen[1]))[:2]
+        got = send(rest, shift(1))
     if len(at_inner) < 2 * cuts:
         at_outer.append(outer_run(1))
         at_inner.append(send(at_outer[1], inward))
@@ -547,34 +550,36 @@
         ]
         return items, terms, send(jnp.stack(sums), outward)
 
-    def put(result, items, terms, other):
-        n_other = 0
+    def put_own(result, items, terms):
         for i, item in enumerate(items):
-            level, h = 1 - item[1] // cuts, item[1] % cuts
             if item[0] == 0:
                 result = add_up(
-                    result, hidden_in, terms, i, None, 0, is_inner, n_f, order[level],
-                    n_t, cuts, cut, h, 0)
-            else:
-                result = add_up(
-                    result, hidden_in, terms, i, other, n_other, is_inner, half,
-                    order[2 * item[0] + level], n_t, cuts, cut, h, item[2] * half)
-                n_other += 1
+                    result, hidden_in, terms, i, None, 0, is_inner, n_f,
+                    order[1 - item[1] // cuts], n_t, cuts, cut, item[1] % cuts, 0)
         return result
 
+    def put_others(result, items, terms, other):
+        others = [i for i, item in enumerate(items) if item[0]]
+        for n, i in enumerate(others):
+            s, r, p = items[i]
+            result = add_up(
+                result, hidden_in, terms, i, other, n, is_inner, half,
+                order[2 * s + 1 - r // cuts], n_t, cuts, cut, r % cuts, p * half)
+        return result
+
     mixed_outer = attend(1)
-    mixed_outer, at_inner, at_outer, projected_queries, seen = tie(
-        (mixed_outer, at_inner, at_outer, projected_queries, seen))
+    mixed_outer, at_inner, at_outer, projected_queries, seen, got = tie(
+        (mixed_outer, at_inner, at_outer, projected_queries, seen, got))
     if groups:
-        arrive(groups[0], got)
+        arrive(groups[0], jnp.concatenate([start, got], axis=0))
     runs = [(0, r) for r in range(2 * cuts)]
     result, phase, from_cores, from_chips, from_levels = hidden_in, 1, None, None, None
-    while phase <= len(groups) or runs or from_cores or from_chips or from_levels:
+    while True:
         got = send_group(groups[phase]) if phase < len(groups) else None
         if len(at_inner) < 2 * cuts:
             at_outer.append(outer_run(len(at_inner)))
             at_inner.append(send(at_outer[-1], inward))
-        received = from_levels
+        received, crossed = from_levels, from_chips
         from_levels = between_levels(*from_chips) if from_chips else None
         from_chips = between_chips(*from_cores) if from_cores else None
         if phase == 1:
@@ -584,10 +589,14 @@
         items = list(groups[phase - 1]) if phase <= len(groups) else []
         ready = runs[:cuts]
         items, runs = items + ready, runs[cuts:]
-        long_ones = (got, at_inner[-1:], from_chips and from_chips[1], from_levels and from_levels[2], there)
+        if phase >= len(groups) and not runs:
+            break
+        if received:
+            result = put_others(result, *received)
+        if crossed:
+            result = put_own(result, *crossed)
+        long_ones = (result, got, at_inner[-1:], from_chips and from_chips[1], from_levels and from_levels[2], there)
         from_cores = between_cores(items, long_ones) if items else None
-        if received:
-            result = put(result, *received)
         moving = [None if x is None else x[1:] for x in (from_cores, from_chips, from_levels)]
         moving, got, at_inner, at_outer, result = tie((moving, got, at_inner, at_outer, result))
         from_cores, from_chips, from_levels = [
@@ -597,7 +606,20 @@
         if got is not None:
             arrive(groups[phase], got)
         phase += 1
-    return result
+
+    if received:
+        result = put_others(result, *received)
+    items, kept, given = between_cores(items, (from_chips and from_chips[1], result))
+    final = between_chips(items, kept, given)
+    if crossed:
+        result = put_own(result, *crossed)
+    if from_levels:
+        result = put_others(result, *from_levels)
+    before = between_levels(*from_chips) if from_chips else None
+    terms, moved, result = tie((final[1], before and before[1:], result))
+    if before:
+        result = put_others(put_own(result, before[0], moved[0]), before[0], *moved)
+    return put_others(put_own(result, items, terms), *between_levels(items, terms))
 
 
 def solution(mesh):

time: 699 us -> 685 us (0.980)
  waiting for transfers between devices: 244 us -> 229 us
  local copies, waits for them, and re-layouts: 69.1 us -> 59.3 us
    ppermute x24 -> x25, waiting for transfers between devices: 130 us -> 117 us  [send(): return lax.ppermute(value, 'tp', pairs)]
    unnamed x90 -> x64, local copies, waits for them, and re-layouts: 23.5 us -> 18.7 us
    ppermute x24 -> x25, starting transfers between devices: 79.5 us -> 77.4 us  [send(): return lax.ppermute(value, 'tp', pairs)]
  transfers between devices with their start and end apart: 42 -> 43, of which waited for: 21 -> 20; matrix products, arithmetic and copies ran while one was open for 12% -> 12% of each run, Pallas kernels for 30% -> 31%
where the time goes in v4:
time: 685 us; the launch traced here: 675 us
  waiting for transfers between devices  229 us (33%)
  Pallas kernels  214 us (31%)
  starting transfers between devices  89.8 us (13%)
  local copies, waits for them, and re-layouts  59.3 us (9%)
  other arithmetic  56.3 us (8%)
  between operations  14.4 us (2%)
  blocking collectives  11.2 us (2%)
    ppermute x25, waiting for transfers between devices, send(): return lax.ppermute(value, 'tp', pairs)  117 us
    ppermute x14, waiting for transfers between devices, swap(): lax.ppermute(value, LEVEL, [(i * n_t + z, (i ^ d) * n_t + z) for i in ran...  113 us
    ppermute x25, starting transfers between devices, send(): return lax.ppermute(value, 'tp', pairs)  77.4 us
    pallas_call x5, Pallas kernels, project(): pl.pallas_call(kernel, grid=(n_rows // block,), in_specs=[pl.BlockSpec((b...  70.9 us
    pallas_call x2, Pallas kernels, attention(): pl.pallas_call(kernel, grid_spec=pltpu.PrefetchScalarGridSpec(num_scalar_...  42.2 us
    pallas_call x8, Pallas kernels, partials_of_two(): pl.pallas_call(kernel, grid=(4,), in_specs=[rows, rows, pl.BlockSpec((wid...  40.7 us
    pallas_call x12, Pallas kernels, add_up(): pl.pallas_call(kernel, grid_spec=pltpu.PrefetchScalarGridSpec(num_scalar_...  36 us
    pallas_call x4, Pallas kernels, partials_of_one(): pl.pallas_call(kernel, grid_spec=pltpu.PrefetchScalarGridSpec(num_scalar_...  19.7 us
  transfers between devices with their start and end apart: 43, of which 20 were waited for; matrix products, arithmetic and copies ran while one was open for 12% of the time, Pallas kernels for 31%

profile of v4, /device:TPU:0, one launch (start us, length us, event | category | flops | bytes accessed | tf_op | source)
XLA Modules:
  0.0 674.6 jit_solution(4743173157349163267)
XLA Ops:
  12.1 2.9 collective-permute-start.1
  17.1 4.8 shard_map.100
  24.0 5.1 collective-permute-start.11
  31.0 12.5 %collective-permute-done = bf16[256,1280]{1,0:T(8,128)(2,1)} collective-permute-done((bf16[256,1280]{1,0:T(8,128)(2,1)}, bf16[256,1280]{1,0:T(8,128)(2,1)}, u32[]{:S(2)}, u32[]{:S(2)}) %collective-permute-start) | collective-permute-done | bytes 655392 | tf_op jit(solution)/shard_map/ppermute | solution.py:317
  47.4 11.2 %all-gather = s32[4,1,256]{2,1,0:T(1,128)S(1)} all-gather(s32[1,1,256]{2,1,0:T(1,128)S(1)} %bitcast.99), channel_id=1, replica_groups=mesh['groups'=2,'fsdp'=4,'tp'=4] {'tp'}, dimensions={0}, use_global_device_ids=true | all-gather | bytes 5120 | tf_op jit(solution)/shard_map/all_gather | solution.py:379
  58.6 3.4 maximum_select_fusion
  71.4 28.9 %collective-permute-done.4 = bf16[256,1280]{1,0:T(8,128)(2,1)S(1)} collective-permute-done((bf16[256,1280]{1,0:T(8,128)(2,1)S(1)}, bf16[256,1280]{1,0:T(8,128)(2,1)S(1)}, u32[]{:S(2)}, u32[]{:S(2)}) %collective-permute-start.4) | collective-permute-done | bytes 655392 | tf_op jit(solution)/shard_map/ppermute | solution.py:317
  100.3 27.7 %collective-permute-done.3 = bf16[256,1280]{1,0:T(8,128)(2,1)S(1)} collective-permute-done((bf16[256,1280]{1,0:T(8,128)(2,1)S(1)}, bf16[256,1280]{1,0:T(8,128)(2,1)S(1)}, u32[]{:S(2)}, u32[]{:S(2)}) %collective-permute-start.3) | collective-permute-done | bytes 655392 | tf_op jit(solution)/shard_map/ppermute | solution.py:317
  130.4 3.2 collective-permute-done.7
  139.2 5.9 collective-permute-start.8
  147.3 3.1 slice.295
  152.3 3.7 pad_maximum_fusion
  158.2 15.3 %shard_map.101.refs_3_ = f32[2048,1280]{1,0:T(8,128)} custom-call(bf16[2048,2048]{1,0:T(8,128)(2,1)} %all-gather.6.cloned.1.call-done.refs_0_, bf16[1024,1280]{1,0:T(8,128)(2,1)S(1)} %copy-done.3, bf16[1024,1280]{1,0:T(8,128)(2,1)S(1)} %copy-done.4), custom_call_target="tpu_custom_call" | custom-call | flops 1 | bytes 1 | tf_op jit(solution)/shard_map/pallas_call | solution.py:155
  173.4 25.2 %collective-permute-done.10 = bf16[256,4096]{1,0:T(8,128)(2,1)} collective-permute-done((bf16[256,4096]{1,0:T(8,128)(2,1)}, bf16[256,4096]{1,0:T(8,128)(2,1)}, u32[]{:S(2)}, u32[]{:S(2)}) %collective-permute-start.10) | collective-permute-done | bytes 2097184 | tf_op jit(solution)/shard_map/ppermute | solution.py:314
  203.1 7.3 %collective-permute-start.12 = (bf16[1024,1280]{1,0:T(8,128)(2,1)}, bf16[1024,1280]{1,0:T(8,128)(2,1)}, u32[]{:S(2)}, u32[]{:S(2)}) collective-permute-start(bf16[1024,1280]{1,0:T(8,128)(2,1)} %pad_maximum_fusion.7.refs_2_), channel_id=1, source_target_pairs={{0,1},{3,2},{4,5},{7,6},{8,9},{11,10},{12,13},{15,14},{16,17},{19,... | collective-permute-start | bytes 7864328 | tf_op jit(solution)/shard_map/ppermute | solution.py:314
  214.2 45.3 %collective-permute-done.14 = bf16[256,4096]{1,0:T(8,128)(2,1)S(1)} collective-permute-done((bf16[256,4096]{1,0:T(8,128)(2,1)S(1)}, bf16[256,4096]{1,0:T(8,128)(2,1)S(1)}, u32[]{:S(2)}, u32[]{:S(2)}) %collective-permute-start.14) | collective-permute-done | bytes 2097184 | tf_op jit(solution)/shard_map/ppermute | solution.py:314
  259.6 3.4 collective-permute-done.12.refs_2_
  271.7 7.0 %collective-permute-start.16 = (bf16[1024,1024]{1,0:T(8,128)(2,1)S(1)}, bf16[1024,1024]{1,0:T(8,128)(2,1)}, u32[]{:S(2)}, u32[]{:S(2)}) collective-permute-start(bf16[1024,1024]{1,0:T(8,128)(2,1)S(1)} %bitcast.93), channel_id=1, source_target_pairs={{0,1},{3,2},{4,5},{7,6},{8,9},{11,10},{12,13},{15,14},{16,17},{19,... | collective-permute-start | bytes 6291464 | tf_op jit(solution)/shard_map/ppermute | solution.py:314
  280.7 18.4 %shard_map.102.refs_3_ = f32[2048,1280]{1,0:T(8,128)} custom-call(bf16[2048,2176]{1,0:T(8,128)(2,1)} %all-gather.10.cloned.1.call-done.refs_0_, bf16[1024,1280]{1,0:T(8,128)(2,1)} %collective-permute-done.8.refs_1_, bf16[1024,1280]{1,0:T(8,128)(2,1)} %collective-permute-done.12.refs_2_, f32[2048,1280]{1,0:T(8,128)} %shard_map.101.refs_3_), custom_call_target="tpu_custom_call", output_to_operand_aliasing={{}: (3, {})} | custom-call | flops 1 | bytes 1 | tf_op jit(solution)/shard_map/pallas_call | solution.py:155
  301.6 5.9 fusion.4
  309.2 16.8 %shard_map.103.refs_3_ = f32[2048,1280]{1,0:T(8,128)} custom-call(bf16[2048,2048]{1,0:T(8,128)(2,1)} %all-gather.8.cloned.1.call-done.refs_0_, bf16[1024,1280]{1,0:T(8,128)(2,1)S(1)} %copy-done.15, bf16[1024,1280]{1,0:T(8,128)(2,1)} %collective-permute-done.9.refs_2_, f32[2048,1280]{1,0:T(8,128)} %shard_map.102.refs_3_), custom_call_target="tpu_custom_call", output_to_operand_aliasing={{}: (3, {})} | custom-call | flops 1 | bytes 1 | tf_op jit(solution)/shard_map/pallas_call | solution.py:155
  331.6 6.0 shard_map.105
  343.2 3.2 constant_dynamic-slice_fusion.2
  346.4 10.3 %collective-permute-start.19 = (bf16[1024,1024]{1,0:T(8,128)(2,1)}, bf16[1024,1024]{1,0:T(8,128)(2,1)}, u32[]{:S(2)}, u32[]{:S(2)}) collective-permute-start(bf16[1024,1024]{1,0:T(8,128)(2,1)} %bitcast.15.second_ref), channel_id=1, source_target_pairs={{0,1},{3,2},{4,5},{7,6},{8,9},{11,10},{12,13},{15,14},{16,17},{19,... | collective-permute-start | bytes 6291464 | tf_op jit(solution)/shard_map/ppermute | solution.py:314
  356.6 2.7 slice.310
  359.3 14.4 %shard_map.104.refs_0_ = f32[2048,1024]{1,0:T(8,128)} custom-call(bf16[2048,2048]{1,0:T(8,128)(2,1)} %all-gather.12.cloned.1.call-done.refs_0_, bf16[1024,1280]{1,0:T(8,128)(2,1)S(1)} %copy-done.7, bf16[1024,1280]{1,0:T(8,128)(2,1)} %collective-permute-done.15.refs_2_, f32[2048,1280]{1,0:T(8,128)} %shard_map.103.refs_3_), custom_call_target="tpu_custom_call" | custom-call | flops 1 | bytes 1 | tf_op jit(solution)/shard_map/pallas_call | solution.py:155
  379.1 21.1 %shard_map.106.b_ref = bf16[1024,1024]{1,0:T(8,128)(2,1)} custom-call(s32[1]{0:T(128)} %bitcast.2.f_ref, f32[2048,1024]{1,0:T(8,128)} %shard_map.104.refs_0_, f32[1,1024]{1,0:T(1,128)S(1)} %bitcast.86, f32[2048,128]{1,0:T(8,128)S(1)} %get-tuple-element.279.refs_2_, f32[2048,128]{1,0:T(8,128)S(1)} %get-tuple-element.228.refs_3_, s32[2048,1]{1,0:T(8,128)S(1)} %copy-done.8, ...), custom_call_target="tpu_custom_call" | custom-call | flops 1 | bytes 1 | tf_op jit(solution)/shard_map/pallas_call | solution.py:113
  401.5 3.1 constant_dynamic-slice_fusion.1
  404.7 10.8 %collective-permute-start.23 = (bf16[1024,1024]{1,0:T(8,128)(2,1)}, bf16[1024,1024]{1,0:T(8,128)(2,1)}, u32[]{:S(2)}, u32[]{:S(2)}) collective-permute-start(bf16[1024,1024]{1,0:T(8,128)(2,1)} %bitcast.25.second_ref), channel_id=1, source_target_pairs={{0,1},{3,2},{4,5},{7,6},{8,9},{11,10},{12,13},{15,14},{16,17},{19,... | collective-permute-start | bytes 6291464 | tf_op jit(solution)/shard_map/ppermute | solution.py:314
  420.6 21.1 %shard_map.107.a_ref = bf16[1024,1024]{1,0:T(8,128)(2,1)} custom-call(s32[1]{0:T(128)} %bitcast.2.f_ref, f32[2048,1024]{1,0:T(8,128)} %shard_map.104.refs_0_, f32[1,1024]{1,0:T(1,128)S(1)} %bitcast.87, f32[2048,128]{1,0:T(8,128)S(1)} %get-tuple-element.279.refs_2_, f32[2048,128]{1,0:T(8,128)S(1)} %get-tuple-element.228.refs_3_, s32[2048,1]{1,0:T(8,128)S(1)} %copy-done.9, ...), custom_call_target="tpu_custom_call" | custom-call | flops 1 | bytes 1 | tf_op jit(solution)/shard_map/pallas_call | solution.py:113
  444.0 5.0 shard_map.108
  449.0 5.0 shard_map.109
  455.8 5.1 shard_map.111
  460.9 4.9 shard_map.110
  466.5 3.1 constant_dynamic-slice_fusion
  469.6 2.6 collective-permute-start.25
  473.6 3.0 add_convert_fusion.1
  482.0 5.5 shard_map.112
  487.5 5.0 shard_map.113
  492.5 4.9 shard_map.114
  497.4 19.6 %collective-permute-done.25.first_ref = bf16[1024,1024]{1,0:T(8,128)(2,1)} collective-permute-done((bf16[1024,1024]{1,0:T(8,128)(2,1)}, bf16[1024,1024]{1,0:T(8,128)(2,1)}, u32[]{:S(2)}, u32[]{:S(2)}) %collective-permute-start.25) | collective-permute-done | bytes 2097184 | tf_op jit(solution)/shard_map/ppermute | solution.py:314
  517.0 4.8 shard_map.115
  524.9 6.6 collective-permute-done.28.refs_1_
  531.5 2.4 add_convert_fusion
  542.6 4.3 shard_map.118.result_ref
  546.8 4.1 shard_map.119.result_ref
  552.7 5.0 shard_map.116
  557.7 5.0 shard_map.117
  562.9 18.9 %collective-permute-done.30.refs_2_ = bf16[4,256,1024]{2,1,0:T(8,128)(2,1)S(1)} collective-permute-done((bf16[4,256,1024]{2,1,0:T(8,128)(2,1)}, bf16[4,256,1024]{2,1,0:T(8,128)(2,1)S(1)}, u32[]{:S(2)}, u32[]{:S(2)}) %collective-permute-start.30) | collective-permute-done | bytes 2097184 | tf_op jit(solution)/shard_map/ppermute | solution.py:317
  582.0 4.0 collective-permute-done.32.refs_1_
  588.3 2.5 shard_map.122.result_ref
  590.8 2.5 shard_map.123.result_ref
  595.1 5.0 shard_map.120
  601.1 5.2 shard_map.121
  606.5 5.2 collective-permute-done.33.refs_2_
  611.7 4.2 collective-permute-done.34.refs_1_
  623.6 4.1 shard_map.124.result_ref
  627.6 4.1 shard_map.125.result_ref
  631.7 5.6 collective-permute-done.37.refs_3_
  637.4 2.5 shard_map.126.result_ref
  640.1 2.5 shard_map.127.result_ref
  642.6 5.2 collective-permute-done.36.refs_3_
  654.2 9.0 %collective-permute-done.38.refs_3_ = bf16[2,256,512]{2,1,0:T(8,128)(2,1)S(1)} collective-permute-done((bf16[2,256,512]{2,1,0:T(8,128)(2,1)S(1)}, bf16[2,256,512]{2,1,0:T(8,128)(2,1)S(1)}, u32[]{:S(2)}, u32[]{:S(2)}) %collective-permute-start.38) | collective-permute-done | bytes 524320 | tf_op jit(solution)/shard_map/ppermute | solution.py:314
  665.6 2.3 shard_map.131
  (248 shorter events, 132.0 us)
Async XLA Ops:
  6.5 149.5 %all-gather.6.cloned.1.call-start = ((), (), s32[]{:S(2)}) async-start(), calls=%async_computation | async-start | bytes 10485760 | tf_op jit(solution)/shard_map/all_gather | solution.py:363
  11.3 5.8 copy-start.16
  12.1 18.8 %collective-permute-start.1 = (bf16[256,1280]{1,0:T(8,128)(2,1)}, bf16[256,1280]{1,0:T(8,128)(2,1)}, u32[]{:S(2)}, u32[]{:S(2)}) collective-permute-start(bf16[256,1280]{1,0:T(8,128)(2,1)} %pad_maximum_fusion.19), channel_id=1, source_target_pairs={{0,8},{1,9},{2,10},{3,11},{4,12},{5,13},{6,14},{7,15},{8,0},{9,1},... | collective-permute-start | bytes 1966088 | tf_op jit(solution)/shard_map/ppermute | solution.py:317
  16.0 15.0 %collective-permute-start.2 = (bf16[256,1280]{1,0:T(8,128)(2,1)}, bf16[256,1280]{1,0:T(8,128)(2,1)}, u32[]{:S(2)}, u32[]{:S(2)}) collective-permute-start(bf16[256,1280]{1,0:T(8,128)(2,1)} %pad_maximum_fusion.20), channel_id=1, source_target_pairs={{0,4},{1,5},{2,6},{3,7},{4,0},{5,1},{6,2},{7,3},{8,12},{9,13},{10,... | collective-permute-start | bytes 1966088 | tf_op jit(solution)/shard_map/ppermute | solution.py:317
  16.9 26.5 %collective-permute-start = (bf16[256,1280]{1,0:T(8,128)(2,1)}, bf16[256,1280]{1,0:T(8,128)(2,1)}, u32[]{:S(2)}, u32[]{:S(2)}) collective-permute-start(bf16[256,1280]{1,0:T(8,128)(2,1)} %pad_maximum_fusion.18), channel_id=1, source_target_pairs={{0,12},{1,13},{2,14},{3,15},{4,8},{5,9},{6,10},{7,11},{8,4},{9,5},... | collective-permute-start | bytes 1966088 | tf_op jit(solution)/shard_map/ppermute | solution.py:317
  17.1 12.0 %copy-start.22 = (bf16[512,4096]{1,0:T(8,128)(2,1)S(1)}, bf16[512,4096]{1,0:T(8,128)(2,1)}, u32[]{:S(2)}) copy-start(bf16[512,4096]{1,0:T(8,128)(2,1)} %param.16) | copy-start | bytes 12582916
  24.0 34.5 %collective-permute-start.11 = (bf16[256,2048]{1,0:T(8,128)(2,1)S(1)}, bf16[256,2048]{1,0:T(8,128)(2,1)}, u32[]{:S(2)}, u32[]{:S(2)}) collective-permute-start(bf16[256,2048]{1,0:T(8,128)(2,1)S(1)} %slice.372), channel_id=1, source_target_pairs={{0,1},{3,2},{4,5},{7,6},{8,9},{11,10},{12,13},{15,14},{16,17},{19,... | collective-permute-start | bytes 3145736 | tf_op jit(solution)/shard_map/ppermute | solution.py:314
  62.0 218.7 %all-gather.10.cloned.1.call-start = ((), (), s32[]{:S(2)}) async-start(), calls=%async_computation.2 | async-start | bytes 11141120 | tf_op jit(solution)/shard_map/all_gather | solution.py:363
  63.9 2.8 slice-start.10
  63.9 2.8 slice-start.11
  64.2 69.4 %collective-permute-start.7 = (bf16[256,6272]{1,0:T(8,128)(2,1)S(1)}, bf16[256,6272]{1,0:T(8,128)(2,1)S(1)}, u32[]{:S(2)}, u32[]{:S(2)}) collective-permute-start(bf16[256,6272]{1,0:T(8,128)(2,1)S(1)} %pad_maximum_fusion.5), channel_id=1, source_target_pairs={{0,1},{3,2},{4,5},{7,6},{8,9},{11,10},{12,13},{15,14},{16,17},{19,... | collective-permute-start | bytes 9633800 | tf_op jit(solution)/shard_map/ppermute | solution.py:314
  65.8 64.6 %collective-permute-start.6 = (bf16[1024,1280]{1,0:T(8,128)(2,1)S(1)}, bf16[1024,1280]{1,0:T(8,128)(2,1)S(1)}, u32[]{:S(2)}, u32[]{:S(2)}) collective-permute-start(bf16[1024,1280]{1,0:T(8,128)(2,1)S(1)} %copy-done.2), channel_id=1, source_target_pairs={{2,1},{1,2},{6,5},{5,6},{10,9},{9,10},{14,13},{13,14},{18,17},{17,... | collective-permute-start | bytes 7864328 | tf_op jit(solution)/shard_map/ppermute | solution.py:314
  69.0 2.4 collective-permute-start.5
  69.1 31.2 %collective-permute-start.4 = (bf16[256,1280]{1,0:T(8,128)(2,1)S(1)}, bf16[256,1280]{1,0:T(8,128)(2,1)S(1)}, u32[]{:S(2)}, u32[]{:S(2)}) collective-permute-start(bf16[256,1280]{1,0:T(8,128)(2,1)S(1)} %pad_maximum_fusion.23), channel_id=1, source_target_pairs={{0,8},{1,9},{2,10},{3,11},{4,12},{5,13},{6,14},{7,15},{8,0},{9,1},... | collective-permute-start | bytes 1966088 | tf_op jit(solution)/shard_map/ppermute | solution.py:317
  70.6 57.5 %collective-permute-start.3 = (bf16[256,1280]{1,0:T(8,128)(2,1)S(1)}, bf16[256,1280]{1,0:T(8,128)(2,1)S(1)}, u32[]{:S(2)}, u32[]{:S(2)}) collective-permute-start(bf16[256,1280]{1,0:T(8,128)(2,1)S(1)} %pad_maximum_fusion.22), channel_id=1, source_target_pairs={{0,12},{1,13},{2,14},{3,15},{4,8},{5,9},{6,10},{7,11},{8,4},{9,5},... | collective-permute-start | bytes 1966088 | tf_op jit(solution)/shard_map/ppermute | solution.py:317
  130.4 3.3 copy-start.23
  130.4 3.6 copy-start.14
  136.7 2.5 copy-start.3
  138.3 169.2 %all-gather.8.cloned.1.call-start = ((), (), s32[]{:S(2)}) async-start(), calls=%async_computation.1 | async-start | bytes 10485760 | tf_op jit(solution)/shard_map/all_gather | solution.py:363
  139.2 59.4 %collective-permute-start.8 = (bf16[1024,1280]{1,0:T(8,128)(2,1)S(1)}, bf16[1024,1280]{1,0:T(8,128)(2,1)}, u32[]{:S(2)}, u32[]{:S(2)}) collective-permute-start(bf16[1024,1280]{1,0:T(8,128)(2,1)S(1)} %copy-done.3), channel_id=1, source_target_pairs={{0,1},{3,2},{4,5},{7,6},{8,9},{11,10},{12,13},{15,14},{16,17},{19,... | collective-permute-start | bytes 7864328 | tf_op jit(solution)/shard_map/ppermute | solution.py:314
  145.1 53.6 %collective-permute-start.9 = (bf16[1024,1280]{1,0:T(8,128)(2,1)}, bf16[1024,1280]{1,0:T(8,128)(2,1)}, u32[]{:S(2)}, u32[]{:S(2)}) collective-permute-start(bf16[1024,1280]{1,0:T(8,128)(2,1)} %pad_maximum_fusion.7.refs_2_), channel_id=1, source_target_pairs={{2,1},{1,2},{6,5},{5,6},{10,9},{9,10},{14,13},{13,14},{18,17},{17,... | collective-permute-start | bytes 7864328 | tf_op jit(solution)/shard_map/ppermute | solution.py:314
  150.4 48.2 %collective-permute-start.10 = (bf16[256,4096]{1,0:T(8,128)(2,1)}, bf16[256,4096]{1,0:T(8,128)(2,1)}, u32[]{:S(2)}, u32[]{:S(2)}) collective-permute-start(bf16[256,4096]{1,0:T(8,128)(2,1)} %slice.295), channel_id=1, source_target_pairs={{1,0},{2,3},{5,4},{6,7},{9,8},{10,11},{13,12},{14,15},{17,16},{18,... | collective-permute-start | bytes 6291464 | tf_op jit(solution)/shard_map/ppermute | solution.py:314
  156.0 2.2 copy-start.4
  198.7 2.2 slice-start.6
  203.1 126.8 %all-gather.12.cloned.1.call-start = ((), (), s32[]{:S(2)}) async-start(), calls=%async_computation.3 | async-start | bytes 10485760 | tf_op jit(solution)/shard_map/all_gather | solution.py:363
  203.1 59.9 %collective-permute-start.12 = (bf16[1024,1280]{1,0:T(8,128)(2,1)}, bf16[1024,1280]{1,0:T(8,128)(2,1)}, u32[]{:S(2)}, u32[]{:S(2)}) collective-permute-start(bf16[1024,1280]{1,0:T(8,128)(2,1)} %pad_maximum_fusion.7.refs_2_), channel_id=1, source_target_pairs={{0,1},{3,2},{4,5},{7,6},{8,9},{11,10},{12,13},{15,14},{16,17},{19,... | collective-permute-start | bytes 7864328 | tf_op jit(solution)/shard_map/ppermute | solution.py:314
  210.4 52.6 %collective-permute-start.13 = (bf16[1024,1280]{1,0:T(8,128)(2,1)}, bf16[1024,1280]{1,0:T(8,128)(2,1)S(1)}, u32[]{:S(2)}, u32[]{:S(2)}) collective-permute-start(bf16[1024,1280]{1,0:T(8,128)(2,1)} %collective-permute-done.8.refs_1_), channel_id=1, source_target_pairs={{2,1},{1,2},{6,5},{5,6},{10,9},{9,10},{14,13},{13,14},{18,17},{17,... | collective-permute-start | bytes 7864328 | tf_op jit(solution)/shard_map/ppermute | solution.py:314
  212.9 46.6 %collective-permute-start.14 = (bf16[256,4096]{1,0:T(8,128)(2,1)S(1)}, bf16[256,4096]{1,0:T(8,128)(2,1)S(1)}, u32[]{:S(2)}, u32[]{:S(2)}) collective-permute-start(bf16[256,4096]{1,0:T(8,128)(2,1)S(1)} %slice.304), channel_id=1, source_target_pairs={{1,0},{2,3},{5,4},{6,7},{9,8},{10,11},{13,12},{14,15},{17,16},{18,... | collective-permute-start | bytes 6291464 | tf_op jit(solution)/shard_map/ppermute | solution.py:314
  263.0 2.5 slice-start.7
  267.8 58.3 %collective-permute-start.15 = (bf16[1024,1280]{1,0:T(8,128)(2,1)}, bf16[1024,1280]{1,0:T(8,128)(2,1)}, u32[]{:S(2)}, u32[]{:S(2)}) collective-permute-start(bf16[1024,1280]{1,0:T(8,128)(2,1)} %collective-permute-done.12.refs_2_), channel_id=1, source_target_pairs={{2,1},{1,2},{6,5},{5,6},{10,9},{9,10},{14,13},{13,14},{18,17},{17,... | collective-permute-start | bytes 7864328 | tf_op jit(solution)/shard_map/ppermute | solution.py:314
  271.7 27.4 %copy-start.25 = (bf16[4,1,256,1024]{3,2,1,0:T(8,128)(2,1)}, bf16[4,1,256,1024]{3,2,1,0:T(8,128)(2,1)S(1)}, u32[]{:S(2)}) copy-start(bf16[4,1,256,1024]{3,2,1,0:T(8,128)(2,1)S(1)} %constant_dynamic-slice_fusion.3) | copy-start | bytes 6291460
  271.7 54.4 %collective-permute-start.16 = (bf16[1024,1024]{1,0:T(8,128)(2,1)S(1)}, bf16[1024,1024]{1,0:T(8,128)(2,1)}, u32[]{:S(2)}, u32[]{:S(2)}) collective-permute-start(bf16[1024,1024]{1,0:T(8,128)(2,1)S(1)} %bitcast.93), channel_id=1, source_target_pairs={{0,1},{3,2},{4,5},{7,6},{8,9},{11,10},{12,13},{15,14},{16,17},{19,... | collective-permute-start | bytes 6291464 | tf_op jit(solution)/shard_map/ppermute | solution.py:314
  328.0 13.6 %collective-permute-start.17 = (bf16[256,1024]{1,0:T(8,128)(2,1)}, bf16[256,1024]{1,0:T(8,128)(2,1)}, u32[]{:S(2)}, u32[]{:S(2)}) collective-permute-start(bf16[256,1024]{1,0:T(8,128)(2,1)} %slice.322), channel_id=1, source_target_pairs={{2,1},{1,2},{6,5},{5,6},{10,9},{9,10},{14,13},{13,14},{18,17},{17,... | collective-permute-start | bytes 1572872 | tf_op jit(solution)/shard_map/ppermute | solution.py:314
  341.6 32.1 %collective-permute-start.18 = (bf16[4,512,256]{2,1,0:T(8,128)(2,1)}, bf16[4,512,256]{2,1,0:T(8,128)(2,1)}, u32[]{:S(2)}, u32[]{:S(2)}) collective-permute-start(bf16[4,512,256]{2,1,0:T(8,128)(2,1)} %pad_maximum_fusion.17), channel_id=1, source_target_pairs={{1,2},{5,6},{9,10},{13,14},{17,18},{21,22},{25,26},{29,30}} | collective-permute-start | bytes 3145736 | tf_op jit(solution)/shard_map/ppermute | solution.py:314
  346.4 13.0 %copy-start.7 = (bf16[1024,1280]{1,0:T(8,128)(2,1)S(1)}, bf16[1024,1280]{1,0:T(8,128)(2,1)}, u32[]{:S(2)}) copy-start(bf16[1024,1280]{1,0:T(8,128)(2,1)} %copy-done.5) | copy-start | bytes 7864324
  346.4 53.9 %collective-permute-start.19 = (bf16[1024,1024]{1,0:T(8,128)(2,1)}, bf16[1024,1024]{1,0:T(8,128)(2,1)}, u32[]{:S(2)}, u32[]{:S(2)}) collective-permute-start(bf16[1024,1024]{1,0:T(8,128)(2,1)} %bitcast.15.second_ref), channel_id=1, source_target_pairs={{0,1},{3,2},{4,5},{7,6},{8,9},{11,10},{12,13},{15,14},{16,17},{19,... | collective-permute-start | bytes 6291464 | tf_op jit(solution)/shard_map/ppermute | solution.py:314
  373.7 26.5 %collective-permute-start.20 = (bf16[768,1024]{1,0:T(8,128)(2,1)}, bf16[768,1024]{1,0:T(8,128)(2,1)}, u32[]{:S(2)}, u32[]{:S(2)}) collective-permute-start(bf16[768,1024]{1,0:T(8,128)(2,1)} %slice.310), channel_id=1, source_target_pairs={{2,1},{1,2},{6,5},{5,6},{10,9},{9,10},{14,13},{13,14},{18,17},{17,... | collective-permute-start | bytes 4718600 | tf_op jit(solution)/shard_map/ppermute | solution.py:314
  400.2 53.7 %collective-permute-start.21 = (bf16[1024,1024]{1,0:T(8,128)(2,1)}, bf16[1024,1024]{1,0:T(8,128)(2,1)}, u32[]{:S(2)}, u32[]{:S(2)}) collective-permute-start(bf16[1024,1024]{1,0:T(8,128)(2,1)} %shard_map.106.b_ref), channel_id=1, source_target_pairs={{1,0},{2,3},{5,4},{6,7},{9,8},{10,11},{13,12},{14,15},{17,16},{18,... | collective-permute-start | bytes 6291464 | tf_op jit(solution)/shard_map/ppermute | solution.py:314
  404.7 61.7 %collective-permute-start.23 = (bf16[1024,1024]{1,0:T(8,128)(2,1)}, bf16[1024,1024]{1,0:T(8,128)(2,1)}, u32[]{:S(2)}, u32[]{:S(2)}) collective-permute-start(bf16[1024,1024]{1,0:T(8,128)(2,1)} %bitcast.25.second_ref), channel_id=1, source_target_pairs={{0,1},{3,2},{4,5},{7,6},{8,9},{11,10},{12,13},{15,14},{16,17},{19,... | collective-permute-start | bytes 6291464 | tf_op jit(solution)/shard_map/ppermute | solution.py:314
  415.5 50.9 %collective-permute-start.22 = (bf16[1024,1024]{1,0:T(8,128)(2,1)}, bf16[1024,1024]{1,0:T(8,128)(2,1)}, u32[]{:S(2)}, u32[]{:S(2)}) collective-permute-start(bf16[1024,1024]{1,0:T(8,128)(2,1)} %collective-permute-done.19.first_ref), channel_id=1, source_target_pairs={{2,1},{1,2},{6,5},{5,6},{10,9},{9,10},{14,13},{13,14},{18,17},{17,... | collective-permute-start | bytes 6291464 | tf_op jit(solution)/shard_map/ppermute | solution.py:314
  441.7 2.2 copy-start
  466.4 7.2 %collective-permute-start.24 = (bf16[4,512,1024]{2,1,0:T(8,128)(2,1)S(1)}, bf16[4,512,1024]{2,1,0:T(8,128)(2,1)S(1)}, u32[]{:S(2)}, u32[]{:S(2)}) collective-permute-start(bf16[4,512,1024]{2,1,0:T(8,128)(2,1)S(1)} %pad_maximum_fusion.2), channel_id=1, source_target_pairs={{0,4},{1,5},{2,6},{3,7},{4,0},{5,1},{6,2},{7,3},{8,12},{9,13},{10,... | collective-permute-start | bytes 12582920 | tf_op jit(solution)/shard_map/ppermute | solution.py:317
  469.6 47.4 %collective-permute-start.25 = (bf16[1024,1024]{1,0:T(8,128)(2,1)}, bf16[1024,1024]{1,0:T(8,128)(2,1)}, u32[]{:S(2)}, u32[]{:S(2)}) collective-permute-start(bf16[1024,1024]{1,0:T(8,128)(2,1)} %bitcast.29.second_ref), channel_id=1, source_target_pairs={{0,1},{3,2},{4,5},{7,6},{8,9},{11,10},{12,13},{15,14},{16,17},{19,... | collective-permute-start | bytes 6291464 | tf_op jit(solution)/shard_map/ppermute | solution.py:314
  472.7 3.9 copy-start.19
  473.6 8.4 %copy-start.21 = (bf16[4,512,1024]{2,1,0:T(8,128)(2,1)}, bf16[4,512,1024]{2,1,0:T(8,128)(2,1)S(1)}, u32[]{:S(2)}) copy-start(bf16[4,512,1024]{2,1,0:T(8,128)(2,1)S(1)} %collective-permute-done.24.refs_1_) | copy-start | bytes 12582916
  476.6 47.8 %collective-permute-start.27 = (bf16[4,256,1024]{2,1,0:T(8,128)(2,1)}, bf16[4,256,1024]{2,1,0:T(8,128)(2,1)S(1)}, u32[]{:S(2)}, u32[]{:S(2)}) collective-permute-start(bf16[4,256,1024]{2,1,0:T(8,128)(2,1)} %add_convert_fusion.1), channel_id=1, source_target_pairs={{0,8},{1,9},{2,10},{3,11},{4,12},{5,13},{6,14},{7,15},{8,0},{9,1},... | collective-permute-start | bytes 6291464 | tf_op jit(solution)/shard_map/ppermute | solution.py:317
  478.3 46.0 %collective-permute-start.26 = (bf16[1024,1024]{1,0:T(8,128)(2,1)}, bf16[1024,1024]{1,0:T(8,128)(2,1)}, u32[]{:S(2)}, u32[]{:S(2)}) collective-permute-start(bf16[1024,1024]{1,0:T(8,128)(2,1)} %collective-permute-done.23.first_ref), channel_id=1, source_target_pairs={{2,1},{1,2},{6,5},{5,6},{10,9},{9,10},{14,13},{13,14},{18,17},{17,... | collective-permute-start | bytes 6291464 | tf_op jit(solution)/shard_map/ppermute | solution.py:314
  524.4 7.2 %collective-permute-start.28 = (bf16[4,512,1024]{2,1,0:T(8,128)(2,1)S(1)}, bf16[4,512,1024]{2,1,0:T(8,128)(2,1)S(1)}, u32[]{:S(2)}, u32[]{:S(2)}) collective-permute-start(bf16[4,512,1024]{2,1,0:T(8,128)(2,1)S(1)} %pad_maximum_fusion.4), channel_id=1, source_target_pairs={{0,4},{1,5},{2,6},{3,7},{4,0},{5,1},{6,2},{7,3},{8,12},{9,13},{10,... | collective-permute-start | bytes 12582920 | tf_op jit(solution)/shard_map/ppermute | solution.py:317
  524.9 9.0 %copy-start.18 = (bf16[4,512,1024]{2,1,0:T(8,128)(2,1)}, bf16[4,512,1024]{2,1,0:T(8,128)(2,1)S(1)}, u32[]{:S(2)}) copy-start(bf16[4,512,1024]{2,1,0:T(8,128)(2,1)S(1)} %pad_maximum_fusion.3.refs_0_) | copy-start | bytes 12582916
  531.5 7.7 %copy-start.20 = (bf16[4,512,1024]{2,1,0:T(8,128)(2,1)}, bf16[4,512,1024]{2,1,0:T(8,128)(2,1)S(1)}, u32[]{:S(2)}) copy-start(bf16[4,512,1024]{2,1,0:T(8,128)(2,1)S(1)} %collective-permute-done.28.refs_1_) | copy-start | bytes 12582916
  531.5 9.0 %copy-start.17 = (bf16[256,8192]{1,0:T(8,128)(2,1)S(1)}, bf16[256,8192]{1,0:T(8,128)(2,1)}, u32[]{:S(2)}) copy-start(bf16[256,8192]{1,0:T(8,128)(2,1)} %hidden_ref.25) | copy-start | bytes 12582916
  534.0 47.9 %collective-permute-start.30 = (bf16[4,256,1024]{2,1,0:T(8,128)(2,1)}, bf16[4,256,1024]{2,1,0:T(8,128)(2,1)S(1)}, u32[]{:S(2)}, u32[]{:S(2)}) collective-permute-start(bf16[4,256,1024]{2,1,0:T(8,128)(2,1)} %add_convert_fusion), channel_id=1, source_target_pairs={{0,8},{1,9},{2,10},{3,11},{4,12},{5,13},{6,14},{7,15},{8,0},{9,1},... | collective-permute-start | bytes 6291464 | tf_op jit(solution)/shard_map/ppermute | solution.py:317
  535.7 46.1 %collective-permute-start.29 = (bf16[1024,1024]{1,0:T(8,128)(2,1)}, bf16[1024,1024]{1,0:T(8,128)(2,1)}, u32[]{:S(2)}, u32[]{:S(2)}) collective-permute-start(bf16[1024,1024]{1,0:T(8,128)(2,1)} %collective-permute-done.25.first_ref), channel_id=1, source_target_pairs={{2,1},{1,2},{6,5},{5,6},{10,9},{9,10},{14,13},{13,14},{18,17},{17,... | collective-permute-start | bytes 6291464 | tf_op jit(solution)/shard_map/ppermute | solution.py:314
  539.2 23.7 %collective-permute-start.31 = (bf16[2,256,512]{2,1,0:T(8,128)(2,1)S(1)}, bf16[2,256,512]{2,1,0:T(8,128)(2,1)S(1)}, u32[]{:S(2)}, u32[]{:S(2)}) collective-permute-start(bf16[2,256,512]{2,1,0:T(8,128)(2,1)S(1)} %pad_maximum_fusion.26), channel_id=1, source_target_pairs={{1,0},{2,3},{5,4},{6,7},{9,8},{10,11},{13,12},{14,15},{17,16},{18,... | collective-permute-start | bytes 1572872 | tf_op jit(solution)/shard_map/ppermute | solution.py:314
  581.8 4.2 collective-permute-start.32
  586.4 25.3 %collective-permute-start.33 = (bf16[2,256,1024]{2,1,0:T(8,128)(2,1)S(1)}, bf16[2,256,1024]{2,1,0:T(8,128)(2,1)S(1)}, u32[]{:S(2)}, u32[]{:S(2)}) collective-permute-start(bf16[2,256,1024]{2,1,0:T(8,128)(2,1)S(1)} %add_convert_fusion.3), channel_id=1, source_target_pairs={{0,8},{1,9},{2,10},{3,11},{4,12},{5,13},{6,14},{7,15},{8,0},{9,1},... | collective-permute-start | bytes 3145736 | tf_op jit(solution)/shard_map/ppermute | solution.py:317
  606.3 9.6 %copy-start.13 = (bf16[512,1024]{1,0:T(8,128)(2,1)S(1)}, bf16[512,1024]{1,0:T(8,128)(2,1)}, u32[]{:S(2)}) copy-start(bf16[512,1024]{1,0:T(8,128)(2,1)} %copy-done.12) | copy-start | bytes 3145732
  611.7 10.1 %copy-start.10 = (bf16[2,256,1024]{2,1,0:T(8,128)(2,1)}, bf16[2,256,1024]{2,1,0:T(8,128)(2,1)S(1)}, u32[]{:S(2)}) copy-start(bf16[2,256,1024]{2,1,0:T(8,128)(2,1)S(1)} %collective-permute-done.33.refs_2_) | copy-start | bytes 3145732
  611.7 4.2 collective-permute-start.34
  617.2 30.6 %collective-permute-start.35 = (bf16[2,256,1024]{2,1,0:T(8,128)(2,1)}, bf16[2,256,1024]{2,1,0:T(8,128)(2,1)S(1)}, u32[]{:S(2)}, u32[]{:S(2)}) collective-permute-start(bf16[2,256,1024]{2,1,0:T(8,128)(2,1)} %add_convert_fusion.2), channel_id=1, source_target_pairs={{0,8},{1,9},{2,10},{3,11},{4,12},{5,13},{6,14},{7,15},{8,0},{9,1},... | collective-permute-start | bytes 3145736 | tf_op jit(solution)/shard_map/ppermute | solution.py:317
  620.5 16.9 %collective-permute-start.37 = (bf16[2,256,512]{2,1,0:T(8,128)(2,1)S(1)}, bf16[2,256,512]{2,1,0:T(8,128)(2,1)S(1)}, u32[]{:S(2)}, u32[]{:S(2)}) collective-permute-start(bf16[2,256,512]{2,1,0:T(8,128)(2,1)S(1)} %pad_maximum_fusion.28), channel_id=1, source_target_pairs={{1,0},{2,3},{5,4},{6,7},{9,8},{10,11},{13,12},{14,15},{17,16},{18,... | collective-permute-start | bytes 1572872 | tf_op jit(solution)/shard_map/ppermute | solution.py:314
  622.2 25.6 %collective-permute-start.36 = (bf16[2,256,512]{2,1,0:T(8,128)(2,1)S(1)}, bf16[2,256,512]{2,1,0:T(8,128)(2,1)S(1)}, u32[]{:S(2)}, u32[]{:S(2)}) collective-permute-start(bf16[2,256,512]{2,1,0:T(8,128)(2,1)S(1)} %pad_maximum_fusion.27), channel_id=1, source_target_pairs={{1,0},{2,3},{5,4},{6,7},{9,8},{10,11},{13,12},{14,15},{17,16},{18,... | collective-permute-start | bytes 1572872 | tf_op jit(solution)/shard_map/ppermute | solution.py:314
  642.6 6.9 %copy-start.11 = (bf16[2,256,1024]{2,1,0:T(8,128)(2,1)S(1)}, bf16[2,256,1024]{2,1,0:T(8,128)(2,1)}, u32[]{:S(2)}) copy-start(bf16[2,256,1024]{2,1,0:T(8,128)(2,1)} %copy-done.10) | copy-start | bytes 3145732
  648.2 15.0 %collective-permute-start.38 = (bf16[2,256,512]{2,1,0:T(8,128)(2,1)S(1)}, bf16[2,256,512]{2,1,0:T(8,128)(2,1)S(1)}, u32[]{:S(2)}, u32[]{:S(2)}) collective-permute-start(bf16[2,256,512]{2,1,0:T(8,128)(2,1)S(1)} %pad_maximum_fusion.29), channel_id=1, source_target_pairs={{1,0},{2,3},{5,4},{6,7},{9,8},{10,11},{13,12},{14,15},{17,16},{18,... | collective-permute-start | bytes 1572872 | tf_op jit(solution)/shard_map/ppermute | solution.py:314
  (21 other events, 34.4 us)
Sparse Core Ops, SparseCore 0:
  62.1 84.4 all-gather.5
  148.1 60.8 all-gather.9
  210.6 58.2 all-gather.7
  270.3 58.2 all-gather.11

commit v5 on v4

--- a/solution.py
+++ b/solution.py
@@ -75,31 +75,39 @@
     return jnp.concatenate([cosine, cosine], -1), jnp.concatenate([-sine, sine], -1)
 
 
-def attention_kernel(heads, scale, q_ref, bias_ref, cos_ref, sin_ref, start_ref, row_ref,
+def attention_kernel(heads, scale, n_keys, q_ref, bias_ref, cos_ref, sin_ref, start_ref, row_ref,
                      col_ref, k_ref, v_ref, out_ref):
     cosine, sine = cos_ref[...], sin_ref[...]
-    columns = col_ref[...]
+    columns = col_ref[:, :n_keys]
     allowed = (columns >= start_ref[...]) & (columns <= row_ref[...])
-    keys, values = k_ref[0], v_ref[0]
-    for head in range(heads):
-        span = slice(head * HEAD, (head + 1) * HEAD)
-        query = q_ref[:, span] + bias_ref[:, span]
-        query = query * cosine + pltpu.roll(query, HEAD // 2, 1) * sine
+    keys, values = k_ref[0, :n_keys], v_ref[0, :n_keys]
+    rows, together = out_ref.shape[0], min(4, heads)
+    for first in range(0, heads, together):
+        spans = [slice(h * HEAD, (h + 1) * HEAD) for h in range(first, first + together)]
+        queries = []
+        for span in spans:
+            query = q_ref[:, span] + bias_ref[:, span]
+            query = query * cosine + pltpu.roll(query, HEAD // 2, 1) * sine
+            queries.append(query.astype(jnp.bfloat16))
         scores = lax.dot_general(
-            query.astype(jnp.bfloat16), keys, (((1,), (1,)), ((), ())),
+            jnp.concatenate(queries, axis=0), keys, (((1,), (1,)), ((), ())),
             preferred_element_type=jnp.float32,
         )
-        scores = jnp.where(allowed, scores, MASKED)
-        highest = jnp.max(scores, axis=-1, keepdims=True)
-        weights = jnp.exp2((scores - highest) * (scale * LOG2E))
-        share = 1.0 / jnp.sum(weights, axis=-1, keepdims=True)
-        probs = (weights * share).astype(jnp.bfloat16)
-        mixed = jnp.dot(probs, values, preferred_element_type=jnp.float32)
-        out_ref[:, span] = mixed.astype(jnp.bfloat16)
+        probs = []
+        for i in range(together):
+            score = jnp.where(allowed, scores[i * rows:(i + 1) * rows], MASKED)
+            highest = jnp.max(score, axis=-1, keepdims=True)
+            weights = jnp.exp2((score - highest) * (scale * LOG2E))
+            share = 1.0 / jnp.sum(weights, axis=-1, keepdims=True)
+            probs.append((weights * share).astype(jnp.bfloat16))
+        mixed = jnp.dot(
+            jnp.concatenate(probs, axis=0), values, preferred_element_type=jnp.float32)
+        for i, span in enumerate(spans):
+            out_ref[:, span] = mixed[i * rows:(i + 1) * rows].astype(jnp.bfloat16)
 
 
 def attention(part, *, rows, groups, width, f, projected, bias, cosine, sine, starts, row_ids,
-              columns, key_value):
+              columns, key_value, near, limit):
     n_keys = key_value.shape[1]
     mine = lambda g, f_ref: (2 * g + part, 0)
 
@@ -107,8 +115,13 @@
         d = g ^ f_ref[0]
         return (d // 2 + (d % 2) * (groups // 2), 0)
 
+    far = starts.reshape(groups, 2, rows)[:, part, 0] < limit
+
     def kernel(f_ref, *refs):
-        attention_kernel(width // HEAD, HEAD ** -0.5, *refs)
+        is_far = f_ref[1 + pl.program_id(0)] == 1
+        for taken, count in ((is_far, n_keys), (jnp.logical_not(is_far), near)):
+            pl.when(taken)(functools.partial(
+                attention_kernel, width // HEAD, HEAD ** -0.5, count, *refs))
 
     return pl.pallas_call(
         kernel,
@@ -131,7 +144,7 @@
         out_shape=jax.ShapeDtypeStruct((groups * rows, width), jnp.bfloat16),
         compiler_params=ROOM,
         cost_estimate=LIGHT,
-    )(jnp.full((1,), f, jnp.int32), projected, bias, cosine, sine, starts, row_ids, columns,
+    )(jnp.concatenate([jnp.full((1,), f, jnp.int32), far.astype(jnp.int32)]), projected, bias, cosine, sine, starts, row_ids, columns,
       key_value, key_value)
 
 
@@ -513,6 +526,8 @@
             bias=lax.dynamic_slice_in_dim(query_bias, f * q_cols, q_cols)[None],
             cosine=cosine, sine=sine, starts=starts[:, None], row_ids=row_ids[:, None],
             columns=jnp.concatenate(columns)[None], key_value=jnp.concatenate(blocks, axis=1),
+            near=reach * rows,
+            limit=((my_outer if outer_rows else my_inner) - reach + 1) * rows,
         )
 
     wide = lambda value: value.astype(jnp.float32)

time: 685 us -> 682 us (level)
  Pallas kernels: 214 us -> 205 us
    pallas_call x2, Pallas kernels: 42.2 us -> 33.2 us  [attention(): pl.pallas_call(kernel, grid_spec=pltpu.PrefetchScalarGridSpec(num_scalar_...]
    unnamed x64 -> x62, local copies, waits for them, and re-layouts: 18.7 us -> 18.6 us
  transfers between devices with their start and end apart: 43 -> 43, of which waited for: 20 -> 21; matrix products, arithmetic and copies ran while one was open for 12% -> 12% of each run, Pallas kernels for 31% -> 30%
where the time goes in v5:
time: 682 us; the launch traced here: 672 us
  waiting for transfers between devices  231 us (34%)
  Pallas kernels  205 us (30%)
  starting transfers between devices  92.9 us (14%)
  local copies, waits for them, and re-layouts  60.5 us (9%)
  other arithmetic  57.4 us (8%)
  between operations  14.5 us (2%)
  blocking collectives  11.2 us (2%)
    ppermute x25, waiting for transfers between devices, send(): return lax.ppermute(value, 'tp', pairs)  118 us
    ppermute x14, waiting for transfers between devices, swap(): lax.ppermute(value, LEVEL, [(i * n_t + z, (i ^ d) * n_t + z) for i in ran...  113 us
    ppermute x25, starting transfers between devices, send(): return lax.ppermute(value, 'tp', pairs)  80.5 us
    pallas_call x5, Pallas kernels, project(): pl.pallas_call(kernel, grid=(n_rows // block,), in_specs=[pl.BlockSpec((b...  70.3 us
    pallas_call x8, Pallas kernels, partials_of_two(): pl.pallas_call(kernel, grid=(4,), in_specs=[rows, rows, pl.BlockSpec((wid...  40.5 us
    pallas_call x12, Pallas kernels, add_up(): pl.pallas_call(kernel, grid_spec=pltpu.PrefetchScalarGridSpec(num_scalar_...  36 us
    pallas_call x2, Pallas kernels, attention(): pl.pallas_call(kernel, grid_spec=pltpu.PrefetchScalarGridSpec(num_scalar_...  33.2 us
    pallas_call x4, Pallas kernels, partials_of_one(): pl.pallas_call(kernel, grid_spec=pltpu.PrefetchScalarGridSpec(num_scalar_...  19.9 us
  transfers between devices with their start and end apart: 43, of which 21 were waited for; matrix products, arithmetic and copies ran while one was open for 12% of the time, Pallas kernels for 30%

profile of v5, /device:TPU:0, one launch (start us, length us, event | category | flops | bytes accessed | tf_op | source)
XLA Modules:
  0.0 672.4 jit_solution(11267557401252365456)
XLA Ops:
  12.1 2.9 collective-permute-start.1
  17.1 4.8 shard_map.100
  24.1 5.0 collective-permute-start.11
  31.0 12.5 %collective-permute-done = bf16[256,1280]{1,0:T(8,128)(2,1)} collective-permute-done((bf16[256,1280]{1,0:T(8,128)(2,1)}, bf16[256,1280]{1,0:T(8,128)(2,1)}, u32[]{:S(2)}, u32[]{:S(2)}) %collective-permute-start) | collective-permute-done | bytes 655392 | tf_op jit(solution)/shard_map/ppermute | solution.py:330
  47.4 11.2 %all-gather = s32[4,1,256]{2,1,0:T(1,128)S(1)} all-gather(s32[1,1,256]{2,1,0:T(1,128)S(1)} %bitcast.97), channel_id=1, replica_groups=mesh['groups'=2,'fsdp'=4,'tp'=4] {'tp'}, dimensions={0}, use_global_device_ids=true | all-gather | bytes 5120 | tf_op jit(solution)/shard_map/all_gather | solution.py:392
  58.6 3.4 maximum_select_fusion.1
  71.4 28.9 %collective-permute-done.4 = bf16[256,1280]{1,0:T(8,128)(2,1)S(1)} collective-permute-done((bf16[256,1280]{1,0:T(8,128)(2,1)S(1)}, bf16[256,1280]{1,0:T(8,128)(2,1)S(1)}, u32[]{:S(2)}, u32[]{:S(2)}) %collective-permute-start.4) | collective-permute-done | bytes 655392 | tf_op jit(solution)/shard_map/ppermute | solution.py:330
  100.4 27.7 %collective-permute-done.3 = bf16[256,1280]{1,0:T(8,128)(2,1)S(1)} collective-permute-done((bf16[256,1280]{1,0:T(8,128)(2,1)S(1)}, bf16[256,1280]{1,0:T(8,128)(2,1)S(1)}, u32[]{:S(2)}, u32[]{:S(2)}) %collective-permute-start.3) | collective-permute-done | bytes 655392 | tf_op jit(solution)/shard_map/ppermute | solution.py:330
  130.5 3.1 collective-permute-done.7
  139.3 5.9 collective-permute-start.8
  147.3 3.1 slice.311
  152.3 3.6 pad_maximum_fusion
  158.1 15.2 %shard_map.101.refs_3_ = f32[2048,1280]{1,0:T(8,128)} custom-call(bf16[2048,2048]{1,0:T(8,128)(2,1)} %all-gather.8.cloned.1.call-done.refs_0_, bf16[1024,1280]{1,0:T(8,128)(2,1)S(1)} %copy-done.3, bf16[1024,1280]{1,0:T(8,128)(2,1)S(1)} %copy-done.4), custom_call_target="tpu_custom_call" | custom-call | flops 1 | bytes 1 | tf_op jit(solution)/shard_map/pallas_call | solution.py:168
  173.3 25.3 %collective-permute-done.10 = bf16[256,4096]{1,0:T(8,128)(2,1)} collective-permute-done((bf16[256,4096]{1,0:T(8,128)(2,1)}, bf16[256,4096]{1,0:T(8,128)(2,1)}, u32[]{:S(2)}, u32[]{:S(2)}) %collective-permute-start.10) | collective-permute-done | bytes 2097184 | tf_op jit(solution)/shard_map/ppermute | solution.py:327
  203.1 7.3 %collective-permute-start.12 = (bf16[1024,1280]{1,0:T(8,128)(2,1)}, bf16[1024,1280]{1,0:T(8,128)(2,1)}, u32[]{:S(2)}, u32[]{:S(2)}) collective-permute-start(bf16[1024,1280]{1,0:T(8,128)(2,1)} %pad_maximum_fusion.7.refs_2_), channel_id=1, source_target_pairs={{0,1},{3,2},{4,5},{7,6},{8,9},{11,10},{12,13},{15,14},{16,17},{19,... | collective-permute-start | bytes 7864328 | tf_op jit(solution)/shard_map/ppermute | solution.py:327
  214.3 45.3 %collective-permute-done.14 = bf16[256,4096]{1,0:T(8,128)(2,1)S(1)} collective-permute-done((bf16[256,4096]{1,0:T(8,128)(2,1)S(1)}, bf16[256,4096]{1,0:T(8,128)(2,1)S(1)}, u32[]{:S(2)}, u32[]{:S(2)}) %collective-permute-start.14) | collective-permute-done | bytes 2097184 | tf_op jit(solution)/shard_map/ppermute | solution.py:327
  259.6 3.4 collective-permute-done.12.refs_2_
  270.1 3.1 constant_dynamic-slice_fusion.3
  273.1 6.9 %collective-permute-start.16 = (bf16[1024,1024]{1,0:T(8,128)(2,1)}, bf16[1024,1024]{1,0:T(8,128)(2,1)}, u32[]{:S(2)}, u32[]{:S(2)}) collective-permute-start(bf16[1024,1024]{1,0:T(8,128)(2,1)} %bitcast.10.second_ref), channel_id=1, source_target_pairs={{0,1},{3,2},{4,5},{7,6},{8,9},{11,10},{12,13},{15,14},{16,17},{19,... | collective-permute-start | bytes 6291464 | tf_op jit(solution)/shard_map/ppermute | solution.py:327
  282.1 17.9 %shard_map.102.refs_3_ = f32[2048,1280]{1,0:T(8,128)} custom-call(bf16[2048,2176]{1,0:T(8,128)(2,1)} %all-gather.6.cloned.1.call-done.refs_0_, bf16[1024,1280]{1,0:T(8,128)(2,1)} %collective-permute-done.8.refs_1_, bf16[1024,1280]{1,0:T(8,128)(2,1)} %collective-permute-done.12.refs_2_, f32[2048,1280]{1,0:T(8,128)} %shard_map.101.refs_3_), custom_call_target="tpu_custom_call", output_to_operand_aliasing={{}: (3, {})} | custom-call | flops 1 | bytes 1 | tf_op jit(solution)/shard_map/pallas_call | solution.py:168
  301.8 5.8 fusion.4
  309.3 16.8 %shard_map.103.refs_3_ = f32[2048,1280]{1,0:T(8,128)} custom-call(bf16[2048,2048]{1,0:T(8,128)(2,1)} %all-gather.10.cloned.1.call-done.refs_0_, bf16[1024,1280]{1,0:T(8,128)(2,1)S(1)} %copy-done.15, bf16[1024,1280]{1,0:T(8,128)(2,1)} %collective-permute-done.9.refs_2_, f32[2048,1280]{1,0:T(8,128)} %shard_map.102.refs_3_), custom_call_target="tpu_custom_call", output_to_operand_aliasing={{}: (3, {})} | custom-call | flops 1 | bytes 1 | tf_op jit(solution)/shard_map/pallas_call | solution.py:168
  331.7 6.0 shard_map.105
  344.3 3.1 constant_dynamic-slice_fusion.2
  347.4 10.3 %collective-permute-start.19 = (bf16[1024,1024]{1,0:T(8,128)(2,1)}, bf16[1024,1024]{1,0:T(8,128)(2,1)}, u32[]{:S(2)}, u32[]{:S(2)}) collective-permute-start(bf16[1024,1024]{1,0:T(8,128)(2,1)} %bitcast.15.second_ref), channel_id=1, source_target_pairs={{0,1},{3,2},{4,5},{7,6},{8,9},{11,10},{12,13},{15,14},{16,17},{19,... | collective-permute-start | bytes 6291464 | tf_op jit(solution)/shard_map/ppermute | solution.py:327
  357.6 2.7 slice.321
  360.3 14.4 %shard_map.104.refs_0_ = f32[2048,1024]{1,0:T(8,128)} custom-call(bf16[2048,2048]{1,0:T(8,128)(2,1)} %all-gather.12.cloned.1.call-done.refs_0_, bf16[1024,1280]{1,0:T(8,128)(2,1)S(1)} %copy-done.7, bf16[1024,1280]{1,0:T(8,128)(2,1)} %collective-permute-done.15.refs_2_, f32[2048,1280]{1,0:T(8,128)} %shard_map.103.refs_3_), custom_call_target="tpu_custom_call" | custom-call | flops 1 | bytes 1 | tf_op jit(solution)/shard_map/pallas_call | solution.py:168
  380.8 16.5 %shard_map.106.b_ref = bf16[1024,1024]{1,0:T(8,128)(2,1)} custom-call(s32[5]{0:T(128)S(1)} %pad_add_fusion.6.f_ref, f32[2048,1024]{1,0:T(8,128)} %shard_map.104.refs_0_, f32[1,1024]{1,0:T(1,128)S(1)} %bitcast.86, f32[2048,128]{1,0:T(8,128)S(1)} %copy-done.8, f32[2048,128]{1,0:T(8,128)S(1)} %get-tuple-element.230.refs_3_, ...), custom_call_target="tpu_custom_call" | custom-call | flops 1 | bytes 1 | tf_op jit(solution)/shard_map/pallas_call | solution.py:126
  399.1 3.1 constant_dynamic-slice_fusion.1
  402.2 14.1 %collective-permute-start.23 = (bf16[1024,1024]{1,0:T(8,128)(2,1)}, bf16[1024,1024]{1,0:T(8,128)(2,1)}, u32[]{:S(2)}, u32[]{:S(2)}) collective-permute-start(bf16[1024,1024]{1,0:T(8,128)(2,1)} %bitcast.25.second_ref), channel_id=1, source_target_pairs={{0,1},{3,2},{4,5},{7,6},{8,9},{11,10},{12,13},{15,14},{16,17},{19,... | collective-permute-start | bytes 6291464 | tf_op jit(solution)/shard_map/ppermute | solution.py:327
  421.4 16.7 %shard_map.107.a_ref = bf16[1024,1024]{1,0:T(8,128)(2,1)} custom-call(s32[5]{0:T(128)S(1)} %pad_add_fusion.5.f_ref, f32[2048,1024]{1,0:T(8,128)} %shard_map.104.refs_0_, f32[1,1024]{1,0:T(1,128)S(1)} %bitcast.87, f32[2048,128]{1,0:T(8,128)S(1)} %copy-done.9, f32[2048,128]{1,0:T(8,128)S(1)} %get-tuple-element.230.refs_3_, ...), custom_call_target="tpu_custom_call" | custom-call | flops 1 | bytes 1 | tf_op jit(solution)/shard_map/pallas_call | solution.py:126
  440.3 5.0 shard_map.108
  445.3 5.0 shard_map.109
  452.1 5.3 shard_map.111
  457.4 4.9 shard_map.110
  463.0 3.1 constant_dynamic-slice_fusion
  466.1 2.6 collective-permute-start.25
  470.1 3.0 add_convert_fusion.1
  478.6 5.2 shard_map.112
  483.8 5.0 shard_map.113
  488.8 4.9 shard_map.114
  493.7 19.8 %collective-permute-done.25.first_ref = bf16[1024,1024]{1,0:T(8,128)(2,1)} collective-permute-done((bf16[1024,1024]{1,0:T(8,128)(2,1)}, bf16[1024,1024]{1,0:T(8,128)(2,1)}, u32[]{:S(2)}, u32[]{:S(2)}) %collective-permute-start.25) | collective-permute-done | bytes 2097184 | tf_op jit(solution)/shard_map/ppermute | solution.py:327
  513.5 4.9 shard_map.115
  521.5 6.6 collective-permute-done.28.refs_1_
  528.1 2.4 add_convert_fusion
  539.1 4.3 shard_map.118.result_ref
  543.4 4.1 shard_map.119.result_ref
  549.3 5.0 shard_map.116
  554.3 5.0 shard_map.117
  559.5 18.9 %collective-permute-done.30.refs_2_ = bf16[4,256,1024]{2,1,0:T(8,128)(2,1)S(1)} collective-permute-done((bf16[4,256,1024]{2,1,0:T(8,128)(2,1)}, bf16[4,256,1024]{2,1,0:T(8,128)(2,1)S(1)}, u32[]{:S(2)}, u32[]{:S(2)}) %collective-permute-start.30) | collective-permute-done | bytes 2097184 | tf_op jit(solution)/shard_map/ppermute | solution.py:330
  578.6 4.0 collective-permute-done.32.refs_1_
  584.9 2.5 shard_map.122.result_ref
  587.4 2.5 shard_map.123.result_ref
  591.6 5.0 shard_map.120
  597.6 5.2 shard_map.121
  603.1 5.1 collective-permute-done.33.refs_2_
  608.2 4.2 collective-permute-done.34.refs_1_
  620.1 4.1 shard_map.124.result_ref
  624.2 4.1 shard_map.125.result_ref
  628.3 6.6 collective-permute-done.37.refs_3_
  634.9 2.5 shard_map.126.result_ref
  637.6 2.5 shard_map.127.result_ref
  640.2 5.2 collective-permute-done.36.refs_3_
  651.8 9.0 %collective-permute-done.38.refs_3_ = bf16[2,256,512]{2,1,0:T(8,128)(2,1)S(1)} collective-permute-done((bf16[2,256,512]{2,1,0:T(8,128)(2,1)S(1)}, bf16[2,256,512]{2,1,0:T(8,128)(2,1)S(1)}, u32[]{:S(2)}, u32[]{:S(2)}) %collective-permute-start.38) | collective-permute-done | bytes 524320 | tf_op jit(solution)/shard_map/ppermute | solution.py:327
  (251 shorter events, 134.1 us)
Async XLA Ops:
  6.5 149.4 %all-gather.8.cloned.1.call-start = ((), (), s32[]{:S(2)}) async-start(), calls=%async_computation.1 | async-start | bytes 10485760 | tf_op jit(solution)/shard_map/all_gather | solution.py:376
  11.2 5.9 copy-start.16
  12.1 18.8 %collective-permute-start.1 = (bf16[256,1280]{1,0:T(8,128)(2,1)}, bf16[256,1280]{1,0:T(8,128)(2,1)}, u32[]{:S(2)}, u32[]{:S(2)}) collective-permute-start(bf16[256,1280]{1,0:T(8,128)(2,1)} %pad_maximum_fusion.19), channel_id=1, source_target_pairs={{0,8},{1,9},{2,10},{3,11},{4,12},{5,13},{6,14},{7,15},{8,0},{9,1},... | collective-permute-start | bytes 1966088 | tf_op jit(solution)/shard_map/ppermute | solution.py:330
  16.0 15.0 %collective-permute-start.2 = (bf16[256,1280]{1,0:T(8,128)(2,1)}, bf16[256,1280]{1,0:T(8,128)(2,1)}, u32[]{:S(2)}, u32[]{:S(2)}) collective-permute-start(bf16[256,1280]{1,0:T(8,128)(2,1)} %pad_maximum_fusion.20), channel_id=1, source_target_pairs={{0,4},{1,5},{2,6},{3,7},{4,0},{5,1},{6,2},{7,3},{8,12},{9,13},{10,... | collective-permute-start | bytes 1966088 | tf_op jit(solution)/shard_map/ppermute | solution.py:330
  16.9 26.5 %collective-permute-start = (bf16[256,1280]{1,0:T(8,128)(2,1)}, bf16[256,1280]{1,0:T(8,128)(2,1)}, u32[]{:S(2)}, u32[]{:S(2)}) collective-permute-start(bf16[256,1280]{1,0:T(8,128)(2,1)} %pad_maximum_fusion.18), channel_id=1, source_target_pairs={{0,12},{1,13},{2,14},{3,15},{4,8},{5,9},{6,10},{7,11},{8,4},{9,5},... | collective-permute-start | bytes 1966088 | tf_op jit(solution)/shard_map/ppermute | solution.py:330
  17.1 12.0 %copy-start.22 = (bf16[512,4096]{1,0:T(8,128)(2,1)S(1)}, bf16[512,4096]{1,0:T(8,128)(2,1)}, u32[]{:S(2)}) copy-start(bf16[512,4096]{1,0:T(8,128)(2,1)} %param.16) | copy-start | bytes 12582916
  24.1 34.5 %collective-permute-start.11 = (bf16[256,2048]{1,0:T(8,128)(2,1)S(1)}, bf16[256,2048]{1,0:T(8,128)(2,1)}, u32[]{:S(2)}, u32[]{:S(2)}) collective-permute-start(bf16[256,2048]{1,0:T(8,128)(2,1)S(1)} %slice.385), channel_id=1, source_target_pairs={{0,1},{3,2},{4,5},{7,6},{8,9},{11,10},{12,13},{15,14},{16,17},{19,... | collective-permute-start | bytes 3145736 | tf_op jit(solution)/shard_map/ppermute | solution.py:327
  62.0 220.0 %all-gather.6.cloned.1.call-start = ((), (), s32[]{:S(2)}) async-start(), calls=%async_computation | async-start | bytes 11141120 | tf_op jit(solution)/shard_map/all_gather | solution.py:376
  64.0 2.8 slice-start.10
  64.0 2.8 slice-start.11
  64.3 69.4 %collective-permute-start.7 = (bf16[256,6272]{1,0:T(8,128)(2,1)S(1)}, bf16[256,6272]{1,0:T(8,128)(2,1)S(1)}, u32[]{:S(2)}, u32[]{:S(2)}) collective-permute-start(bf16[256,6272]{1,0:T(8,128)(2,1)S(1)} %pad_maximum_fusion.5), channel_id=1, source_target_pairs={{0,1},{3,2},{4,5},{7,6},{8,9},{11,10},{12,13},{15,14},{16,17},{19,... | collective-permute-start | bytes 9633800 | tf_op jit(solution)/shard_map/ppermute | solution.py:327
  65.9 64.6 %collective-permute-start.6 = (bf16[1024,1280]{1,0:T(8,128)(2,1)S(1)}, bf16[1024,1280]{1,0:T(8,128)(2,1)S(1)}, u32[]{:S(2)}, u32[]{:S(2)}) collective-permute-start(bf16[1024,1280]{1,0:T(8,128)(2,1)S(1)} %copy-done.2), channel_id=1, source_target_pairs={{2,1},{1,2},{6,5},{5,6},{10,9},{9,10},{14,13},{13,14},{18,17},{17,... | collective-permute-start | bytes 7864328 | tf_op jit(solution)/shard_map/ppermute | solution.py:327
  69.0 2.4 collective-permute-start.5
  69.2 31.2 %collective-permute-start.4 = (bf16[256,1280]{1,0:T(8,128)(2,1)S(1)}, bf16[256,1280]{1,0:T(8,128)(2,1)S(1)}, u32[]{:S(2)}, u32[]{:S(2)}) collective-permute-start(bf16[256,1280]{1,0:T(8,128)(2,1)S(1)} %pad_maximum_fusion.23), channel_id=1, source_target_pairs={{0,8},{1,9},{2,10},{3,11},{4,12},{5,13},{6,14},{7,15},{8,0},{9,1},... | collective-permute-start | bytes 1966088 | tf_op jit(solution)/shard_map/ppermute | solution.py:330
  70.6 57.5 %collective-permute-start.3 = (bf16[256,1280]{1,0:T(8,128)(2,1)S(1)}, bf16[256,1280]{1,0:T(8,128)(2,1)S(1)}, u32[]{:S(2)}, u32[]{:S(2)}) collective-permute-start(bf16[256,1280]{1,0:T(8,128)(2,1)S(1)} %pad_maximum_fusion.22), channel_id=1, source_target_pairs={{0,12},{1,13},{2,14},{3,15},{4,8},{5,9},{6,10},{7,11},{8,4},{9,5},... | collective-permute-start | bytes 1966088 | tf_op jit(solution)/shard_map/ppermute | solution.py:330
  130.5 3.3 copy-start.23
  130.5 3.5 copy-start.14
  133.8 2.0 slice-start.1
  136.7 2.5 copy-start.3
  138.4 169.2 %all-gather.10.cloned.1.call-start = ((), (), s32[]{:S(2)}) async-start(), calls=%async_computation.2 | async-start | bytes 10485760 | tf_op jit(solution)/shard_map/all_gather | solution.py:376
  139.3 59.3 %collective-permute-start.8 = (bf16[1024,1280]{1,0:T(8,128)(2,1)S(1)}, bf16[1024,1280]{1,0:T(8,128)(2,1)}, u32[]{:S(2)}, u32[]{:S(2)}) collective-permute-start(bf16[1024,1280]{1,0:T(8,128)(2,1)S(1)} %copy-done.3), channel_id=1, source_target_pairs={{0,1},{3,2},{4,5},{7,6},{8,9},{11,10},{12,13},{15,14},{16,17},{19,... | collective-permute-start | bytes 7864328 | tf_op jit(solution)/shard_map/ppermute | solution.py:327
  145.2 53.5 %collective-permute-start.9 = (bf16[1024,1280]{1,0:T(8,128)(2,1)}, bf16[1024,1280]{1,0:T(8,128)(2,1)}, u32[]{:S(2)}, u32[]{:S(2)}) collective-permute-start(bf16[1024,1280]{1,0:T(8,128)(2,1)} %pad_maximum_fusion.7.refs_2_), channel_id=1, source_target_pairs={{2,1},{1,2},{6,5},{5,6},{10,9},{9,10},{14,13},{13,14},{18,17},{17,... | collective-permute-start | bytes 7864328 | tf_op jit(solution)/shard_map/ppermute | solution.py:327
  150.4 48.2 %collective-permute-start.10 = (bf16[256,4096]{1,0:T(8,128)(2,1)}, bf16[256,4096]{1,0:T(8,128)(2,1)}, u32[]{:S(2)}, u32[]{:S(2)}) collective-permute-start(bf16[256,4096]{1,0:T(8,128)(2,1)} %slice.311), channel_id=1, source_target_pairs={{1,0},{2,3},{5,4},{6,7},{9,8},{10,11},{13,12},{14,15},{17,16},{18,... | collective-permute-start | bytes 6291464 | tf_op jit(solution)/shard_map/ppermute | solution.py:327
  155.9 2.2 copy-start.4
  198.6 2.2 slice-start.6
  203.1 126.9 %all-gather.12.cloned.1.call-start = ((), (), s32[]{:S(2)}) async-start(), calls=%async_computation.3 | async-start | bytes 10485760 | tf_op jit(solution)/shard_map/all_gather | solution.py:376
  203.1 59.9 %collective-permute-start.12 = (bf16[1024,1280]{1,0:T(8,128)(2,1)}, bf16[1024,1280]{1,0:T(8,128)(2,1)}, u32[]{:S(2)}, u32[]{:S(2)}) collective-permute-start(bf16[1024,1280]{1,0:T(8,128)(2,1)} %pad_maximum_fusion.7.refs_2_), channel_id=1, source_target_pairs={{0,1},{3,2},{4,5},{7,6},{8,9},{11,10},{12,13},{15,14},{16,17},{19,... | collective-permute-start | bytes 7864328 | tf_op jit(solution)/shard_map/ppermute | solution.py:327
  210.4 52.6 %collective-permute-start.13 = (bf16[1024,1280]{1,0:T(8,128)(2,1)}, bf16[1024,1280]{1,0:T(8,128)(2,1)S(1)}, u32[]{:S(2)}, u32[]{:S(2)}) collective-permute-start(bf16[1024,1280]{1,0:T(8,128)(2,1)} %collective-permute-done.8.refs_1_), channel_id=1, source_target_pairs={{2,1},{1,2},{6,5},{5,6},{10,9},{9,10},{14,13},{13,14},{18,17},{17,... | collective-permute-start | bytes 7864328 | tf_op jit(solution)/shard_map/ppermute | solution.py:327
  213.0 46.6 %collective-permute-start.14 = (bf16[256,4096]{1,0:T(8,128)(2,1)S(1)}, bf16[256,4096]{1,0:T(8,128)(2,1)S(1)}, u32[]{:S(2)}, u32[]{:S(2)}) collective-permute-start(bf16[256,4096]{1,0:T(8,128)(2,1)S(1)} %slice.320), channel_id=1, source_target_pairs={{1,0},{2,3},{5,4},{6,7},{9,8},{10,11},{13,12},{14,15},{17,16},{18,... | collective-permute-start | bytes 6291464 | tf_op jit(solution)/shard_map/ppermute | solution.py:327
  263.1 2.5 slice-start.7
  267.9 58.3 %collective-permute-start.15 = (bf16[1024,1280]{1,0:T(8,128)(2,1)}, bf16[1024,1280]{1,0:T(8,128)(2,1)}, u32[]{:S(2)}, u32[]{:S(2)}) collective-permute-start(bf16[1024,1280]{1,0:T(8,128)(2,1)} %collective-permute-done.12.refs_2_), channel_id=1, source_target_pairs={{2,1},{1,2},{6,5},{5,6},{10,9},{9,10},{14,13},{13,14},{18,17},{17,... | collective-permute-start | bytes 7864328 | tf_op jit(solution)/shard_map/ppermute | solution.py:327
  273.1 53.0 %collective-permute-start.16 = (bf16[1024,1024]{1,0:T(8,128)(2,1)}, bf16[1024,1024]{1,0:T(8,128)(2,1)}, u32[]{:S(2)}, u32[]{:S(2)}) collective-permute-start(bf16[1024,1024]{1,0:T(8,128)(2,1)} %bitcast.10.second_ref), channel_id=1, source_target_pairs={{0,1},{3,2},{4,5},{7,6},{8,9},{11,10},{12,13},{15,14},{16,17},{19,... | collective-permute-start | bytes 6291464 | tf_op jit(solution)/shard_map/ppermute | solution.py:327
  328.0 14.6 %collective-permute-start.17 = (bf16[256,1024]{1,0:T(8,128)(2,1)}, bf16[256,1024]{1,0:T(8,128)(2,1)}, u32[]{:S(2)}, u32[]{:S(2)}) collective-permute-start(bf16[256,1024]{1,0:T(8,128)(2,1)} %slice.330), channel_id=1, source_target_pairs={{2,1},{1,2},{6,5},{5,6},{10,9},{9,10},{14,13},{13,14},{18,17},{17,... | collective-permute-start | bytes 1572872 | tf_op jit(solution)/shard_map/ppermute | solution.py:327
  342.6 32.0 %collective-permute-start.18 = (bf16[4,512,256]{2,1,0:T(8,128)(2,1)}, bf16[4,512,256]{2,1,0:T(8,128)(2,1)}, u32[]{:S(2)}, u32[]{:S(2)}) collective-permute-start(bf16[4,512,256]{2,1,0:T(8,128)(2,1)} %pad_maximum_fusion.17), channel_id=1, source_target_pairs={{1,2},{5,6},{9,10},{13,14},{17,18},{21,22},{25,26},{29,30}} | collective-permute-start | bytes 3145736 | tf_op jit(solution)/shard_map/ppermute | solution.py:327
  347.4 12.9 %copy-start.7 = (bf16[1024,1280]{1,0:T(8,128)(2,1)S(1)}, bf16[1024,1280]{1,0:T(8,128)(2,1)}, u32[]{:S(2)}) copy-start(bf16[1024,1280]{1,0:T(8,128)(2,1)} %copy-done.5) | copy-start | bytes 7864324
  347.4 50.5 %collective-permute-start.19 = (bf16[1024,1024]{1,0:T(8,128)(2,1)}, bf16[1024,1024]{1,0:T(8,128)(2,1)}, u32[]{:S(2)}, u32[]{:S(2)}) collective-permute-start(bf16[1024,1024]{1,0:T(8,128)(2,1)} %bitcast.15.second_ref), channel_id=1, source_target_pairs={{0,1},{3,2},{4,5},{7,6},{8,9},{11,10},{12,13},{15,14},{16,17},{19,... | collective-permute-start | bytes 6291464 | tf_op jit(solution)/shard_map/ppermute | solution.py:327
  374.7 23.2 %collective-permute-start.20 = (bf16[768,1024]{1,0:T(8,128)(2,1)}, bf16[768,1024]{1,0:T(8,128)(2,1)}, u32[]{:S(2)}, u32[]{:S(2)}) collective-permute-start(bf16[768,1024]{1,0:T(8,128)(2,1)} %slice.321), channel_id=1, source_target_pairs={{2,1},{1,2},{6,5},{5,6},{10,9},{9,10},{14,13},{13,14},{18,17},{17,... | collective-permute-start | bytes 4718600 | tf_op jit(solution)/shard_map/ppermute | solution.py:327
  397.9 52.4 %collective-permute-start.21 = (bf16[1024,1024]{1,0:T(8,128)(2,1)}, bf16[1024,1024]{1,0:T(8,128)(2,1)}, u32[]{:S(2)}, u32[]{:S(2)}) collective-permute-start(bf16[1024,1024]{1,0:T(8,128)(2,1)} %shard_map.106.b_ref), channel_id=1, source_target_pairs={{1,0},{2,3},{5,4},{6,7},{9,8},{10,11},{13,12},{14,15},{17,16},{18,... | collective-permute-start | bytes 6291464 | tf_op jit(solution)/shard_map/ppermute | solution.py:327
  402.2 60.6 %collective-permute-start.23 = (bf16[1024,1024]{1,0:T(8,128)(2,1)}, bf16[1024,1024]{1,0:T(8,128)(2,1)}, u32[]{:S(2)}, u32[]{:S(2)}) collective-permute-start(bf16[1024,1024]{1,0:T(8,128)(2,1)} %bitcast.25.second_ref), channel_id=1, source_target_pairs={{0,1},{3,2},{4,5},{7,6},{8,9},{11,10},{12,13},{15,14},{16,17},{19,... | collective-permute-start | bytes 6291464 | tf_op jit(solution)/shard_map/ppermute | solution.py:327
  416.4 46.5 %collective-permute-start.22 = (bf16[1024,1024]{1,0:T(8,128)(2,1)}, bf16[1024,1024]{1,0:T(8,128)(2,1)}, u32[]{:S(2)}, u32[]{:S(2)}) collective-permute-start(bf16[1024,1024]{1,0:T(8,128)(2,1)} %collective-permute-done.19.first_ref), channel_id=1, source_target_pairs={{2,1},{1,2},{6,5},{5,6},{10,9},{9,10},{14,13},{13,14},{18,17},{17,... | collective-permute-start | bytes 6291464 | tf_op jit(solution)/shard_map/ppermute | solution.py:327
  438.0 2.2 copy-start
  462.9 7.2 %collective-permute-start.24 = (bf16[4,512,1024]{2,1,0:T(8,128)(2,1)S(1)}, bf16[4,512,1024]{2,1,0:T(8,128)(2,1)S(1)}, u32[]{:S(2)}, u32[]{:S(2)}) collective-permute-start(bf16[4,512,1024]{2,1,0:T(8,128)(2,1)S(1)} %pad_maximum_fusion.2), channel_id=1, source_target_pairs={{0,4},{1,5},{2,6},{3,7},{4,0},{5,1},{6,2},{7,3},{8,12},{9,13},{10,... | collective-permute-start | bytes 12582920 | tf_op jit(solution)/shard_map/ppermute | solution.py:330
  466.1 47.4 %collective-permute-start.25 = (bf16[1024,1024]{1,0:T(8,128)(2,1)}, bf16[1024,1024]{1,0:T(8,128)(2,1)}, u32[]{:S(2)}, u32[]{:S(2)}) collective-permute-start(bf16[1024,1024]{1,0:T(8,128)(2,1)} %bitcast.29.second_ref), channel_id=1, source_target_pairs={{0,1},{3,2},{4,5},{7,6},{8,9},{11,10},{12,13},{15,14},{16,17},{19,... | collective-permute-start | bytes 6291464 | tf_op jit(solution)/shard_map/ppermute | solution.py:327
  469.2 3.8 copy-start.19
  470.1 8.5 %copy-start.21 = (bf16[4,512,1024]{2,1,0:T(8,128)(2,1)}, bf16[4,512,1024]{2,1,0:T(8,128)(2,1)S(1)}, u32[]{:S(2)}) copy-start(bf16[4,512,1024]{2,1,0:T(8,128)(2,1)S(1)} %collective-permute-done.24.refs_1_) | copy-start | bytes 12582916
  473.1 47.9 %collective-permute-start.27 = (bf16[4,256,1024]{2,1,0:T(8,128)(2,1)}, bf16[4,256,1024]{2,1,0:T(8,128)(2,1)S(1)}, u32[]{:S(2)}, u32[]{:S(2)}) collective-permute-start(bf16[4,256,1024]{2,1,0:T(8,128)(2,1)} %add_convert_fusion.1), channel_id=1, source_target_pairs={{0,8},{1,9},{2,10},{3,11},{4,12},{5,13},{6,14},{7,15},{8,0},{9,1},... | collective-permute-start | bytes 6291464 | tf_op jit(solution)/shard_map/ppermute | solution.py:330
  474.9 46.1 %collective-permute-start.26 = (bf16[1024,1024]{1,0:T(8,128)(2,1)}, bf16[1024,1024]{1,0:T(8,128)(2,1)}, u32[]{:S(2)}, u32[]{:S(2)}) collective-permute-start(bf16[1024,1024]{1,0:T(8,128)(2,1)} %collective-permute-done.23.first_ref), channel_id=1, source_target_pairs={{2,1},{1,2},{6,5},{5,6},{10,9},{9,10},{14,13},{13,14},{18,17},{17,... | collective-permute-start | bytes 6291464 | tf_op jit(solution)/shard_map/ppermute | solution.py:327
  520.9 7.2 %collective-permute-start.28 = (bf16[4,512,1024]{2,1,0:T(8,128)(2,1)S(1)}, bf16[4,512,1024]{2,1,0:T(8,128)(2,1)S(1)}, u32[]{:S(2)}, u32[]{:S(2)}) collective-permute-start(bf16[4,512,1024]{2,1,0:T(8,128)(2,1)S(1)} %pad_maximum_fusion.4), channel_id=1, source_target_pairs={{0,4},{1,5},{2,6},{3,7},{4,0},{5,1},{6,2},{7,3},{8,12},{9,13},{10,... | collective-permute-start | bytes 12582920 | tf_op jit(solution)/shard_map/ppermute | solution.py:330
  521.5 9.0 %copy-start.18 = (bf16[4,512,1024]{2,1,0:T(8,128)(2,1)}, bf16[4,512,1024]{2,1,0:T(8,128)(2,1)S(1)}, u32[]{:S(2)}) copy-start(bf16[4,512,1024]{2,1,0:T(8,128)(2,1)S(1)} %pad_maximum_fusion.3.refs_0_) | copy-start | bytes 12582916
  528.1 7.6 %copy-start.20 = (bf16[4,512,1024]{2,1,0:T(8,128)(2,1)}, bf16[4,512,1024]{2,1,0:T(8,128)(2,1)S(1)}, u32[]{:S(2)}) copy-start(bf16[4,512,1024]{2,1,0:T(8,128)(2,1)S(1)} %collective-permute-done.28.refs_1_) | copy-start | bytes 12582916
  528.1 9.0 %copy-start.17 = (bf16[256,8192]{1,0:T(8,128)(2,1)S(1)}, bf16[256,8192]{1,0:T(8,128)(2,1)}, u32[]{:S(2)}) copy-start(bf16[256,8192]{1,0:T(8,128)(2,1)} %hidden_ref.25) | copy-start | bytes 12582916
  530.5 47.9 %collective-permute-start.30 = (bf16[4,256,1024]{2,1,0:T(8,128)(2,1)}, bf16[4,256,1024]{2,1,0:T(8,128)(2,1)S(1)}, u32[]{:S(2)}, u32[]{:S(2)}) collective-permute-start(bf16[4,256,1024]{2,1,0:T(8,128)(2,1)} %add_convert_fusion), channel_id=1, source_target_pairs={{0,8},{1,9},{2,10},{3,11},{4,12},{5,13},{6,14},{7,15},{8,0},{9,1},... | collective-permute-start | bytes 6291464 | tf_op jit(solution)/shard_map/ppermute | solution.py:330
  532.3 46.1 %collective-permute-start.29 = (bf16[1024,1024]{1,0:T(8,128)(2,1)}, bf16[1024,1024]{1,0:T(8,128)(2,1)}, u32[]{:S(2)}, u32[]{:S(2)}) collective-permute-start(bf16[1024,1024]{1,0:T(8,128)(2,1)} %collective-permute-done.25.first_ref), channel_id=1, source_target_pairs={{2,1},{1,2},{6,5},{5,6},{10,9},{9,10},{14,13},{13,14},{18,17},{17,... | collective-permute-start | bytes 6291464 | tf_op jit(solution)/shard_map/ppermute | solution.py:327
  535.7 23.7 %collective-permute-start.31 = (bf16[2,256,512]{2,1,0:T(8,128)(2,1)S(1)}, bf16[2,256,512]{2,1,0:T(8,128)(2,1)S(1)}, u32[]{:S(2)}, u32[]{:S(2)}) collective-permute-start(bf16[2,256,512]{2,1,0:T(8,128)(2,1)S(1)} %pad_maximum_fusion.26), channel_id=1, source_target_pairs={{1,0},{2,3},{5,4},{6,7},{9,8},{10,11},{13,12},{14,15},{17,16},{18,... | collective-permute-start | bytes 1572872 | tf_op jit(solution)/shard_map/ppermute | solution.py:327
  578.4 4.2 collective-permute-start.32
  583.0 25.3 %collective-permute-start.33 = (bf16[2,256,1024]{2,1,0:T(8,128)(2,1)S(1)}, bf16[2,256,1024]{2,1,0:T(8,128)(2,1)S(1)}, u32[]{:S(2)}, u32[]{:S(2)}) collective-permute-start(bf16[2,256,1024]{2,1,0:T(8,128)(2,1)S(1)} %add_convert_fusion.3), channel_id=1, source_target_pairs={{0,8},{1,9},{2,10},{3,11},{4,12},{5,13},{6,14},{7,15},{8,0},{9,1},... | collective-permute-start | bytes 3145736 | tf_op jit(solution)/shard_map/ppermute | solution.py:330
  602.9 9.5 %copy-start.13 = (bf16[512,1024]{1,0:T(8,128)(2,1)S(1)}, bf16[512,1024]{1,0:T(8,128)(2,1)}, u32[]{:S(2)}) copy-start(bf16[512,1024]{1,0:T(8,128)(2,1)} %copy-done.12) | copy-start | bytes 3145732
  608.2 10.1 %copy-start.10 = (bf16[2,256,1024]{2,1,0:T(8,128)(2,1)}, bf16[2,256,1024]{2,1,0:T(8,128)(2,1)S(1)}, u32[]{:S(2)}) copy-start(bf16[2,256,1024]{2,1,0:T(8,128)(2,1)S(1)} %collective-permute-done.33.refs_2_) | copy-start | bytes 3145732
  608.2 4.2 collective-permute-start.34
  613.8 31.6 %collective-permute-start.35 = (bf16[2,256,1024]{2,1,0:T(8,128)(2,1)}, bf16[2,256,1024]{2,1,0:T(8,128)(2,1)S(1)}, u32[]{:S(2)}, u32[]{:S(2)}) collective-permute-start(bf16[2,256,1024]{2,1,0:T(8,128)(2,1)} %add_convert_fusion.2), channel_id=1, source_target_pairs={{0,8},{1,9},{2,10},{3,11},{4,12},{5,13},{6,14},{7,15},{8,0},{9,1},... | collective-permute-start | bytes 3145736 | tf_op jit(solution)/shard_map/ppermute | solution.py:330
  617.0 17.9 %collective-permute-start.37 = (bf16[2,256,512]{2,1,0:T(8,128)(2,1)S(1)}, bf16[2,256,512]{2,1,0:T(8,128)(2,1)S(1)}, u32[]{:S(2)}, u32[]{:S(2)}) collective-permute-start(bf16[2,256,512]{2,1,0:T(8,128)(2,1)S(1)} %pad_maximum_fusion.28), channel_id=1, source_target_pairs={{1,0},{2,3},{5,4},{6,7},{9,8},{10,11},{13,12},{14,15},{17,16},{18,... | collective-permute-start | bytes 1572872 | tf_op jit(solution)/shard_map/ppermute | solution.py:327
  618.7 26.6 %collective-permute-start.36 = (bf16[2,256,512]{2,1,0:T(8,128)(2,1)S(1)}, bf16[2,256,512]{2,1,0:T(8,128)(2,1)S(1)}, u32[]{:S(2)}, u32[]{:S(2)}) collective-permute-start(bf16[2,256,512]{2,1,0:T(8,128)(2,1)S(1)} %pad_maximum_fusion.27), channel_id=1, source_target_pairs={{1,0},{2,3},{5,4},{6,7},{9,8},{10,11},{13,12},{14,15},{17,16},{18,... | collective-permute-start | bytes 1572872 | tf_op jit(solution)/shard_map/ppermute | solution.py:327
  640.2 6.9 %copy-start.11 = (bf16[2,256,1024]{2,1,0:T(8,128)(2,1)S(1)}, bf16[2,256,1024]{2,1,0:T(8,128)(2,1)}, u32[]{:S(2)}) copy-start(bf16[2,256,1024]{2,1,0:T(8,128)(2,1)} %copy-done.10) | copy-start | bytes 3145732
  645.7 15.0 %collective-permute-start.38 = (bf16[2,256,512]{2,1,0:T(8,128)(2,1)S(1)}, bf16[2,256,512]{2,1,0:T(8,128)(2,1)S(1)}, u32[]{:S(2)}, u32[]{:S(2)}) collective-permute-start(bf16[2,256,512]{2,1,0:T(8,128)(2,1)S(1)} %pad_maximum_fusion.29), channel_id=1, source_target_pairs={{1,0},{2,3},{5,4},{6,7},{9,8},{10,11},{13,12},{14,15},{17,16},{18,... | collective-permute-start | bytes 1572872 | tf_op jit(solution)/shard_map/ppermute | solution.py:327
  (20 other events, 32.4 us)
Sparse Core Ops, SparseCore 0:
  62.2 84.4 all-gather.7
  148.2 60.8 all-gather.5
  210.7 58.2 all-gather.9
  270.4 58.2 all-gather.11
